TPU v7x, 32 devices: a whole 2x2x4 slice. The times are simulated.
32 devices in a mesh: grp: 2 (over x), aux: 16 (over z, y, core).
Axes of the slice: x: 2, y: 2, z: 4, core: 2. Of those that a mesh axis runs over, the one named last changes fastest.
Arguments:
- tiles: float32 [1024, 4, 128, 128], P(('grp', 'aux')), parts along dimension 0, may hold values from -0.8 to 0.8
- tile_owner: int32 [1024, 1], P(('grp', 'aux')), parts along dimension 0, may hold values from 0 to 15; in each aligned block of 32 rows (0 to 31, 32 to 63, ...) at most 4 rows name the same one
- tile_sub: int32 [1024], P(('grp', 'aux')), parts along dimension 0, may hold values from 0 to 1
- tile_cols: int32 [1024], P(('grp', 'aux')), parts along dimension 0, may hold values from 0 to 31
- row_order: int32 [64], P('grp'), parts along dimension 0, may hold values from 0 to 31, each once
- orbitals: float32 [8192, 128], P(('grp', 'aux')), parts along dimension 0, may hold values from -0.5 to 0.5
Outputs:
- exchange_rows: float32 [8192, 128], P(('grp', 'aux')), parts along dimension 0
There are 2 independent parts, one for each index of `grp`. A program takes and returns all parts, laid end to end along the dimension named above; each array names one. Nothing has to cross between parts.
Inputs may be any that keep to these rules, and one draw needn't show every extreme that they name: `tile_owner`: in the rows of one device no owner is named by more than 4 tiles, a bound that some block reaches. Owner o holds the row blocks row_order[o * 2] .. row_order[o * 2 + 1].
All inputs are finite; a program needn't handle non-finite values.
Results may differ from a plain program's by a relative error of at most 0.00011.
Values sent between devices are 32-bit elements; how exact they have to be, the bound alone decides.
No kernel may reach another device: no remote copies, remote signals or barrier semaphores. Data moves between devices by JAX's collectives and lax.ppermute only.
A program may use at most 64 MiB of HBM per device.

v0:
```python
import jax
import jax.numpy as jnp
from jax import lax
from jax.sharding import PartitionSpec as P


def local(tiles, tile_owner, tile_sub, tile_cols, row_order, orbitals):
    highest = lax.Precision.HIGHEST
    n_aux = lax.axis_size("aux")
    n_tiles, aux_dev, block, _ = tiles.shape
    n_blocks = row_order.shape[0]
    per_owner = n_blocks // n_aux
    coeff = lax.all_gather(orbitals, "aux", axis=0, tiled=True)
    blocked = coeff.reshape(n_blocks, block, -1)
    owner = tile_owner[:, 0]
    position = owner * per_owner + tile_sub
    row_block = row_order[position]
    half = jnp.einsum("tprl,tlj->tprj", tiles, blocked[tile_cols], precision=highest)
    fitted = jnp.einsum("tprj,tri->pji", half, blocked[row_block], precision=highest)
    partial_value = jnp.einsum("tprj,pji->tri", half, fitted, precision=highest)
    width = partial_value.shape[2]
    count = per_owner * block * lax.axis_size("aux")
    keys = jnp.arange(count // block, dtype=jnp.int32)
    select = (position[None, :] == keys[:, None]).astype(jnp.float32)
    summed = jnp.einsum("kt,tri->kri", select, partial_value, precision=highest)
    return lax.psum_scatter(summed.reshape(count, width), "aux", scatter_dimension=0, tiled=True)


def solution(mesh):
    in_specs = (
        P(("grp", "aux"), None, None, None),
        P(("grp", "aux"), None),
        P(("grp", "aux")),
        P(("grp", "aux")),
        P("grp"),
        P(("grp", "aux"), None),
    )
    out_specs = P(("grp", "aux"), None)
    return jax.shard_map(local, mesh=mesh, in_specs=in_specs, out_specs=out_specs, check_vma=False)
```

profile of v0, /device:TPU:0, one launch (start us, length us, event | category | flops | bytes accessed | tf_op | source)
XLA Modules:
  0.0 163.7 jit_solution(9767462437081177768)
XLA Ops:
  6.5 0.0 copy-start
  6.5 0.0 all-gather.2.cloned.1.call-start
  6.5 0.7 all-gather.2.cloned.1.call-update
  7.3 0.0 reduce-scatter.2.cloned.1.call-start
  7.3 0.7 compare_select_fusion.1
  8.0 0.0 copy-done
  8.0 0.7 gather_fusion.1
  8.7 0.7 compare_select_fusion.2
  9.4 44.3 %all-gather.2.cloned.1.call-done = f32[4096,128]{1,0:T(8,128)} async-done(((f32[256,128]{1,0:T(8,128)}), f32[4096,128]{1,0:T(8,128)}) %all-gather.2.cloned.1.call-update) | async-done | bytes 2097168 | tf_op jit(solution)/shard_map/all_gather | solution.py:13
  53.7 2.3 %gather_fusion = f32[32,128,128]{2,1,0:T(8,128)S(1)} fusion(f32[32,128,128]{2,1,0:T(8,128)} %bitcast.33, s32[1024]{0:T(1024)S(1)} %pad_clamp_fusion.2), kind=kCustom, calls=%fused_computation | custom fusion | bytes 4194432 | tf_op jit(solution)/shard_map/gather | solution.py:18
  55.9 3.6 %gather_fusion.2 = f32[32,128,128]{2,1,0:T(8,128)} fusion(f32[32,128,128]{2,1,0:T(8,128)} %bitcast.34, s32[1024]{0:T(1024)S(1)} %pad_clamp_fusion), kind=kCustom, calls=%fused_computation.2 | custom fusion | bytes 4194432 | tf_op jit(solution)/shard_map/gather | solution.py:19
  59.5 0.0 copy-start.1
  59.5 11.1 %fusion.4 = f32[32,128,4,128]{3,1,2,0:T(8,128)S(1)} fusion(f32[32,4,128,128]{3,2,1,0:T(8,128)} %param.6, f32[32,128,128]{2,1,0:T(8,128)S(1)} %gather_fusion), kind=kOutput, calls=%fused_computation.7 | convolution fusion | flops 3221225472 | bytes 18874368 | tf_op jit(solution)/shard_map/tprl,tlj->tprj/dot_general | solution.py:18
  70.6 0.0 copy-done.1
  70.6 6.7 %fusion.2 = f32[4,128,128,1]{2,1,0,3:T(8,128)S(1)} fusion(f32[32,128,4,128]{3,1,2,0:T(8,128)S(1)} %fusion.4, f32[32,128,128]{2,1,0:T(8,128)S(1)} %copy-done.1), kind=kOutput, calls=%fused_computation.5 | convolution fusion | flops 3221225472 | bytes 10747904 | tf_op jit(solution)/shard_map/tprj,tri->pji/dot_general | solution.py:19
  77.3 14.1 %fusion = f32[32,128,128,1]{2,1,3,0:T(8,128)S(1)} fusion(f32[4,128,128,1]{2,1,0,3:T(8,128)S(1)} %fusion.2, f32[32,128,4,128]{3,1,2,0:T(8,128)S(1)} %fusion.4), kind=kOutput, calls=%fused_computation.3 | convolution fusion | flops 3221225472 | bytes 10747904 | tf_op jit(solution)/shard_map/tprj,pji->tri/dot_general | solution.py:20
  91.4 2.4 %fusion.7 = f32[32,128,128]{2,0,1:T(8,128)S(1)} fusion(f32[32,128,128,1]{2,1,3,0:T(8,128)S(1)} %fusion, s32[32]{0:T(128)S(1)} %get-tuple-element.6), kind=kOutput, calls=%fused_computation.10 | convolution fusion | flops 201327616 | bytes 4194432 | tf_op jit(solution)/shard_map/kt,tri->kri/dot_general | solution.py:25
  93.8 2.6 %copy.8 = f32[32,128,128]{2,1,0:T(8,128)} copy(f32[32,128,128]{2,0,1:T(8,128)S(1)} %fusion.7) | data formatting | bytes 4194304 | tf_op jit(solution)/shard_map/kt,tri->kri/dot_general | solution.py:25
  96.4 0.0 reduce-scatter.2.cloned.1.call-update
  96.4 60.5 %reduce-scatter.2.cloned.1.call-done = f32[256,128]{1,0:T(8,128)} async-done(((f32[4096,128]{1,0:T(8,128)}), f32[256,128]{1,0:T(8,128)}) %reduce-scatter.2.cloned.1.call-update) | async-done | bytes 131088 | tf_op jit(solution)/shard_map/reduce_scatter | solution.py:26
  (4 shorter events, 0.0 us)
Async XLA Ops:
  6.5 1.5 copy-start
  6.5 47.1 %all-gather.2.cloned.1.call-start = ((), (), s32[]{:S(2)}) async-start(), calls=%async_computation.1 | async-start | bytes 2228224 | tf_op jit(solution)/shard_map/all_gather | solution.py:13
  7.3 149.6 %reduce-scatter.2.cloned.1.call-start = ((), (), s32[]{:S(2)}) async-start(), calls=%async_computation.2 | async-start | bytes 2228224 | tf_op jit(solution)/shard_map/reduce_scatter | solution.py:26
  59.5 11.1 %copy-start.1 = (f32[32,128,128]{2,1,0:T(8,128)S(1)}, f32[32,128,128]{2,1,0:T(8,128)}, u32[]{:S(2)}) copy-start(f32[32,128,128]{2,1,0:T(8,128)} %gather_fusion.2) | copy-start | bytes 6291460
Sparse Core Ops, SparseCore 0:
  9.5 44.0 all-gather.1
  96.5 60.3 reduce-scatter.1
where the time goes:
time: 164 us
  waiting for transfers between devices  105 us (64%)
  matrix products  34.3 us (21%)
  between operations  13.5 us (8%)
  local copies, waits for them, and re-layouts  9.13 us (6%)
    reduce_scatter x1, waiting for transfers between devices, local(): lax.psum_scatter(summed.reshape(count, width), 'aux', scatter_dimension=0...  60.5 us
    all_gather x1, waiting for transfers between devices, local(): coeff = lax.all_gather(orbitals, 'aux', axis=0, tiled=True)  44.3 us
    dot_general x1, matrix products, local(): partial_value = jnp.einsum('tprj,pji->tri', half, fitted, precision=highest)  14.1 us
    dot_general x1, matrix products, local(): jnp.einsum('tprl,tlj->tprj', tiles, blocked[tile_cols], precision=highest)  11.1 us
    dot_general x1, matrix products, local(): jnp.einsum('tprj,tri->pji', half, blocked[row_block], precision=highest)  6.66 us
    gather x1, local copies, waits for them, and re-layouts, local(): blocked[row_block]  3.58 us
  transfers between devices with their start and end apart: 2, of which 2 were waited for; matrix products, arithmetic and copies ran while one was open for 1% of the time, Pallas kernels for 0%

commit v1 on v0

v1 whole, which is shorter than its diff:
```python
import functools

import jax
import jax.numpy as jnp
from jax import lax
from jax.experimental import pallas as pl
from jax.experimental.pallas import tpu as pltpu
from jax.sharding import PartitionSpec as P

F32, BF16 = jnp.float32, jnp.bfloat16
MIB = 1 << 20


def halves(x):
    hi = x.astype(BF16)
    return hi, (x - hi.astype(F32)).astype(BF16)


def dot(a, b):
    return jnp.dot(a, b, preferred_element_type=F32)


def prepare_kernel(per_owner, n_keys, owner_ref, sub_ref, cols_ref, order_ref, tiles_ref,
                   split_ref, tile_ref, slot_ref, first_ref, col_ref, key_ref, row_ref, used_ref, count_ref, buf, sem):
    n_tiles = tiles_ref.shape[0]
    depth, group = buf.shape[0], buf.shape[1]
    steps = n_tiles // group

    def fetch(step, at):
        return pltpu.make_async_copy(tiles_ref.at[pl.ds(step * group, group)], buf.at[at], sem.at[at])

    for step in range(min(depth, steps)):
        fetch(step, step).start()

    def clear(k, _):
        count_ref[k] = 0
        return 0

    lax.fori_loop(0, n_keys, clear, 0)

    def tally(t, _):
        k = owner_ref[t, 0] * per_owner + sub_ref[t]
        count_ref[k] += 1
        slot_ref[t] = 0
        key_ref[t] = 0
        row_ref[t] = 0
        return 0

    lax.fori_loop(0, n_tiles, tally, 0)

    def place(k, carry):
        start, used = carry
        here = count_ref[k]
        count_ref[k] = start

        @pl.when(here > 0)
        def _():
            key_ref[used] = k
            row_ref[used] = order_ref[k]
            slot_ref[start] = 1

        return start + here, used + (here > 0).astype(jnp.int32)

    _, used = lax.fori_loop(0, n_keys, place, (0, 0))
    used_ref[0] = used

    def settle(t, _):
        k = owner_ref[t, 0] * per_owner + sub_ref[t]
        at = count_ref[k]
        count_ref[k] = at + 1
        tile_ref[at] = t
        col_ref[at] = cols_ref[t]
        return 0

    lax.fori_loop(0, n_tiles, settle, 0)

    def number(t, last):
        first_ref[t] = slot_ref[t]
        now = last + slot_ref[t]
        slot_ref[t] = now
        return now

    lax.fori_loop(0, n_tiles, number, -1)

    for step in range(steps):
        at = step % depth
        fetch(step, at).wait()
        for i in range(group):
            hi, lo = halves(buf[at, i].reshape(-1, buf.shape[-1]))
            split_ref[step * group + i, :, : buf.shape[-1]] = hi
            split_ref[step * group + i, :, buf.shape[-1] :] = lo
        if step + depth < steps:
            fetch(step + depth, at).start()


def prepare(tile_owner, tile_sub, tile_cols, row_order, tiles, per_owner):
    n_tiles, aux_dev, block, _ = tiles.shape
    n_keys = row_order.shape[0]
    smem = pl.BlockSpec(memory_space=pltpu.SMEM)
    ints = jax.ShapeDtypeStruct((n_tiles,), jnp.int32)
    return pl.pallas_call(
        functools.partial(prepare_kernel, per_owner, n_keys),
        out_shape=(pltpu.VMEM((n_tiles, aux_dev * block, 2 * block), BF16),) + (ints,) * 6 + (jax.ShapeDtypeStruct((1,), jnp.int32),),
        in_specs=[smem] * 4 + [pl.BlockSpec(memory_space=pl.ANY)],
        out_specs=(pl.BlockSpec(memory_space=pltpu.VMEM),) + (smem,) * 7,
        scratch_shapes=[
            pltpu.SMEM((n_keys,), jnp.int32),
            pltpu.VMEM((4, 2, aux_dev, block, block), F32),
            pltpu.SemaphoreType.DMA((4,)),
        ],
        compiler_params=pltpu.CompilerParams(vmem_limit_bytes=24 * MIB),
        name="prepare",
    )(tile_owner, tile_sub, tile_cols, row_order, tiles)


class Grid:
    def __init__(self, n_aux):
        self.y, self.core = 2, 2
        self.z = n_aux // (self.y * self.core)
        self.offsets = [(k, j, c) for c in range(self.core) for k in range(self.z) for j in range(self.y)]

    def index(self, z, y, core):
        return (z * self.y + y) * self.core + core

    def other(self, me, offset):
        k, j, c = offset
        z, y, core = me // (self.y * self.core), me // self.core % self.y, me % self.core
        return self.index((z + k) % self.z, (y + j) % self.y, (core + c) % self.core)

    def shift(self, x, offset):
        return lax.ppermute(x, "aux", [(i, self.other(i, offset)) for i in range(self.z * self.y * self.core)])

    def back(self, offset):
        return (-offset[0]) % self.z, offset[1], offset[2]


def hops(grid):
    return sorted(range(1, grid.z), key=lambda k: min(k, grid.z - k))


def gather_shards(grid, x):
    held = {(0, 0, 0): x}
    for k in hops(grid):
        held[k, 0, 0] = grid.shift(x, (-k, 0, 0))
    for k in [0] + hops(grid):
        held[k, 1, 0] = grid.shift(held[k, 0, 0], (0, 1, 0))
    for k, j, _ in list(held):
        held[k, j, 1] = grid.shift(held[k, j, 0], (0, 0, 1))
    return [held[o] for o in grid.offsets]


def scatter_sums(grid, parts):
    order = hops(grid)[::-1] + [0]
    crossed = {k: grid.shift(parts[1][k], (0, 0, 1)) for k in order}
    total = {}
    for k in order:
        pair = parts[0][k] + crossed[k]
        total[k] = pair[0] + grid.shift(pair[1], (0, 1, 0))
    out = total[0]
    for k in order[:-1]:
        out = out + grid.shift(total[k], (k, 0, 0))
    return out


def exchange_kernel(grid, per_owner, tile_ref, slot_ref, first_ref, col_ref, key_ref, row_ref, used_ref, split_ref, *refs):
    n_tiles, rows, pair = split_ref.shape
    block = pair // 2
    aux_dev = rows // block
    n_shards = len(grid.offsets) if grid else 1
    shards, refs = refs[:n_shards], refs[n_shards:]
    *outs, coeff, wide, running, fitted, weights, summed = refs
    me = lax.axis_index("aux")
    if grid:
        for ref, offset in zip(shards, grid.offsets):
            coeff[pl.ds(grid.other(me, offset) * per_owner, per_owner)] = ref[...].reshape(per_owner, block, -1)
    else:
        coeff[...] = shards[0][...].reshape(coeff.shape)

    def half_step(t, _):
        c = coeff[col_ref[t]]
        c_hi, c_lo = halves(c)
        top = jnp.concatenate([c_hi, c_lo], axis=1)
        both = dot(split_ref[tile_ref[t]], jnp.concatenate([top, top], axis=0))
        value = both[:, :block] + both[:, block:]
        value = jnp.where(first_ref[t] == 1, value, value + running[...])
        running[...] = value
        hi, lo = halves(value)
        s = slot_ref[t]
        for p in range(aux_dev):
            wide[s, :, p * pair : p * pair + block] = hi[p * block : (p + 1) * block]
            wide[s, :, p * pair + block : (p + 1) * pair] = lo[p * block : (p + 1) * block]
        return 0

    lax.fori_loop(0, n_tiles, half_step, 0)
    used = used_ref[0]
    fitted[...] = jnp.zeros_like(fitted)

    def fit_step(s, _):
        c_hi, c_lo = halves(coeff[row_ref[s]].T)
        left = jnp.concatenate([jnp.concatenate([c_hi, c_hi], axis=1), jnp.concatenate([c_lo, c_lo], axis=1)], axis=0)
        w = wide[s]
        hi = jnp.concatenate([w[:, p * pair : p * pair + block] for p in range(aux_dev)], axis=1)
        lo = jnp.concatenate([w[:, p * pair + block : (p + 1) * pair] for p in range(aux_dev)], axis=1)
        fitted[...] += dot(left, jnp.concatenate([hi, lo], axis=0))
        return 0

    lax.fori_loop(0, used, fit_step, 0)
    for p in range(aux_dev):
        at = pl.ds(p * block, block)
        f_hi, f_lo = halves((fitted[:block, at] + fitted[block:, at]).T)
        both = jnp.concatenate([f_hi, f_lo], axis=1)
        weights[p * pair : p * pair + block, :] = both
        weights[p * pair + block : (p + 1) * pair, :] = both
    if grid:
        summed[...] = jnp.zeros_like(summed)
    else:
        outs[0][...] = jnp.zeros_like(outs[0])

    def out_step(s, _):
        both = dot(wide[s], weights[...])
        value = both[:, :block] + both[:, block:]
        if grid:
            summed[key_ref[s]] = value
        else:
            outs[0][pl.ds(pl.multiple_of(key_ref[s] * block, block), block)] = value
        return 0

    lax.fori_loop(0, used, out_step, 0)
    if grid:
        for c in range(grid.core):
            for k in range(grid.z):
                for j in range(grid.y):
                    at = grid.other(me, (k, j, c)) * per_owner
                    outs[c * grid.z + k][j] = summed[pl.ds(at, per_owner)].reshape(outs[0].shape[1:])


def exchange(grid, meta, split, shards, n_blocks, per_owner):
    n_tiles, rows, pair = split.shape
    block, width = pair // 2, shards[0].shape[1]
    aux_dev = rows // block
    smem = pl.BlockSpec(memory_space=pltpu.SMEM)
    vmem = pl.BlockSpec(memory_space=pltpu.VMEM)
    if grid:
        out_shape = [pltpu.VMEM((grid.y, per_owner * block, width), F32)] * (grid.core * grid.z)
    else:
        out_shape = [jax.ShapeDtypeStruct((n_blocks * block, width), F32)]
    return pl.pallas_call(
        functools.partial(exchange_kernel, grid, per_owner),
        out_shape=out_shape,
        in_specs=[smem] * 7 + [vmem] * (1 + len(shards)),
        out_specs=[vmem] * len(out_shape),
        scratch_shapes=[
            pltpu.VMEM((n_blocks, block, width), F32),
            pltpu.VMEM((n_tiles, block, aux_dev * pair), BF16),
            pltpu.VMEM((rows, width), F32),
            pltpu.VMEM((2 * width, aux_dev * block), F32),
            pltpu.VMEM((aux_dev * pair, 2 * width), BF16),
            pltpu.VMEM((n_blocks if grid else 1, block, width), F32),
        ],
        compiler_params=pltpu.CompilerParams(vmem_limit_bytes=48 * MIB),
        name="exchange",
    )(*meta, split, *shards)


def local(tiles, tile_owner, tile_sub, tile_cols, row_order, orbitals):
    n_aux = lax.axis_size("aux")
    n_blocks = row_order.shape[0]
    per_owner = n_blocks // n_aux
    grid = Grid(n_aux) if n_aux % 4 == 0 and n_aux <= 16 else None
    if grid:
        shards = gather_shards(grid, orbitals)
    else:
        shards = [lax.all_gather(orbitals, "aux", axis=0, tiled=True)]
    split, *meta = prepare(tile_owner, tile_sub, tile_cols, row_order, tiles, per_owner)
    split = pltpu.with_memory_space_constraint(split, pltpu.VMEM)
    outs = exchange(grid, meta, split, shards, n_blocks, per_owner)
    if not grid:
        return lax.psum_scatter(outs[0], "aux", scatter_dimension=0, tiled=True)
    return scatter_sums(grid, [outs[: grid.z], outs[grid.z :]])


def solution(mesh):
    in_specs = (
        P(("grp", "aux"), None, None, None),
        P(("grp", "aux"), None),
        P(("grp", "aux")),
        P(("grp", "aux")),
        P("grp"),
        P(("grp", "aux"), None),
    )
    out_specs = P(("grp", "aux"), None)
    return jax.shard_map(local, mesh=mesh, in_specs=in_specs, out_specs=out_specs, check_vma=False)
```

time: 164 us -> 87.4 us (0.53)
  waiting for transfers between devices: 105 us -> 25.6 us
  matrix products: 34.3 us -> 0 us
  Pallas kernels: 0 us -> 26.9 us
  starting transfers between devices: 0.04 us -> 26.8 us
  between operations: 13.5 us -> 0.32 us
  local copies, waits for them, and re-layouts: 9.13 us -> 6.84 us
    reduce_scatter x1 -> x0, waiting for transfers between devices: 60.5 us -> none  [local(): lax.psum_scatter(summed.reshape(count, width), 'aux', scatter_dimension=0...]
    all_gather x1 -> x0, waiting for transfers between devices: 44.3 us -> none  [local(): coeff = lax.all_gather(orbitals, 'aux', axis=0, tiled=True)]
    dot_general x4 -> x0, matrix products: 34.3 us -> none  [the longest x1 14.1 us: local(): partial_value = jnp.einsum('tprj,pji->tri', half, fitted, precision=highest)]
    pallas_call x0 -> x2, Pallas kernels: none -> 26.9 us  [the longest x1 21.8 us: exchange(): pl.pallas_call(functools.partial(exchange_kernel, grid, per_owner), out_s...]
    ppermute x0 -> x26, starting transfers between devices: none -> 26.8 us  [shift(): lax.ppermute(x, 'aux', [(i, self.other(i, offset)) for i in range(self.z...]
    ppermute x0 -> x26, waiting for transfers between devices: none -> 25.6 us  [shift(): lax.ppermute(x, 'aux', [(i, self.other(i, offset)) for i in range(self.z...]
    unnamed x4 -> x51, local copies, waits for them, and re-layouts: 0.01 us -> 6.81 us
    gather x3 -> x0, local copies, waits for them, and re-layouts: 6.55 us -> none  [the longest x1 3.58 us: local(): blocked[row_block]]
  transfers between devices with their start and end apart: 2 -> 26, of which waited for: 2 -> 11; matrix products, arithmetic and copies ran while one was open for 1% -> 1% of each run, Pallas kernels for 0% -> 6%
where the time goes in v1:
time: 87.4 us
  Pallas kernels  26.9 us (31%)
  starting transfers between devices  26.8 us (31%)
  waiting for transfers between devices  25.6 us (29%)
  local copies, waits for them, and re-layouts  6.84 us (8%)
  other arithmetic  0.91 us (1%)
    ppermute x26, starting transfers between devices, shift(): lax.ppermute(x, 'aux', [(i, self.other(i, offset)) for i in range(self.z...  26.8 us
    ppermute x26, waiting for transfers between devices, shift(): lax.ppermute(x, 'aux', [(i, self.other(i, offset)) for i in range(self.z...  25.6 us
    pallas_call x1, Pallas kernels, exchange(): pl.pallas_call(functools.partial(exchange_kernel, grid, per_owner), out_s...  21.8 us
    unnamed x51, local copies, waits for them, and re-layouts  6.81 us
    pallas_call x1, Pallas kernels, prepare(): pl.pallas_call(functools.partial(prepare_kernel, per_owner, n_keys), out_...  5.19 us
  transfers between devices with their start and end apart: 26, of which 11 were waited for; matrix products, arithmetic and copies ran while one was open for 1% of the time, Pallas kernels for 6%

profile of v1, /device:TPU:0, one launch (start us, length us, event | category | flops | bytes accessed | tf_op | source)
XLA Modules:
  0.0 87.4 jit_solution(17724287850989287317)
XLA Ops:
  0.0 3.0 %collective-permute-start.5 = (f32[256,128]{1,0:T(8,128)}, f32[256,128]{1,0:T(8,128)S(1)}, u32[]{:S(2)}, u32[]{:S(2)}) collective-permute-start(f32[256,128]{1,0:T(8,128)} %refs_0_.1), channel_id=1, source_target_pairs={{0,4},{1,5},{2,6},{3,7},{4,8},{5,9},{6,10},{7,11},{8,12},{9,13},{1... | collective-permute-start | bytes 393224 | tf_op jit(solution)/shard_map/ppermute | solution.py:131
  3.0 2.6 %collective-permute-start.3 = (f32[256,128]{1,0:T(8,128)}, f32[256,128]{1,0:T(8,128)S(1)}, u32[]{:S(2)}, u32[]{:S(2)}) collective-permute-start(f32[256,128]{1,0:T(8,128)} %refs_0_.1), channel_id=1, source_target_pairs={{0,8},{1,9},{2,10},{3,11},{4,12},{5,13},{6,14},{7,15},{8,0},{9,1},... | collective-permute-start | bytes 393224 | tf_op jit(solution)/shard_map/ppermute | solution.py:131
  5.6 1.3 %collective-permute-start.1 = (f32[256,128]{1,0:T(8,128)}, f32[256,128]{1,0:T(8,128)S(1)}, u32[]{:S(2)}, u32[]{:S(2)}) collective-permute-start(f32[256,128]{1,0:T(8,128)} %refs_0_.1), channel_id=1, source_target_pairs={{0,12},{1,13},{2,14},{3,15},{4,0},{5,1},{6,2},{7,3},{8,4},{9,5},{1... | collective-permute-start | bytes 393224 | tf_op jit(solution)/shard_map/ppermute | solution.py:131
  7.0 1.5 %collective-permute-start = (f32[256,128]{1,0:T(8,128)}, f32[256,128]{1,0:T(8,128)S(1)}, u32[]{:S(2)}, u32[]{:S(2)}) collective-permute-start(f32[256,128]{1,0:T(8,128)} %refs_0_.1), channel_id=1, source_target_pairs={{0,2},{1,3},{2,0},{3,1},{4,6},{5,7},{6,4},{7,5},{8,10},{9,11},{10,... | collective-permute-start | bytes 393224 | tf_op jit(solution)/shard_map/ppermute | solution.py:131
  8.5 0.0 collective-permute-start.7
  8.5 1.2 %collective-permute-done.5.refs_6_ = f32[256,128]{1,0:T(8,128)S(1)} collective-permute-done((f32[256,128]{1,0:T(8,128)}, f32[256,128]{1,0:T(8,128)S(1)}, u32[]{:S(2)}, u32[]{:S(2)}) %collective-permute-start.5) | collective-permute-done | bytes 131104 | tf_op jit(solution)/shard_map/ppermute | solution.py:131
  9.7 0.0 collective-permute-start.13
  9.7 4.8 %collective-permute-done.3.refs_4_ = f32[256,128]{1,0:T(8,128)S(1)} collective-permute-done((f32[256,128]{1,0:T(8,128)}, f32[256,128]{1,0:T(8,128)S(1)}, u32[]{:S(2)}, u32[]{:S(2)}) %collective-permute-start.3) | collective-permute-done | bytes 131104 | tf_op jit(solution)/shard_map/ppermute | solution.py:131
  14.5 1.5 %collective-permute-start.6 = (f32[256,128]{1,0:T(8,128)S(1)}, f32[256,128]{1,0:T(8,128)S(1)}, u32[]{:S(2)}, u32[]{:S(2)}) collective-permute-start(f32[256,128]{1,0:T(8,128)S(1)} %collective-permute-done.5.refs_6_), channel_id=1, source_target_pairs={{0,2},{1,3},{2,0},{3,1},{4,6},{5,7},{6,4},{7,5},{8,10},{9,11},{10,... | collective-permute-start | bytes 393224 | tf_op jit(solution)/shard_map/ppermute | solution.py:131
  16.0 0.0 collective-permute-done.1.refs_2_
  16.0 0.0 collective-permute-start.11
  16.0 0.0 collective-permute-done.refs_1_
  16.0 0.0 copy-start.13
  16.0 0.6 collective-permute-start.4
  16.6 0.0 collective-permute-done.7.refs_8_
  16.6 1.5 %collective-permute-start.2 = (f32[256,128]{1,0:T(8,128)S(1)}, f32[256,128]{1,0:T(8,128)S(1)}, u32[]{:S(2)}, u32[]{:S(2)}) collective-permute-start(f32[256,128]{1,0:T(8,128)S(1)} %collective-permute-done.1.refs_2_), channel_id=1, source_target_pairs={{0,2},{1,3},{2,0},{3,1},{4,6},{5,7},{6,4},{7,5},{8,10},{9,11},{10,... | collective-permute-start | bytes 393224 | tf_op jit(solution)/shard_map/ppermute | solution.py:131
  18.1 0.0 collective-permute-done.13.refs_14_
  18.1 0.0 collective-permute-start.9
  18.1 2.3 %collective-permute-done.6.refs_7_ = f32[256,128]{1,0:T(8,128)S(1)} collective-permute-done((f32[256,128]{1,0:T(8,128)S(1)}, f32[256,128]{1,0:T(8,128)S(1)}, u32[]{:S(2)}, u32[]{:S(2)}) %collective-permute-start.6) | collective-permute-done | bytes 131104 | tf_op jit(solution)/shard_map/ppermute | solution.py:131
  20.5 0.0 collective-permute-start.8
  20.5 0.0 collective-permute-done.11.refs_12_
  20.5 0.5 collective-permute-start.14
  21.0 2.3 %collective-permute-done.4.refs_5_ = f32[256,128]{1,0:T(8,128)S(1)} collective-permute-done((f32[256,128]{1,0:T(8,128)S(1)}, f32[256,128]{1,0:T(8,128)S(1)}, u32[]{:S(2)}, u32[]{:S(2)}) %collective-permute-start.4) | collective-permute-done | bytes 131104 | tf_op jit(solution)/shard_map/ppermute | solution.py:131
  23.3 0.0 collective-permute-start.12
  23.3 2.1 %collective-permute-done.2.refs_3_ = f32[256,128]{1,0:T(8,128)S(1)} collective-permute-done((f32[256,128]{1,0:T(8,128)S(1)}, f32[256,128]{1,0:T(8,128)S(1)}, u32[]{:S(2)}, u32[]{:S(2)}) %collective-permute-start.2) | collective-permute-done | bytes 131104 | tf_op jit(solution)/shard_map/ppermute | solution.py:131
  25.4 0.0 collective-permute-start.10
  25.4 0.7 copy.7.owner_ref
  26.2 3.4 %copy-done = f32[32,4,128,128]{3,2,1,0:T(8,128)S(1)} copy-done((f32[32,4,128,128]{3,2,1,0:T(8,128)S(1)}, f32[32,4,128,128]{3,2,1,0:T(8,128)}, u32[]{:S(2)}) %copy-start) | copy-done | bytes 8388632
  29.5 0.7 copy-done.1
  30.2 0.7 copy-done.2
  30.8 0.7 copy-done.3
  31.5 5.2 %prepare.1 = (bf16[32,512,256]{2,1,0:T(8,128)(2,1)S(1)}, s32[32]{0:T(128)S(1)}, s32[32]{0:T(128)S(1)}, s32[32]{0:T(128)S(1)}, s32[32]{0:T(128)S(1)}, /*index=5*/s32[32]{0:T(128)S(1)}, s32[32]{0:T(128)S(1)}, s32[1]{0:T(128)}) custom-call(s32[32,1]{1,0:T(8,128)S(1)} %copy.7.owner_ref, s32[32]{0:T(128)S(1)} %copy-done.1, s32[32]{0:T(128)S(1)} %copy-done.2, ...), custom_call_target="tpu_custom_call" | custom-call | tf_op jit(solution)/shard_map/prepare/pallas_call | solution.py:101
  36.8 0.0 collective-permute-done.9.refs_10_
  36.8 0.0 collective-permute-done.14.refs_15_
  36.8 0.0 collective-permute-done.12.refs_13_
  36.9 0.4 copy-done.4
  37.3 0.0 copy-done.5
  37.3 0.0 copy-done.8
  37.4 0.0 copy-done.20
  37.4 0.0 copy-done.21
  37.5 0.1 copy-done.22
  37.5 0.0 copy-done.23
  37.6 0.0 copy-done.24
  37.6 21.8 %exchange.1 = (f32[2,256,128]{2,1,0:T(8,128)S(1)}, f32[2,256,128]{2,1,0:T(8,128)S(1)}, f32[2,256,128]{2,1,0:T(8,128)S(1)}, f32[2,256,128]{2,1,0:T(8,128)S(1)}, f...) custom-call(s32[32]{0:T(128)} %copy-done.4, ...), custom_call_target="tpu_custom_call" | custom-call | tf_op jit(solution)/shard_map/exchange/pallas_call | solution.py:247
  59.4 2.6 %collective-permute-start.15 = (f32[2,256,128]{2,1,0:T(8,128)S(1)}, f32[2,256,128]{2,1,0:T(8,128)S(1)}, u32[]{:S(2)}, u32[]{:S(2)}) collective-permute-start(f32[2,256,128]{2,1,0:T(8,128)S(1)} %get-tuple-element.30), channel_id=1, source_target_pairs={{0,1},{1,0},{2,3},{3,2},{4,5},{5,4},{6,7},{7,6},{8,9},{9,8},{10,11... | collective-permute-start | bytes 786440 | tf_op jit(solution)/shard_map/ppermute | solution.py:131
  62.0 0.1 collective-permute-start.17
  62.0 0.4 collective-permute-start.20
  62.5 0.1 collective-permute-start.23
  62.6 0.6 collective-permute-done.15
  63.2 2.0 %collective-permute-start.16 = (f32[256,128]{1,0:T(8,128)S(1)}, f32[256,128]{1,0:T(8,128)S(1)}, u32[]{:S(2)}, u32[]{:S(2)}) collective-permute-start(f32[256,128]{1,0:T(8,128)S(1)} %slice_bitcast_fusion.6), channel_id=1, source_target_pairs={{0,2},{1,3},{2,0},{3,1},{4,6},{5,7},{6,4},{7,5},{8,10},{9,11},{10,... | collective-permute-start | bytes 393224 | tf_op jit(solution)/shard_map/ppermute | solution.py:131
  65.1 0.0 collective-permute-done.17
  65.2 0.3 collective-permute-start.18
  65.5 0.0 collective-permute-done.20
  65.6 1.8 %collective-permute-start.21 = (f32[256,128]{1,0:T(8,128)S(1)}, f32[256,128]{1,0:T(8,128)S(1)}, u32[]{:S(2)}, u32[]{:S(2)}) collective-permute-start(f32[256,128]{1,0:T(8,128)S(1)} %slice_bitcast_fusion.2), channel_id=1, source_target_pairs={{0,2},{1,3},{2,0},{3,1},{4,6},{5,7},{6,4},{7,5},{8,10},{9,11},{10,... | collective-permute-start | bytes 393224 | tf_op jit(solution)/shard_map/ppermute | solution.py:131
  67.5 0.3 collective-permute-start.24
  67.8 4.6 %collective-permute-done.18 = f32[256,128]{1,0:T(8,128)S(1)} collective-permute-done((f32[256,128]{1,0:T(8,128)S(1)}, f32[256,128]{1,0:T(8,128)S(1)}, u32[]{:S(2)}, u32[]{:S(2)}) %collective-permute-start.18) | collective-permute-done | bytes 131104 | tf_op jit(solution)/shard_map/ppermute | solution.py:131
  72.4 1.9 %collective-permute-start.19 = (f32[256,128]{1,0:T(8,128)S(1)}, f32[256,128]{1,0:T(8,128)S(1)}, u32[]{:S(2)}, u32[]{:S(2)}) collective-permute-start(f32[256,128]{1,0:T(8,128)S(1)} %fusion.2), channel_id=1, source_target_pairs={{0,8},{1,9},{2,10},{3,11},{4,12},{5,13},{6,14},{7,15},{8,0},{9,1},... | collective-permute-start | bytes 393224 | tf_op jit(solution)/shard_map/ppermute | solution.py:131
  74.4 0.8 collective-permute-done.21
  75.2 4.6 %collective-permute-start.22 = (f32[256,128]{1,0:T(8,128)S(1)}, f32[256,128]{1,0:T(8,128)S(1)}, u32[]{:S(2)}, u32[]{:S(2)}) collective-permute-start(f32[256,128]{1,0:T(8,128)S(1)} %fusion.1), channel_id=1, source_target_pairs={{0,12},{1,13},{2,14},{3,15},{4,0},{5,1},{6,2},{7,3},{8,4},{9,5},{1... | collective-permute-start | bytes 393224 | tf_op jit(solution)/shard_map/ppermute | solution.py:131
  79.8 0.1 collective-permute-start.25
  79.9 2.1 %collective-permute-done.19 = f32[256,128]{1,0:T(8,128)S(1)} collective-permute-done((f32[256,128]{1,0:T(8,128)S(1)}, f32[256,128]{1,0:T(8,128)S(1)}, u32[]{:S(2)}, u32[]{:S(2)}) %collective-permute-start.19) | collective-permute-done | bytes 131104 | tf_op jit(solution)/shard_map/ppermute | solution.py:131
  82.0 1.7 %collective-permute-done.22 = f32[256,128]{1,0:T(8,128)S(1)} collective-permute-done((f32[256,128]{1,0:T(8,128)S(1)}, f32[256,128]{1,0:T(8,128)S(1)}, u32[]{:S(2)}, u32[]{:S(2)}) %collective-permute-start.22) | collective-permute-done | bytes 131104 | tf_op jit(solution)/shard_map/ppermute | solution.py:131
  83.7 3.0 %collective-permute-done.25 = f32[256,128]{1,0:T(8,128)S(1)} collective-permute-done((f32[256,128]{1,0:T(8,128)S(1)}, f32[256,128]{1,0:T(8,128)S(1)}, u32[]{:S(2)}, u32[]{:S(2)}) %collective-permute-start.25) | collective-permute-done | bytes 131104 | tf_op jit(solution)/shard_map/ppermute | solution.py:131
  86.7 0.7 fusion.6
  (53 shorter events, 0.3 us)
Async XLA Ops:
  0.0 9.7 %collective-permute-start.5 = (f32[256,128]{1,0:T(8,128)}, f32[256,128]{1,0:T(8,128)S(1)}, u32[]{:S(2)}, u32[]{:S(2)}) collective-permute-start(f32[256,128]{1,0:T(8,128)} %refs_0_.1), channel_id=1, source_target_pairs={{0,4},{1,5},{2,6},{3,7},{4,8},{5,9},{6,10},{7,11},{8,12},{9,13},{1... | collective-permute-start | bytes 393224 | tf_op jit(solution)/shard_map/ppermute | solution.py:131
  3.0 11.4 %collective-permute-start.3 = (f32[256,128]{1,0:T(8,128)}, f32[256,128]{1,0:T(8,128)S(1)}, u32[]{:S(2)}, u32[]{:S(2)}) collective-permute-start(f32[256,128]{1,0:T(8,128)} %refs_0_.1), channel_id=1, source_target_pairs={{0,8},{1,9},{2,10},{3,11},{4,12},{5,13},{6,14},{7,15},{8,0},{9,1},... | collective-permute-start | bytes 393224 | tf_op jit(solution)/shard_map/ppermute | solution.py:131
  5.6 10.4 %collective-permute-start.1 = (f32[256,128]{1,0:T(8,128)}, f32[256,128]{1,0:T(8,128)S(1)}, u32[]{:S(2)}, u32[]{:S(2)}) collective-permute-start(f32[256,128]{1,0:T(8,128)} %refs_0_.1), channel_id=1, source_target_pairs={{0,12},{1,13},{2,14},{3,15},{4,0},{5,1},{6,2},{7,3},{8,4},{9,5},{1... | collective-permute-start | bytes 393224 | tf_op jit(solution)/shard_map/ppermute | solution.py:131
  7.0 9.0 %collective-permute-start = (f32[256,128]{1,0:T(8,128)}, f32[256,128]{1,0:T(8,128)S(1)}, u32[]{:S(2)}, u32[]{:S(2)}) collective-permute-start(f32[256,128]{1,0:T(8,128)} %refs_0_.1), channel_id=1, source_target_pairs={{0,2},{1,3},{2,0},{3,1},{4,6},{5,7},{6,4},{7,5},{8,10},{9,11},{10,... | collective-permute-start | bytes 393224 | tf_op jit(solution)/shard_map/ppermute | solution.py:131
  8.5 8.1 %collective-permute-start.7 = (f32[256,128]{1,0:T(8,128)}, f32[256,128]{1,0:T(8,128)S(1)}, u32[]{:S(2)}, u32[]{:S(2)}) collective-permute-start(f32[256,128]{1,0:T(8,128)} %refs_0_.1), channel_id=1, source_target_pairs={{0,1},{1,0},{2,3},{3,2},{4,5},{5,4},{6,7},{7,6},{8,9},{9,8},{10,11... | collective-permute-start | bytes 393224 | tf_op jit(solution)/shard_map/ppermute | solution.py:131
  9.7 27.7 %copy-start.10 = (f32[256,128]{1,0:T(8,128)}, f32[256,128]{1,0:T(8,128)S(1)}, u32[]{:S(2)}) copy-start(f32[256,128]{1,0:T(8,128)S(1)} %collective-permute-done.5.refs_6_) | copy-start | bytes 393220
  9.7 8.4 %collective-permute-start.13 = (f32[256,128]{1,0:T(8,128)S(1)}, f32[256,128]{1,0:T(8,128)S(1)}, u32[]{:S(2)}, u32[]{:S(2)}) collective-permute-start(f32[256,128]{1,0:T(8,128)S(1)} %collective-permute-done.5.refs_6_), channel_id=1, source_target_pairs={{0,1},{1,0},{2,3},{3,2},{4,5},{5,4},{6,7},{7,6},{8,9},{9,8},{10,11... | collective-permute-start | bytes 393224 | tf_op jit(solution)/shard_map/ppermute | solution.py:131
  14.5 22.9 %copy-start.11 = (f32[256,128]{1,0:T(8,128)}, f32[256,128]{1,0:T(8,128)S(1)}, u32[]{:S(2)}) copy-start(f32[256,128]{1,0:T(8,128)S(1)} %collective-permute-done.3.refs_4_) | copy-start | bytes 393220
  14.5 6.0 %collective-permute-start.6 = (f32[256,128]{1,0:T(8,128)S(1)}, f32[256,128]{1,0:T(8,128)S(1)}, u32[]{:S(2)}, u32[]{:S(2)}) collective-permute-start(f32[256,128]{1,0:T(8,128)S(1)} %collective-permute-done.5.refs_6_), channel_id=1, source_target_pairs={{0,2},{1,3},{2,0},{3,1},{4,6},{5,7},{6,4},{7,5},{8,10},{9,11},{10,... | collective-permute-start | bytes 393224 | tf_op jit(solution)/shard_map/ppermute | solution.py:131
  16.0 21.4 %copy-start.12 = (f32[256,128]{1,0:T(8,128)}, f32[256,128]{1,0:T(8,128)S(1)}, u32[]{:S(2)}) copy-start(f32[256,128]{1,0:T(8,128)S(1)} %collective-permute-done.1.refs_2_) | copy-start | bytes 393220
  16.0 4.5 %collective-permute-start.11 = (f32[256,128]{1,0:T(8,128)S(1)}, f32[256,128]{1,0:T(8,128)S(1)}, u32[]{:S(2)}, u32[]{:S(2)}) collective-permute-start(f32[256,128]{1,0:T(8,128)S(1)} %collective-permute-done.3.refs_4_), channel_id=1, source_target_pairs={{0,1},{1,0},{2,3},{3,2},{4,5},{5,4},{6,7},{7,6},{8,9},{9,8},{10,11... | collective-permute-start | bytes 393224 | tf_op jit(solution)/shard_map/ppermute | solution.py:131
  16.0 21.3 %copy-start.13 = (f32[256,128]{1,0:T(8,128)}, f32[256,128]{1,0:T(8,128)S(1)}, u32[]{:S(2)}) copy-start(f32[256,128]{1,0:T(8,128)S(1)} %collective-permute-done.refs_1_) | copy-start | bytes 393220
  16.0 7.2 %collective-permute-start.4 = (f32[256,128]{1,0:T(8,128)S(1)}, f32[256,128]{1,0:T(8,128)S(1)}, u32[]{:S(2)}, u32[]{:S(2)}) collective-permute-start(f32[256,128]{1,0:T(8,128)S(1)} %collective-permute-done.3.refs_4_), channel_id=1, source_target_pairs={{0,2},{1,3},{2,0},{3,1},{4,6},{5,7},{6,4},{7,5},{8,10},{9,11},{10,... | collective-permute-start | bytes 393224 | tf_op jit(solution)/shard_map/ppermute | solution.py:131
  16.6 20.8 %copy-start.14 = (f32[256,128]{1,0:T(8,128)}, f32[256,128]{1,0:T(8,128)S(1)}, u32[]{:S(2)}) copy-start(f32[256,128]{1,0:T(8,128)S(1)} %collective-permute-done.7.refs_8_) | copy-start | bytes 393220
  16.6 8.8 %collective-permute-start.2 = (f32[256,128]{1,0:T(8,128)S(1)}, f32[256,128]{1,0:T(8,128)S(1)}, u32[]{:S(2)}, u32[]{:S(2)}) collective-permute-start(f32[256,128]{1,0:T(8,128)S(1)} %collective-permute-done.1.refs_2_), channel_id=1, source_target_pairs={{0,2},{1,3},{2,0},{3,1},{4,6},{5,7},{6,4},{7,5},{8,10},{9,11},{10,... | collective-permute-start | bytes 393224 | tf_op jit(solution)/shard_map/ppermute | solution.py:131
  18.1 19.2 %copy-start.15 = (f32[256,128]{1,0:T(8,128)}, f32[256,128]{1,0:T(8,128)S(1)}, u32[]{:S(2)}) copy-start(f32[256,128]{1,0:T(8,128)S(1)} %collective-permute-done.13.refs_14_) | copy-start | bytes 393220
  18.1 18.6 %collective-permute-start.9 = (f32[256,128]{1,0:T(8,128)S(1)}, f32[256,128]{1,0:T(8,128)S(1)}, u32[]{:S(2)}, u32[]{:S(2)}) collective-permute-start(f32[256,128]{1,0:T(8,128)S(1)} %collective-permute-done.1.refs_2_), channel_id=1, source_target_pairs={{0,1},{1,0},{2,3},{3,2},{4,5},{5,4},{6,7},{7,6},{8,9},{9,8},{10,11... | collective-permute-start | bytes 393224 | tf_op jit(solution)/shard_map/ppermute | solution.py:131
  20.5 16.9 %copy-start.16 = (f32[256,128]{1,0:T(8,128)}, f32[256,128]{1,0:T(8,128)S(1)}, u32[]{:S(2)}) copy-start(f32[256,128]{1,0:T(8,128)S(1)} %collective-permute-done.6.refs_7_) | copy-start | bytes 393220
  20.5 16.3 %collective-permute-start.8 = (f32[256,128]{1,0:T(8,128)S(1)}, f32[256,128]{1,0:T(8,128)S(1)}, u32[]{:S(2)}, u32[]{:S(2)}) collective-permute-start(f32[256,128]{1,0:T(8,128)S(1)} %collective-permute-done.refs_1_), channel_id=1, source_target_pairs={{0,1},{1,0},{2,3},{3,2},{4,5},{5,4},{6,7},{7,6},{8,9},{9,8},{10,11... | collective-permute-start | bytes 393224 | tf_op jit(solution)/shard_map/ppermute | solution.py:131
  20.5 16.9 %copy-start.17 = (f32[256,128]{1,0:T(8,128)}, f32[256,128]{1,0:T(8,128)S(1)}, u32[]{:S(2)}) copy-start(f32[256,128]{1,0:T(8,128)S(1)} %collective-permute-done.11.refs_12_) | copy-start | bytes 393220
  20.5 16.3 %collective-permute-start.14 = (f32[256,128]{1,0:T(8,128)S(1)}, f32[256,128]{1,0:T(8,128)S(1)}, u32[]{:S(2)}, u32[]{:S(2)}) collective-permute-start(f32[256,128]{1,0:T(8,128)S(1)} %collective-permute-done.6.refs_7_), channel_id=1, source_target_pairs={{0,1},{1,0},{2,3},{3,2},{4,5},{5,4},{6,7},{7,6},{8,9},{9,8},{10,11... | collective-permute-start | bytes 393224 | tf_op jit(solution)/shard_map/ppermute | solution.py:131
  23.3 14.1 %copy-start.18 = (f32[256,128]{1,0:T(8,128)}, f32[256,128]{1,0:T(8,128)S(1)}, u32[]{:S(2)}) copy-start(f32[256,128]{1,0:T(8,128)S(1)} %collective-permute-done.4.refs_5_) | copy-start | bytes 393220
  23.3 13.6 %collective-permute-start.12 = (f32[256,128]{1,0:T(8,128)S(1)}, f32[256,128]{1,0:T(8,128)S(1)}, u32[]{:S(2)}, u32[]{:S(2)}) collective-permute-start(f32[256,128]{1,0:T(8,128)S(1)} %collective-permute-done.4.refs_5_), channel_id=1, source_target_pairs={{0,1},{1,0},{2,3},{3,2},{4,5},{5,4},{6,7},{7,6},{8,9},{9,8},{10,11... | collective-permute-start | bytes 393224 | tf_op jit(solution)/shard_map/ppermute | solution.py:131
  25.4 12.0 %copy-start.19 = (f32[256,128]{1,0:T(8,128)}, f32[256,128]{1,0:T(8,128)S(1)}, u32[]{:S(2)}) copy-start(f32[256,128]{1,0:T(8,128)S(1)} %collective-permute-done.2.refs_3_) | copy-start | bytes 393220
  25.4 11.4 %collective-permute-start.10 = (f32[256,128]{1,0:T(8,128)S(1)}, f32[256,128]{1,0:T(8,128)S(1)}, u32[]{:S(2)}, u32[]{:S(2)}) collective-permute-start(f32[256,128]{1,0:T(8,128)S(1)} %collective-permute-done.2.refs_3_), channel_id=1, source_target_pairs={{0,1},{1,0},{2,3},{3,2},{4,5},{5,4},{6,7},{7,6},{8,9},{9,8},{10,11... | collective-permute-start | bytes 393224 | tf_op jit(solution)/shard_map/ppermute | solution.py:131
  26.2 3.4 %copy-start = (f32[32,4,128,128]{3,2,1,0:T(8,128)S(1)}, f32[32,4,128,128]{3,2,1,0:T(8,128)}, u32[]{:S(2)}) copy-start(f32[32,4,128,128]{3,2,1,0:T(8,128)} %tiles_ref.1) | copy-start | bytes 25165828
  29.5 0.7 copy-start.1
  30.2 0.7 copy-start.2
  30.8 0.7 copy-start.3
  36.7 0.6 copy-start.4
  36.7 0.6 copy-start.5
  36.7 0.6 copy-start.6
  36.7 0.6 copy-start.7
  36.7 0.6 copy-start.8
  36.8 0.6 copy-start.9
  36.8 0.7 copy-start.20
  36.8 0.7 copy-start.21
  36.8 0.7 copy-start.22
  36.8 0.7 copy-start.23
  36.9 0.8 copy-start.24
  59.4 3.8 %collective-permute-start.15 = (f32[2,256,128]{2,1,0:T(8,128)S(1)}, f32[2,256,128]{2,1,0:T(8,128)S(1)}, u32[]{:S(2)}, u32[]{:S(2)}) collective-permute-start(f32[2,256,128]{2,1,0:T(8,128)S(1)} %get-tuple-element.30), channel_id=1, source_target_pairs={{0,1},{1,0},{2,3},{3,2},{4,5},{5,4},{6,7},{7,6},{8,9},{9,8},{10,11... | collective-permute-start | bytes 786440 | tf_op jit(solution)/shard_map/ppermute | solution.py:131
  62.0 3.2 %collective-permute-start.17 = (f32[2,256,128]{2,1,0:T(8,128)S(1)}, f32[2,256,128]{2,1,0:T(8,128)S(1)}, u32[]{:S(2)}, u32[]{:S(2)}) collective-permute-start(f32[2,256,128]{2,1,0:T(8,128)S(1)} %get-tuple-element.32), channel_id=1, source_target_pairs={{0,1},{1,0},{2,3},{3,2},{4,5},{5,4},{6,7},{7,6},{8,9},{9,8},{10,11... | collective-permute-start | bytes 786440 | tf_op jit(solution)/shard_map/ppermute | solution.py:131
  62.0 3.5 %collective-permute-start.20 = (f32[2,256,128]{2,1,0:T(8,128)S(1)}, f32[2,256,128]{2,1,0:T(8,128)S(1)}, u32[]{:S(2)}, u32[]{:S(2)}) collective-permute-start(f32[2,256,128]{2,1,0:T(8,128)S(1)} %get-tuple-element.34), channel_id=1, source_target_pairs={{0,1},{1,0},{2,3},{3,2},{4,5},{5,4},{6,7},{7,6},{8,9},{9,8},{10,11... | collective-permute-start | bytes 786440 | tf_op jit(solution)/shard_map/ppermute | solution.py:131
  62.5 5.0 %collective-permute-start.23 = (f32[2,256,128]{2,1,0:T(8,128)S(1)}, f32[2,256,128]{2,1,0:T(8,128)S(1)}, u32[]{:S(2)}, u32[]{:S(2)}) collective-permute-start(f32[2,256,128]{2,1,0:T(8,128)S(1)} %get-tuple-element.36), channel_id=1, source_target_pairs={{0,1},{1,0},{2,3},{3,2},{4,5},{5,4},{6,7},{7,6},{8,9},{9,8},{10,11... | collective-permute-start | bytes 786440 | tf_op jit(solution)/shard_map/ppermute | solution.py:131
  63.2 16.7 %collective-permute-start.16 = (f32[256,128]{1,0:T(8,128)S(1)}, f32[256,128]{1,0:T(8,128)S(1)}, u32[]{:S(2)}, u32[]{:S(2)}) collective-permute-start(f32[256,128]{1,0:T(8,128)S(1)} %slice_bitcast_fusion.6), channel_id=1, source_target_pairs={{0,2},{1,3},{2,0},{3,1},{4,6},{5,7},{6,4},{7,5},{8,10},{9,11},{10,... | collective-permute-start | bytes 393224 | tf_op jit(solution)/shard_map/ppermute | solution.py:131
  65.2 7.2 %collective-permute-start.18 = (f32[256,128]{1,0:T(8,128)S(1)}, f32[256,128]{1,0:T(8,128)S(1)}, u32[]{:S(2)}, u32[]{:S(2)}) collective-permute-start(f32[256,128]{1,0:T(8,128)S(1)} %slice_bitcast_fusion.4), channel_id=1, source_target_pairs={{0,2},{1,3},{2,0},{3,1},{4,6},{5,7},{6,4},{7,5},{8,10},{9,11},{10,... | collective-permute-start | bytes 393224 | tf_op jit(solution)/shard_map/ppermute | solution.py:131
  65.6 9.6 %collective-permute-start.21 = (f32[256,128]{1,0:T(8,128)S(1)}, f32[256,128]{1,0:T(8,128)S(1)}, u32[]{:S(2)}, u32[]{:S(2)}) collective-permute-start(f32[256,128]{1,0:T(8,128)S(1)} %slice_bitcast_fusion.2), channel_id=1, source_target_pairs={{0,2},{1,3},{2,0},{3,1},{4,6},{5,7},{6,4},{7,5},{8,10},{9,11},{10,... | collective-permute-start | bytes 393224 | tf_op jit(solution)/shard_map/ppermute | solution.py:131
  67.5 12.3 %collective-permute-start.24 = (f32[256,128]{1,0:T(8,128)S(1)}, f32[256,128]{1,0:T(8,128)S(1)}, u32[]{:S(2)}, u32[]{:S(2)}) collective-permute-start(f32[256,128]{1,0:T(8,128)S(1)} %slice_bitcast_fusion), channel_id=1, source_target_pairs={{0,2},{1,3},{2,0},{3,1},{4,6},{5,7},{6,4},{7,5},{8,10},{9,11},{10,... | collective-permute-start | bytes 393224 | tf_op jit(solution)/shard_map/ppermute | solution.py:131
  72.4 9.6 %collective-permute-start.19 = (f32[256,128]{1,0:T(8,128)S(1)}, f32[256,128]{1,0:T(8,128)S(1)}, u32[]{:S(2)}, u32[]{:S(2)}) collective-permute-start(f32[256,128]{1,0:T(8,128)S(1)} %fusion.2), channel_id=1, source_target_pairs={{0,8},{1,9},{2,10},{3,11},{4,12},{5,13},{6,14},{7,15},{8,0},{9,1},... | collective-permute-start | bytes 393224 | tf_op jit(solution)/shard_map/ppermute | solution.py:131
  75.2 8.4 %collective-permute-start.22 = (f32[256,128]{1,0:T(8,128)S(1)}, f32[256,128]{1,0:T(8,128)S(1)}, u32[]{:S(2)}, u32[]{:S(2)}) collective-permute-start(f32[256,128]{1,0:T(8,128)S(1)} %fusion.1), channel_id=1, source_target_pairs={{0,12},{1,13},{2,14},{3,15},{4,0},{5,1},{6,2},{7,3},{8,4},{9,5},{1... | collective-permute-start | bytes 393224 | tf_op jit(solution)/shard_map/ppermute | solution.py:131
  79.8 6.9 %collective-permute-start.25 = (f32[256,128]{1,0:T(8,128)S(1)}, f32[256,128]{1,0:T(8,128)S(1)}, u32[]{:S(2)}, u32[]{:S(2)}) collective-permute-start(f32[256,128]{1,0:T(8,128)S(1)} %fusion), channel_id=1, source_target_pairs={{0,4},{1,5},{2,6},{3,7},{4,8},{5,9},{6,10},{7,11},{8,12},{9,13},{1... | collective-permute-start | bytes 393224 | tf_op jit(solution)/shard_map/ppermute | solution.py:131

commit v2 on v1

v2 whole, which is shorter than its diff:
```python
import functools

import jax
import jax.numpy as jnp
from jax import lax
from jax.experimental import pallas as pl
from jax.experimental.pallas import tpu as pltpu
from jax.sharding import PartitionSpec as P

F32, BF16 = jnp.float32, jnp.bfloat16
MIB = 1 << 20
HALF_UNROLL, FIT, OUT = 16, 16, 16


def halves(x):
    hi = x.astype(BF16)
    return hi, (x - hi.astype(F32)).astype(BF16)


def dot(a, b):
    return jnp.dot(a, b, preferred_element_type=F32)


def prepare_kernel(tiles_ref, split_ref, buf, sem):
    n_tiles = tiles_ref.shape[0]
    depth, group = buf.shape[0], buf.shape[1]
    steps = n_tiles // group

    def fetch(step, at):
        return pltpu.make_async_copy(tiles_ref.at[pl.ds(step * group, group)], buf.at[at], sem.at[at])

    for step in range(min(depth, steps)):
        fetch(step, step).start()
    for step in range(steps):
        at = step % depth
        fetch(step, at).wait()
        for i in range(group):
            hi, lo = halves(buf[at, i].reshape(-1, buf.shape[-1]))
            split_ref[step * group + i, :, : buf.shape[-1]] = hi
            split_ref[step * group + i, :, buf.shape[-1] :] = lo
        if step + depth < steps:
            fetch(step + depth, at).start()


def prepare(tiles):
    n_tiles, aux_dev, block, _ = tiles.shape
    return pl.pallas_call(
        prepare_kernel,
        out_shape=pltpu.VMEM((n_tiles, aux_dev * block, 2 * block), BF16),
        in_specs=[pl.BlockSpec(memory_space=pltpu.HBM)],
        out_specs=pl.BlockSpec(memory_space=pltpu.VMEM),
        scratch_shapes=[
            pltpu.VMEM((4, 2, aux_dev, block, block), F32),
            pltpu.SemaphoreType.DMA((4,)),
        ],
        compiler_params=pltpu.CompilerParams(vmem_limit_bytes=24 * MIB),
        cost_estimate=pl.CostEstimate(flops=6 * tiles.size, bytes_accessed=8 * tiles.size, transcendentals=0),
        name="prepare",
    )(pltpu.with_memory_space_constraint(tiles, pltpu.HBM))


class Grid:
    def __init__(self, n_aux):
        self.y, self.core = 2, 2
        self.z = n_aux // (self.y * self.core)
        self.offsets = [(k, j, c) for c in range(self.core) for k in range(self.z) for j in range(self.y)]

    def index(self, z, y, core):
        return (z * self.y + y) * self.core + core

    def other(self, me, offset):
        k, j, c = offset
        z, y, core = me // (self.y * self.core), me // self.core % self.y, me % self.core
        return self.index((z + k) % self.z, (y + j) % self.y, (core + c) % self.core)

    def shift(self, x, offset):
        return lax.ppermute(x, "aux", [(i, self.other(i, offset)) for i in range(self.z * self.y * self.core)])

    def back(self, offset):
        return (-offset[0]) % self.z, offset[1], offset[2]


def hops(grid):
    return sorted(range(1, grid.z), key=lambda k: min(k, grid.z - k))


def gather_shards(grid, x, beside):
    held = {(0, 0, 0): x}
    for k in hops(grid):
        held[k, 0, 0] = grid.shift(x, (-k, 0, 0))
    first = hops(grid)[0]
    held[first, 0, 0], beside = lax.optimization_barrier((held[first, 0, 0], beside))
    for k in [0] + hops(grid):
        held[k, 1, 0] = grid.shift(held[k, 0, 0], (0, 1, 0))
    for k, j, _ in list(held):
        held[k, j, 1] = grid.shift(held[k, j, 0], (0, 0, 1))
    return [held[o] for o in grid.offsets], beside


def scatter_sums(grid, parts):
    order = hops(grid)[::-1] + [0]
    crossed = {k: grid.shift(parts[1][k], (0, 0, 1)) for k in order}
    total = {}
    for k in order:
        pair = parts[0][k] + crossed[k]
        total[k] = pair[0] + grid.shift(pair[1], (0, 1, 0))
    out = total[0]
    for k in order[:-1]:
        out = out + grid.shift(total[k], (k, 0, 0))
    return out


def exchange_kernel(grid, per_owner, owner_ref, sub_ref, cols_ref, order_ref, split_ref, *refs):
    n_tiles, rows, pair = split_ref.shape
    block = pair // 2
    aux_dev = rows // block
    n_shards = len(grid.offsets) if grid else 1
    shards, refs = refs[:n_shards], refs[n_shards:]
    *outs, coeff, wide, fitted, weights, summed = refs
    me = lax.axis_index("aux")
    if grid:
        for ref, offset in zip(shards, grid.offsets):
            coeff[pl.ds(grid.other(me, offset) * per_owner, per_owner)] = ref[...].reshape(per_owner, block, -1)
    else:
        coeff[...] = shards[0][...].reshape(coeff.shape)

    def position(t):
        return owner_ref[t] * per_owner + sub_ref[t]

    def half_step(t, _):
        c_hi, c_lo = halves(coeff[cols_ref[t]])
        top = jnp.concatenate([c_hi, c_lo], axis=1)
        both = dot(split_ref[t], jnp.concatenate([top, top], axis=0))
        hi, lo = halves(both[:, :block] + both[:, block:])
        for p in range(aux_dev):
            wide[t, :, p * pair : p * pair + block] = hi[p * block : (p + 1) * block]
            wide[t, :, p * pair + block : (p + 1) * pair] = lo[p * block : (p + 1) * block]
        return 0

    lax.fori_loop(0, n_tiles, half_step, 0, unroll=HALF_UNROLL)
    fitted[...] = jnp.zeros_like(fitted)

    def fit_step(step, _):
        left, right = [], []
        for i in range(FIT):
            t = step * FIT + i
            c_hi, c_lo = halves(coeff[order_ref[position(t)]].T)
            left.append(jnp.concatenate([jnp.concatenate([c_hi, c_hi], axis=1), jnp.concatenate([c_lo, c_lo], axis=1)], axis=0))
            w = wide[t]
            right.append(jnp.concatenate([w[:, p * pair : p * pair + block] for p in range(aux_dev)], axis=1))
            right.append(jnp.concatenate([w[:, p * pair + block : (p + 1) * pair] for p in range(aux_dev)], axis=1))
        fitted[...] += dot(jnp.concatenate(left, axis=1), jnp.concatenate(right, axis=0))
        return 0

    lax.fori_loop(0, n_tiles // FIT, fit_step, 0)
    for p in range(aux_dev):
        at = pl.ds(p * block, block)
        f_hi, f_lo = halves((fitted[:block, at] + fitted[block:, at]).T)
        both = jnp.concatenate([f_hi, f_lo], axis=1)
        weights[p * pair : p * pair + block, :] = both
        weights[p * pair + block : (p + 1) * pair, :] = both
    summed[...] = jnp.zeros_like(summed)

    def out_step(step, _):
        both = dot(wide[pl.ds(step * OUT, OUT)].reshape(OUT * block, -1), weights[...])
        value = both[:, :block] + both[:, block:]
        for i in range(OUT):
            summed[position(step * OUT + i)] += value[i * block : (i + 1) * block]
        return 0

    lax.fori_loop(0, n_tiles // OUT, out_step, 0)
    if grid:
        for c in range(grid.core):
            for k in range(grid.z):
                for j in range(grid.y):
                    at = grid.other(me, (k, j, c)) * per_owner
                    outs[c * grid.z + k][j] = summed[pl.ds(at, per_owner)].reshape(outs[0].shape[1:])
    else:
        outs[0][...] = summed[...].reshape(outs[0].shape)


def exchange(grid, tile_owner, tile_sub, tile_cols, row_order, split, shards):
    n_tiles, rows, pair = split.shape
    block, width = pair // 2, shards[0].shape[1]
    aux_dev = rows // block
    n_blocks = row_order.shape[0]
    per_owner = n_blocks // lax.axis_size("aux")
    smem = pl.BlockSpec(memory_space=pltpu.SMEM)
    vmem = pl.BlockSpec(memory_space=pltpu.VMEM)
    if grid:
        out_shape = [pltpu.VMEM((grid.y, per_owner * block, width), F32)] * (grid.core * grid.z)
    else:
        out_shape = [jax.ShapeDtypeStruct((n_blocks * block, width), F32)]
    return pl.pallas_call(
        functools.partial(exchange_kernel, grid, per_owner),
        out_shape=out_shape,
        in_specs=[smem] * 4 + [vmem] * (1 + len(shards)),
        out_specs=[vmem] * len(out_shape),
        scratch_shapes=[
            pltpu.VMEM((n_blocks, block, width), F32),
            pltpu.VMEM((n_tiles, block, aux_dev * pair), BF16),
            pltpu.VMEM((2 * width, aux_dev * block), F32),
            pltpu.VMEM((aux_dev * pair, 2 * width), BF16),
            pltpu.VMEM((n_blocks, block, width), F32),
        ],
        compiler_params=pltpu.CompilerParams(vmem_limit_bytes=(24 if grid else 44) * MIB),
        name="exchange",
    )(tile_owner.reshape(-1), tile_sub, tile_cols, row_order, split, *shards)


def local(tiles, tile_owner, tile_sub, tile_cols, row_order, orbitals):
    n_aux = lax.axis_size("aux")
    grid = Grid(n_aux) if n_aux % 4 == 0 and n_aux <= 16 else None
    split = prepare(tiles)
    if grid:
        shards, split = gather_shards(grid, orbitals, split)
    else:
        shards = [lax.all_gather(orbitals, "aux", axis=0, tiled=True)]
    split = pltpu.with_memory_space_constraint(split, pltpu.VMEM)
    outs = exchange(grid, tile_owner, tile_sub, tile_cols, row_order, split, shards)
    if not grid:
        return lax.psum_scatter(outs[0], "aux", scatter_dimension=0, tiled=True)
    return scatter_sums(grid, [outs[: grid.z], outs[grid.z :]])


def solution(mesh):
    in_specs = (
        P(("grp", "aux"), None, None, None),
        P(("grp", "aux"), None),
        P(("grp", "aux")),
        P(("grp", "aux")),
        P("grp"),
        P(("grp", "aux"), None),
    )
    out_specs = P(("grp", "aux"), None)
    return jax.shard_map(local, mesh=mesh, in_specs=in_specs, out_specs=out_specs, check_vma=False)
```

time: 87.4 us -> 60 us (0.69)
  Pallas kernels: 26.9 us -> 14 us
  local copies, waits for them, and re-layouts: 6.84 us -> 0.06 us
  starting transfers between devices: 26.8 us -> 22.6 us
  waiting for transfers between devices: 25.6 us -> 22.1 us
    pallas_call x1, Pallas kernels: 21.8 us -> 8.83 us  [exchange(): pl.pallas_call(functools.partial(exchange_kernel, grid, per_owner), out_s...]
    unnamed x51 -> x10, local copies, waits for them, and re-layouts: 6.81 us -> 0.02 us
    ppermute x26, starting transfers between devices: 26.8 us -> 22.6 us  [shift(): lax.ppermute(x, 'aux', [(i, self.other(i, offset)) for i in range(self.z...]
    ppermute x26, waiting for transfers between devices: 25.6 us -> 22.1 us  [shift(): lax.ppermute(x, 'aux', [(i, self.other(i, offset)) for i in range(self.z...]
  transfers between devices with their start and end apart: 26 -> 26, of which waited for: 11 -> 11; matrix products, arithmetic and copies ran while one was open for 1% -> 0% of each run, Pallas kernels for 6% -> 9%
where the time goes in v2:
time: 60 us; the launch traced here: 59.8 us
  starting transfers between devices  22.6 us (38%)
  waiting for transfers between devices  22.1 us (37%)
  Pallas kernels  14 us (23%)
  other arithmetic  0.91 us (2%)
    ppermute x26, starting transfers between devices, shift(): lax.ppermute(x, 'aux', [(i, self.other(i, offset)) for i in range(self.z...  22.6 us
    ppermute x26, waiting for transfers between devices, shift(): lax.ppermute(x, 'aux', [(i, self.other(i, offset)) for i in range(self.z...  22.1 us
    pallas_call x1, Pallas kernels, exchange(): pl.pallas_call(functools.partial(exchange_kernel, grid, per_owner), out_s...  8.83 us
    pallas_call x1, Pallas kernels, prepare(): pl.pallas_call(prepare_kernel, out_shape=pltpu.VMEM((n_tiles, aux_dev * b...  5.2 us
  transfers between devices with their start and end apart: 26, of which 11 were waited for; matrix products, arithmetic and copies ran while one was open for 0% of the time, Pallas kernels for 9%

profile of v2, /device:TPU:0, one launch (start us, length us, event | category | flops | bytes accessed | tf_op | source)
XLA Modules:
  0.0 59.8 jit_solution(3571042282806384649)
XLA Ops:
  0.0 0.0 copy-start
  0.0 0.0 copy-start.4
  0.0 0.0 copy-start.3
  0.0 0.0 copy-start.2
  0.0 5.1 %collective-permute-start = (f32[256,128]{1,0:T(8,128)}, f32[256,128]{1,0:T(8,128)S(1)}, u32[]{:S(2)}, u32[]{:S(2)}) collective-permute-start(f32[256,128]{1,0:T(8,128)} %refs_0_.1), channel_id=1, source_target_pairs={{0,12},{1,13},{2,14},{3,15},{4,0},{5,1},{6,2},{7,3},{8,4},{9,5},{1... | collective-permute-start | bytes 393224 | tf_op jit(solution)/shard_map/ppermute | solution.py:77
  5.1 0.0 collective-permute-start.5
  5.1 1.0 %collective-permute-start.3 = (f32[256,128]{1,0:T(8,128)}, f32[256,128]{1,0:T(8,128)S(1)}, u32[]{:S(2)}, u32[]{:S(2)}) collective-permute-start(f32[256,128]{1,0:T(8,128)} %refs_0_.1), channel_id=1, source_target_pairs={{0,8},{1,9},{2,10},{3,11},{4,12},{5,13},{6,14},{7,15},{8,0},{9,1},... | collective-permute-start | bytes 393224 | tf_op jit(solution)/shard_map/ppermute | solution.py:77
  6.1 1.5 %collective-permute-start.1 = (f32[256,128]{1,0:T(8,128)}, f32[256,128]{1,0:T(8,128)S(1)}, u32[]{:S(2)}, u32[]{:S(2)}) collective-permute-start(f32[256,128]{1,0:T(8,128)} %refs_0_.1), channel_id=1, source_target_pairs={{0,2},{1,3},{2,0},{3,1},{4,6},{5,7},{6,4},{7,5},{8,10},{9,11},{10,... | collective-permute-start | bytes 393224 | tf_op jit(solution)/shard_map/ppermute | solution.py:77
  7.7 0.0 collective-permute-start.7
  7.7 5.2 %prepare.1.split_ref = bf16[32,512,256]{2,1,0:T(8,128)(2,1)S(1)} custom-call(f32[32,4,128,128]{3,2,1,0:T(8,128)} %tiles_ref.1), custom_call_target="tpu_custom_call" | custom-call | flops 12582912 | bytes 16777216 | tf_op jit(solution)/shard_map/prepare/pallas_call | solution.py:47
  12.9 0.0 collective-permute-done.refs_2_
  12.9 0.7 %collective-permute-done.5.refs_6_ = f32[256,128]{1,0:T(8,128)S(1)} collective-permute-done((f32[256,128]{1,0:T(8,128)}, f32[256,128]{1,0:T(8,128)S(1)}, u32[]{:S(2)}, u32[]{:S(2)}) %collective-permute-start.5) | collective-permute-done | bytes 131104 | tf_op jit(solution)/shard_map/ppermute | solution.py:77
  13.6 0.0 collective-permute-start.13
  13.6 1.5 %collective-permute-start.6 = (f32[256,128]{1,0:T(8,128)S(1)}, f32[256,128]{1,0:T(8,128)S(1)}, u32[]{:S(2)}, u32[]{:S(2)}) collective-permute-start(f32[256,128]{1,0:T(8,128)S(1)} %collective-permute-done.5.refs_6_), channel_id=1, source_target_pairs={{0,2},{1,3},{2,0},{3,1},{4,6},{5,7},{6,4},{7,5},{8,10},{9,11},{10,... | collective-permute-start | bytes 393224 | tf_op jit(solution)/shard_map/ppermute | solution.py:77
  15.1 1.7 %collective-permute-done.3.refs_4_ = f32[256,128]{1,0:T(8,128)S(1)} collective-permute-done((f32[256,128]{1,0:T(8,128)}, f32[256,128]{1,0:T(8,128)S(1)}, u32[]{:S(2)}, u32[]{:S(2)}) %collective-permute-start.3) | collective-permute-done | bytes 131104 | tf_op jit(solution)/shard_map/ppermute | solution.py:77
  16.8 0.0 collective-permute-start.11
  16.8 0.0 collective-permute-done.1.refs_1_
  16.8 1.5 %collective-permute-start.4 = (f32[256,128]{1,0:T(8,128)S(1)}, f32[256,128]{1,0:T(8,128)S(1)}, u32[]{:S(2)}, u32[]{:S(2)}) collective-permute-start(f32[256,128]{1,0:T(8,128)S(1)} %collective-permute-done.3.refs_4_), channel_id=1, source_target_pairs={{0,2},{1,3},{2,0},{3,1},{4,6},{5,7},{6,4},{7,5},{8,10},{9,11},{10,... | collective-permute-start | bytes 393224 | tf_op jit(solution)/shard_map/ppermute | solution.py:77
  18.3 0.0 collective-permute-done.7.refs_8_
  18.4 0.5 collective-permute-start.2
  18.9 0.0 collective-permute-done.13.refs_14_
  18.9 0.0 collective-permute-start.9
  18.9 0.7 %collective-permute-done.6.refs_7_ = f32[256,128]{1,0:T(8,128)S(1)} collective-permute-done((f32[256,128]{1,0:T(8,128)S(1)}, f32[256,128]{1,0:T(8,128)S(1)}, u32[]{:S(2)}, u32[]{:S(2)}) %collective-permute-start.6) | collective-permute-done | bytes 131104 | tf_op jit(solution)/shard_map/ppermute | solution.py:77
  19.5 0.0 collective-permute-start.8
  19.5 0.0 collective-permute-done.11.refs_12_
  19.5 0.5 collective-permute-start.14
  20.0 3.1 %collective-permute-done.4.refs_5_ = f32[256,128]{1,0:T(8,128)S(1)} collective-permute-done((f32[256,128]{1,0:T(8,128)S(1)}, f32[256,128]{1,0:T(8,128)S(1)}, u32[]{:S(2)}, u32[]{:S(2)}) %collective-permute-start.4) | collective-permute-done | bytes 131104 | tf_op jit(solution)/shard_map/ppermute | solution.py:77
  23.1 0.0 collective-permute-start.12
  23.1 2.4 %collective-permute-done.2.refs_3_ = f32[256,128]{1,0:T(8,128)S(1)} collective-permute-done((f32[256,128]{1,0:T(8,128)S(1)}, f32[256,128]{1,0:T(8,128)S(1)}, u32[]{:S(2)}, u32[]{:S(2)}) %collective-permute-start.2) | collective-permute-done | bytes 131104 | tf_op jit(solution)/shard_map/ppermute | solution.py:77
  25.5 0.0 collective-permute-start.10
  25.5 0.0 collective-permute-done.8.refs_9_
  25.6 0.0 collective-permute-done.9.refs_10_
  25.6 0.0 collective-permute-done.14.refs_15_
  25.6 0.0 collective-permute-done.12.refs_13_
  25.6 1.3 %collective-permute-done.10.refs_11_ = f32[256,128]{1,0:T(8,128)S(1)} collective-permute-done((f32[256,128]{1,0:T(8,128)S(1)}, f32[256,128]{1,0:T(8,128)S(1)}, u32[]{:S(2)}, u32[]{:S(2)}) %collective-permute-start.10) | collective-permute-done | bytes 131104 | tf_op jit(solution)/shard_map/ppermute | solution.py:77
  26.9 0.0 copy-done
  26.9 0.0 copy-done.4
  26.9 0.0 copy-done.3
  26.9 0.0 copy-done.2
  26.9 0.0 copy-done.1
  26.9 8.8 %exchange.1 = (f32[2,256,128]{2,1,0:T(8,128)S(1)}, f32[2,256,128]{2,1,0:T(8,128)S(1)}, f32[2,256,128]{2,1,0:T(8,128)S(1)}, f32[2,256,128]{2,1,0:T(8,128)S(1)}, f...) custom-call(s32[32]{0:T(128)S(1)} %bitcast.31, ...), custom_call_target="tpu_custom_call" | custom-call | tf_op jit(solution)/shard_map/exchange/pallas_call | solution.py:194
  35.8 0.2 collective-permute-start.15
  36.0 0.4 collective-permute-start.17
  36.3 0.1 collective-permute-start.20
  36.5 0.4 collective-permute-start.23
  36.8 0.5 collective-permute-done.15
  37.4 1.6 %collective-permute-start.16 = (f32[256,128]{1,0:T(8,128)S(1)}, f32[256,128]{1,0:T(8,128)S(1)}, u32[]{:S(2)}, u32[]{:S(2)}) collective-permute-start(f32[256,128]{1,0:T(8,128)S(1)} %slice_bitcast_fusion.6), channel_id=1, source_target_pairs={{0,2},{1,3},{2,0},{3,1},{4,6},{5,7},{6,4},{7,5},{8,10},{9,11},{10,... | collective-permute-start | bytes 393224 | tf_op jit(solution)/shard_map/ppermute | solution.py:77
  39.0 0.0 collective-permute-done.17
  39.1 0.6 collective-permute-start.18
  39.6 0.0 collective-permute-done.20
  39.7 1.6 %collective-permute-start.21 = (f32[256,128]{1,0:T(8,128)S(1)}, f32[256,128]{1,0:T(8,128)S(1)}, u32[]{:S(2)}, u32[]{:S(2)}) collective-permute-start(f32[256,128]{1,0:T(8,128)S(1)} %slice_bitcast_fusion.2), channel_id=1, source_target_pairs={{0,2},{1,3},{2,0},{3,1},{4,6},{5,7},{6,4},{7,5},{8,10},{9,11},{10,... | collective-permute-start | bytes 393224 | tf_op jit(solution)/shard_map/ppermute | solution.py:77
  41.3 0.0 collective-permute-done.23
  41.3 0.6 collective-permute-start.24
  41.9 4.7 %collective-permute-done.18 = f32[256,128]{1,0:T(8,128)S(1)} collective-permute-done((f32[256,128]{1,0:T(8,128)S(1)}, f32[256,128]{1,0:T(8,128)S(1)}, u32[]{:S(2)}, u32[]{:S(2)}) %collective-permute-start.18) | collective-permute-done | bytes 131104 | tf_op jit(solution)/shard_map/ppermute | solution.py:77
  46.7 1.0 %collective-permute-start.19 = (f32[256,128]{1,0:T(8,128)S(1)}, f32[256,128]{1,0:T(8,128)S(1)}, u32[]{:S(2)}, u32[]{:S(2)}) collective-permute-start(f32[256,128]{1,0:T(8,128)S(1)} %fusion.2), channel_id=1, source_target_pairs={{0,8},{1,9},{2,10},{3,11},{4,12},{5,13},{6,14},{7,15},{8,0},{9,1},... | collective-permute-start | bytes 393224 | tf_op jit(solution)/shard_map/ppermute | solution.py:77
  47.7 1.8 %collective-permute-done.21 = f32[256,128]{1,0:T(8,128)S(1)} collective-permute-done((f32[256,128]{1,0:T(8,128)S(1)}, f32[256,128]{1,0:T(8,128)S(1)}, u32[]{:S(2)}, u32[]{:S(2)}) %collective-permute-start.21) | collective-permute-done | bytes 131104 | tf_op jit(solution)/shard_map/ppermute | solution.py:77
  49.5 2.3 %collective-permute-start.22 = (f32[256,128]{1,0:T(8,128)S(1)}, f32[256,128]{1,0:T(8,128)S(1)}, u32[]{:S(2)}, u32[]{:S(2)}) collective-permute-start(f32[256,128]{1,0:T(8,128)S(1)} %fusion.1), channel_id=1, source_target_pairs={{0,12},{1,13},{2,14},{3,15},{4,0},{5,1},{6,2},{7,3},{8,4},{9,5},{1... | collective-permute-start | bytes 393224 | tf_op jit(solution)/shard_map/ppermute | solution.py:77
  51.8 0.0 collective-permute-done.24
  51.8 2.1 %collective-permute-start.25 = (f32[256,128]{1,0:T(8,128)S(1)}, f32[256,128]{1,0:T(8,128)S(1)}, u32[]{:S(2)}, u32[]{:S(2)}) collective-permute-start(f32[256,128]{1,0:T(8,128)S(1)} %fusion), channel_id=1, source_target_pairs={{0,4},{1,5},{2,6},{3,7},{4,8},{5,9},{6,10},{7,11},{8,12},{9,13},{1... | collective-permute-start | bytes 393224 | tf_op jit(solution)/shard_map/ppermute | solution.py:77
  53.9 0.0 collective-permute-done.16
  53.9 2.1 %collective-permute-done.19 = f32[256,128]{1,0:T(8,128)S(1)} collective-permute-done((f32[256,128]{1,0:T(8,128)S(1)}, f32[256,128]{1,0:T(8,128)S(1)}, u32[]{:S(2)}, u32[]{:S(2)}) %collective-permute-start.19) | collective-permute-done | bytes 131104 | tf_op jit(solution)/shard_map/ppermute | solution.py:77
  56.0 0.0 collective-permute-done.22
  56.0 3.1 %collective-permute-done.25 = f32[256,128]{1,0:T(8,128)S(1)} collective-permute-done((f32[256,128]{1,0:T(8,128)S(1)}, f32[256,128]{1,0:T(8,128)S(1)}, u32[]{:S(2)}, u32[]{:S(2)}) %collective-permute-start.25) | collective-permute-done | bytes 131104 | tf_op jit(solution)/shard_map/ppermute | solution.py:77
  59.1 0.7 %fusion.6 = f32[256,128]{1,0:T(8,128)} fusion(f32[256,128]{1,0:T(8,128)S(1)} %collective-permute-done.25, f32[256,128]{1,0:T(8,128)S(1)} %collective-permute-done.22, f32[256,128]{1,0:T(8,128)S(1)} %collective-permute-done.19, f32[256,128]{1,0:T(8,128)S(1)} %collective-permute-done.16, f32[2,256,128]{2,1,0:T(8,128)S(1)} %add.33), kind=kLoop, calls=%fused_computation.14 | loop fusion | flops 131072 | bytes 786432 | tf_op jit(solution)/shard_map/add | solution.py:109
  (12 shorter events, 0.3 us)
Async XLA Ops:
  0.0 26.9 %copy-start = (f32[256,128]{1,0:T(8,128)S(1)}, f32[256,128]{1,0:T(8,128)}, u32[]{:S(2)}) copy-start(f32[256,128]{1,0:T(8,128)} %refs_0_.1) | copy-start | bytes 393220
  0.0 26.9 %copy-start.4 = (s32[32]{0:T(128)S(1)}, s32[32]{0:T(128)}, u32[]{:S(2)}) copy-start(s32[32]{0:T(128)} %order_ref.1) | copy-start | bytes 388
  0.0 26.9 %copy-start.3 = (s32[32]{0:T(128)S(1)}, s32[32]{0:T(128)}, u32[]{:S(2)}) copy-start(s32[32]{0:T(128)} %cols_ref.1) | copy-start | bytes 388
  0.0 26.9 %copy-start.2 = (s32[32]{0:T(128)S(1)}, s32[32]{0:T(128)}, u32[]{:S(2)}) copy-start(s32[32]{0:T(128)} %sub_ref.1) | copy-start | bytes 388
  0.0 26.9 %copy-start.1 = (s32[32,1]{0,1:T(1,128)S(1)}, s32[32,1]{0,1:T(1,128)}, u32[]{:S(2)}) copy-start(s32[32,1]{0,1:T(1,128)} %param.7) | copy-start | bytes 388
  0.0 12.9 %collective-permute-start = (f32[256,128]{1,0:T(8,128)}, f32[256,128]{1,0:T(8,128)S(1)}, u32[]{:S(2)}, u32[]{:S(2)}) collective-permute-start(f32[256,128]{1,0:T(8,128)} %refs_0_.1), channel_id=1, source_target_pairs={{0,12},{1,13},{2,14},{3,15},{4,0},{5,1},{6,2},{7,3},{8,4},{9,5},{1... | collective-permute-start | bytes 393224 | tf_op jit(solution)/shard_map/ppermute | solution.py:77
  5.1 8.5 %collective-permute-start.5 = (f32[256,128]{1,0:T(8,128)}, f32[256,128]{1,0:T(8,128)S(1)}, u32[]{:S(2)}, u32[]{:S(2)}) collective-permute-start(f32[256,128]{1,0:T(8,128)} %refs_0_.1), channel_id=1, source_target_pairs={{0,4},{1,5},{2,6},{3,7},{4,8},{5,9},{6,10},{7,11},{8,12},{9,13},{1... | collective-permute-start | bytes 393224 | tf_op jit(solution)/shard_map/ppermute | solution.py:77
  5.1 11.7 %collective-permute-start.3 = (f32[256,128]{1,0:T(8,128)}, f32[256,128]{1,0:T(8,128)S(1)}, u32[]{:S(2)}, u32[]{:S(2)}) collective-permute-start(f32[256,128]{1,0:T(8,128)} %refs_0_.1), channel_id=1, source_target_pairs={{0,8},{1,9},{2,10},{3,11},{4,12},{5,13},{6,14},{7,15},{8,0},{9,1},... | collective-permute-start | bytes 393224 | tf_op jit(solution)/shard_map/ppermute | solution.py:77
  6.1 10.7 %collective-permute-start.1 = (f32[256,128]{1,0:T(8,128)}, f32[256,128]{1,0:T(8,128)S(1)}, u32[]{:S(2)}, u32[]{:S(2)}) collective-permute-start(f32[256,128]{1,0:T(8,128)} %refs_0_.1), channel_id=1, source_target_pairs={{0,2},{1,3},{2,0},{3,1},{4,6},{5,7},{6,4},{7,5},{8,10},{9,11},{10,... | collective-permute-start | bytes 393224 | tf_op jit(solution)/shard_map/ppermute | solution.py:77
  7.7 10.7 %collective-permute-start.7 = (f32[256,128]{1,0:T(8,128)}, f32[256,128]{1,0:T(8,128)S(1)}, u32[]{:S(2)}, u32[]{:S(2)}) collective-permute-start(f32[256,128]{1,0:T(8,128)} %refs_0_.1), channel_id=1, source_target_pairs={{0,1},{1,0},{2,3},{3,2},{4,5},{5,4},{6,7},{7,6},{8,9},{9,8},{10,11... | collective-permute-start | bytes 393224 | tf_op jit(solution)/shard_map/ppermute | solution.py:77
  13.6 5.3 %collective-permute-start.13 = (f32[256,128]{1,0:T(8,128)S(1)}, f32[256,128]{1,0:T(8,128)S(1)}, u32[]{:S(2)}, u32[]{:S(2)}) collective-permute-start(f32[256,128]{1,0:T(8,128)S(1)} %collective-permute-done.5.refs_6_), channel_id=1, source_target_pairs={{0,1},{1,0},{2,3},{3,2},{4,5},{5,4},{6,7},{7,6},{8,9},{9,8},{10,11... | collective-permute-start | bytes 393224 | tf_op jit(solution)/shard_map/ppermute | solution.py:77
  13.6 5.9 %collective-permute-start.6 = (f32[256,128]{1,0:T(8,128)S(1)}, f32[256,128]{1,0:T(8,128)S(1)}, u32[]{:S(2)}, u32[]{:S(2)}) collective-permute-start(f32[256,128]{1,0:T(8,128)S(1)} %collective-permute-done.5.refs_6_), channel_id=1, source_target_pairs={{0,2},{1,3},{2,0},{3,1},{4,6},{5,7},{6,4},{7,5},{8,10},{9,11},{10,... | collective-permute-start | bytes 393224 | tf_op jit(solution)/shard_map/ppermute | solution.py:77
  16.8 2.7 %collective-permute-start.11 = (f32[256,128]{1,0:T(8,128)S(1)}, f32[256,128]{1,0:T(8,128)S(1)}, u32[]{:S(2)}, u32[]{:S(2)}) collective-permute-start(f32[256,128]{1,0:T(8,128)S(1)} %collective-permute-done.3.refs_4_), channel_id=1, source_target_pairs={{0,1},{1,0},{2,3},{3,2},{4,5},{5,4},{6,7},{7,6},{8,9},{9,8},{10,11... | collective-permute-start | bytes 393224 | tf_op jit(solution)/shard_map/ppermute | solution.py:77
  16.8 6.3 %collective-permute-start.4 = (f32[256,128]{1,0:T(8,128)S(1)}, f32[256,128]{1,0:T(8,128)S(1)}, u32[]{:S(2)}, u32[]{:S(2)}) collective-permute-start(f32[256,128]{1,0:T(8,128)S(1)} %collective-permute-done.3.refs_4_), channel_id=1, source_target_pairs={{0,2},{1,3},{2,0},{3,1},{4,6},{5,7},{6,4},{7,5},{8,10},{9,11},{10,... | collective-permute-start | bytes 393224 | tf_op jit(solution)/shard_map/ppermute | solution.py:77
  18.4 7.2 %collective-permute-start.2 = (f32[256,128]{1,0:T(8,128)S(1)}, f32[256,128]{1,0:T(8,128)S(1)}, u32[]{:S(2)}, u32[]{:S(2)}) collective-permute-start(f32[256,128]{1,0:T(8,128)S(1)} %collective-permute-done.refs_2_), channel_id=1, source_target_pairs={{0,2},{1,3},{2,0},{3,1},{4,6},{5,7},{6,4},{7,5},{8,10},{9,11},{10,... | collective-permute-start | bytes 393224 | tf_op jit(solution)/shard_map/ppermute | solution.py:77
  18.9 6.7 %collective-permute-start.9 = (f32[256,128]{1,0:T(8,128)S(1)}, f32[256,128]{1,0:T(8,128)S(1)}, u32[]{:S(2)}, u32[]{:S(2)}) collective-permute-start(f32[256,128]{1,0:T(8,128)S(1)} %collective-permute-done.refs_2_), channel_id=1, source_target_pairs={{0,1},{1,0},{2,3},{3,2},{4,5},{5,4},{6,7},{7,6},{8,9},{9,8},{10,11... | collective-permute-start | bytes 393224 | tf_op jit(solution)/shard_map/ppermute | solution.py:77
  19.5 6.0 %collective-permute-start.8 = (f32[256,128]{1,0:T(8,128)S(1)}, f32[256,128]{1,0:T(8,128)S(1)}, u32[]{:S(2)}, u32[]{:S(2)}) collective-permute-start(f32[256,128]{1,0:T(8,128)S(1)} %collective-permute-done.1.refs_1_), channel_id=1, source_target_pairs={{0,1},{1,0},{2,3},{3,2},{4,5},{5,4},{6,7},{7,6},{8,9},{9,8},{10,11... | collective-permute-start | bytes 393224 | tf_op jit(solution)/shard_map/ppermute | solution.py:77
  19.5 6.0 %collective-permute-start.14 = (f32[256,128]{1,0:T(8,128)S(1)}, f32[256,128]{1,0:T(8,128)S(1)}, u32[]{:S(2)}, u32[]{:S(2)}) collective-permute-start(f32[256,128]{1,0:T(8,128)S(1)} %collective-permute-done.6.refs_7_), channel_id=1, source_target_pairs={{0,1},{1,0},{2,3},{3,2},{4,5},{5,4},{6,7},{7,6},{8,9},{9,8},{10,11... | collective-permute-start | bytes 393224 | tf_op jit(solution)/shard_map/ppermute | solution.py:77
  23.1 2.5 %collective-permute-start.12 = (f32[256,128]{1,0:T(8,128)S(1)}, f32[256,128]{1,0:T(8,128)S(1)}, u32[]{:S(2)}, u32[]{:S(2)}) collective-permute-start(f32[256,128]{1,0:T(8,128)S(1)} %collective-permute-done.4.refs_5_), channel_id=1, source_target_pairs={{0,1},{1,0},{2,3},{3,2},{4,5},{5,4},{6,7},{7,6},{8,9},{9,8},{10,11... | collective-permute-start | bytes 393224 | tf_op jit(solution)/shard_map/ppermute | solution.py:77
  25.5 1.3 %collective-permute-start.10 = (f32[256,128]{1,0:T(8,128)S(1)}, f32[256,128]{1,0:T(8,128)S(1)}, u32[]{:S(2)}, u32[]{:S(2)}) collective-permute-start(f32[256,128]{1,0:T(8,128)S(1)} %collective-permute-done.2.refs_3_), channel_id=1, source_target_pairs={{0,1},{1,0},{2,3},{3,2},{4,5},{5,4},{6,7},{7,6},{8,9},{9,8},{10,11... | collective-permute-start | bytes 393224 | tf_op jit(solution)/shard_map/ppermute | solution.py:77
  35.8 1.6 %collective-permute-start.15 = (f32[2,256,128]{2,1,0:T(8,128)S(1)}, f32[2,256,128]{2,1,0:T(8,128)S(1)}, u32[]{:S(2)}, u32[]{:S(2)}) collective-permute-start(f32[2,256,128]{2,1,0:T(8,128)S(1)} %get-tuple-element.18), channel_id=1, source_target_pairs={{0,1},{1,0},{2,3},{3,2},{4,5},{5,4},{6,7},{7,6},{8,9},{9,8},{10,11... | collective-permute-start | bytes 786440 | tf_op jit(solution)/shard_map/ppermute | solution.py:77
  36.0 3.0 %collective-permute-start.17 = (f32[2,256,128]{2,1,0:T(8,128)S(1)}, f32[2,256,128]{2,1,0:T(8,128)S(1)}, u32[]{:S(2)}, u32[]{:S(2)}) collective-permute-start(f32[2,256,128]{2,1,0:T(8,128)S(1)} %get-tuple-element.20), channel_id=1, source_target_pairs={{0,1},{1,0},{2,3},{3,2},{4,5},{5,4},{6,7},{7,6},{8,9},{9,8},{10,11... | collective-permute-start | bytes 786440 | tf_op jit(solution)/shard_map/ppermute | solution.py:77
  36.3 3.3 %collective-permute-start.20 = (f32[2,256,128]{2,1,0:T(8,128)S(1)}, f32[2,256,128]{2,1,0:T(8,128)S(1)}, u32[]{:S(2)}, u32[]{:S(2)}) collective-permute-start(f32[2,256,128]{2,1,0:T(8,128)S(1)} %get-tuple-element.22), channel_id=1, source_target_pairs={{0,1},{1,0},{2,3},{3,2},{4,5},{5,4},{6,7},{7,6},{8,9},{9,8},{10,11... | collective-permute-start | bytes 786440 | tf_op jit(solution)/shard_map/ppermute | solution.py:77
  36.5 4.8 %collective-permute-start.23 = (f32[2,256,128]{2,1,0:T(8,128)S(1)}, f32[2,256,128]{2,1,0:T(8,128)S(1)}, u32[]{:S(2)}, u32[]{:S(2)}) collective-permute-start(f32[2,256,128]{2,1,0:T(8,128)S(1)} %get-tuple-element.24), channel_id=1, source_target_pairs={{0,1},{1,0},{2,3},{3,2},{4,5},{5,4},{6,7},{7,6},{8,9},{9,8},{10,11... | collective-permute-start | bytes 786440 | tf_op jit(solution)/shard_map/ppermute | solution.py:77
  37.4 16.5 %collective-permute-start.16 = (f32[256,128]{1,0:T(8,128)S(1)}, f32[256,128]{1,0:T(8,128)S(1)}, u32[]{:S(2)}, u32[]{:S(2)}) collective-permute-start(f32[256,128]{1,0:T(8,128)S(1)} %slice_bitcast_fusion.6), channel_id=1, source_target_pairs={{0,2},{1,3},{2,0},{3,1},{4,6},{5,7},{6,4},{7,5},{8,10},{9,11},{10,... | collective-permute-start | bytes 393224 | tf_op jit(solution)/shard_map/ppermute | solution.py:77
  39.1 7.6 %collective-permute-start.18 = (f32[256,128]{1,0:T(8,128)S(1)}, f32[256,128]{1,0:T(8,128)S(1)}, u32[]{:S(2)}, u32[]{:S(2)}) collective-permute-start(f32[256,128]{1,0:T(8,128)S(1)} %slice_bitcast_fusion.4), channel_id=1, source_target_pairs={{0,2},{1,3},{2,0},{3,1},{4,6},{5,7},{6,4},{7,5},{8,10},{9,11},{10,... | collective-permute-start | bytes 393224 | tf_op jit(solution)/shard_map/ppermute | solution.py:77
  39.7 9.7 %collective-permute-start.21 = (f32[256,128]{1,0:T(8,128)S(1)}, f32[256,128]{1,0:T(8,128)S(1)}, u32[]{:S(2)}, u32[]{:S(2)}) collective-permute-start(f32[256,128]{1,0:T(8,128)S(1)} %slice_bitcast_fusion.2), channel_id=1, source_target_pairs={{0,2},{1,3},{2,0},{3,1},{4,6},{5,7},{6,4},{7,5},{8,10},{9,11},{10,... | collective-permute-start | bytes 393224 | tf_op jit(solution)/shard_map/ppermute | solution.py:77
  41.3 10.4 %collective-permute-start.24 = (f32[256,128]{1,0:T(8,128)S(1)}, f32[256,128]{1,0:T(8,128)S(1)}, u32[]{:S(2)}, u32[]{:S(2)}) collective-permute-start(f32[256,128]{1,0:T(8,128)S(1)} %slice_bitcast_fusion), channel_id=1, source_target_pairs={{0,2},{1,3},{2,0},{3,1},{4,6},{5,7},{6,4},{7,5},{8,10},{9,11},{10,... | collective-permute-start | bytes 393224 | tf_op jit(solution)/shard_map/ppermute | solution.py:77
  46.7 9.3 %collective-permute-start.19 = (f32[256,128]{1,0:T(8,128)S(1)}, f32[256,128]{1,0:T(8,128)S(1)}, u32[]{:S(2)}, u32[]{:S(2)}) collective-permute-start(f32[256,128]{1,0:T(8,128)S(1)} %fusion.2), channel_id=1, source_target_pairs={{0,8},{1,9},{2,10},{3,11},{4,12},{5,13},{6,14},{7,15},{8,0},{9,1},... | collective-permute-start | bytes 393224 | tf_op jit(solution)/shard_map/ppermute | solution.py:77
  49.5 6.5 %collective-permute-start.22 = (f32[256,128]{1,0:T(8,128)S(1)}, f32[256,128]{1,0:T(8,128)S(1)}, u32[]{:S(2)}, u32[]{:S(2)}) collective-permute-start(f32[256,128]{1,0:T(8,128)S(1)} %fusion.1), channel_id=1, source_target_pairs={{0,12},{1,13},{2,14},{3,15},{4,0},{5,1},{6,2},{7,3},{8,4},{9,5},{1... | collective-permute-start | bytes 393224 | tf_op jit(solution)/shard_map/ppermute | solution.py:77
  51.8 7.3 %collective-permute-start.25 = (f32[256,128]{1,0:T(8,128)S(1)}, f32[256,128]{1,0:T(8,128)S(1)}, u32[]{:S(2)}, u32[]{:S(2)}) collective-permute-start(f32[256,128]{1,0:T(8,128)S(1)} %fusion), channel_id=1, source_target_pairs={{0,4},{1,5},{2,6},{3,7},{4,8},{5,9},{6,10},{7,11},{8,12},{9,13},{1... | collective-permute-start | bytes 393224 | tf_op jit(solution)/shard_map/ppermute | solution.py:77

commit v3 on v2

--- a/solution.py
+++ b/solution.py
@@ -59,38 +59,33 @@
     )(pltpu.with_memory_space_constraint(tiles, pltpu.HBM))
 
 
+def tie(x, *others):
+    x, *others = lax.optimization_barrier((x, *others))
+    return x, others
+
+
 class Grid:
     def __init__(self, n_aux):
         self.y, self.core = 2, 2
         self.z = n_aux // (self.y * self.core)
         self.offsets = [(k, j, c) for c in range(self.core) for k in range(self.z) for j in range(self.y)]
 
-    def index(self, z, y, core):
-        return (z * self.y + y) * self.core + core
-
     def other(self, me, offset):
         k, j, c = offset
-        z, y, core = me // (self.y * self.core), me // self.core % self.y, me % self.core
-        return self.index((z + k) % self.z, (y + j) % self.y, (core + c) % self.core)
+        return me ^ ((k * self.y + j) * self.core + c)
 
     def shift(self, x, offset):
         return lax.ppermute(x, "aux", [(i, self.other(i, offset)) for i in range(self.z * self.y * self.core)])
 
-    def back(self, offset):
-        return (-offset[0]) % self.z, offset[1], offset[2]
-
-
-def hops(grid):
-    return sorted(range(1, grid.z), key=lambda k: min(k, grid.z - k))
-
 
 def gather_shards(grid, x, beside):
     held = {(0, 0, 0): x}
-    for k in hops(grid):
-        held[k, 0, 0] = grid.shift(x, (-k, 0, 0))
-    first = hops(grid)[0]
-    held[first, 0, 0], beside = lax.optimization_barrier((held[first, 0, 0], beside))
-    for k in [0] + hops(grid):
+    held[3, 0, 0] = grid.shift(x, (3, 0, 0))
+    held[1, 0, 0] = grid.shift(x, (1, 0, 0))
+    held[0, 1, 0] = grid.shift(x, (0, 1, 0))
+    held[3, 0, 0], (beside, held[1, 0, 0]) = tie(held[3, 0, 0], beside, held[1, 0, 0])
+    held[2, 0, 0] = grid.shift(held[3, 0, 0], (1, 0, 0))
+    for k in (3, 1, 2):
         held[k, 1, 0] = grid.shift(held[k, 0, 0], (0, 1, 0))
     for k, j, _ in list(held):
         held[k, j, 1] = grid.shift(held[k, j, 0], (0, 0, 1))
@@ -98,16 +93,13 @@
 
 
 def scatter_sums(grid, parts):
-    order = hops(grid)[::-1] + [0]
-    crossed = {k: grid.shift(parts[1][k], (0, 0, 1)) for k in order}
-    total = {}
-    for k in order:
-        pair = parts[0][k] + crossed[k]
-        total[k] = pair[0] + grid.shift(pair[1], (0, 1, 0))
-    out = total[0]
-    for k in order[:-1]:
-        out = out + grid.shift(total[k], (k, 0, 0))
-    return out
+    crossed = {k: grid.shift(parts[1][k], (0, 0, 1)) for k in (2, 1, 3, 0)}
+    pairs = {k: parts[0][k] + crossed[k] for k in (2, 1, 3, 0)}
+    total = {k: pairs[k][0] + grid.shift(pairs[k][1], (0, 1, 0)) for k in (2, 1, 3)}
+    got = {k: grid.shift(total[k], (k, 0, 0)) for k in (2, 1, 3)}
+    last, (got[2],) = tie(pairs[0][1], got[2])
+    out = pairs[0][0] + grid.shift(last, (0, 1, 0))
+    return out + got[2] + got[1] + got[3]
 
 
 def exchange_kernel(grid, per_owner, owner_ref, sub_ref, cols_ref, order_ref, split_ref, *refs):
@@ -210,7 +202,7 @@
 
 def local(tiles, tile_owner, tile_sub, tile_cols, row_order, orbitals):
     n_aux = lax.axis_size("aux")
-    grid = Grid(n_aux) if n_aux % 4 == 0 and n_aux <= 16 else None
+    grid = Grid(n_aux) if n_aux == 16 else None
     split = prepare(tiles)
     if grid:
         shards, split = gather_shards(grid, orbitals, split)

time: 60 us -> 56.8 us (0.947)
  starting transfers between devices: 22.6 us -> 20.7 us
  waiting for transfers between devices: 22.1 us -> 20.8 us
    ppermute x26, starting transfers between devices: 22.6 us -> 20.7 us  [shift(): lax.ppermute(x, 'aux', [(i, self.other(i, offset)) for i in range(self.z...]
    ppermute x26, waiting for transfers between devices: 22.1 us -> 20.8 us  [shift(): lax.ppermute(x, 'aux', [(i, self.other(i, offset)) for i in range(self.z...]
  transfers between devices with their start and end apart: 26 -> 26, of which waited for: 11 -> 13; matrix products, arithmetic and copies ran while one was open for 0% -> 0% of each run, Pallas kernels for 9% -> 9%
where the time goes in v3:
time: 56.8 us; the launch traced here: 56.6 us
  waiting for transfers between devices  20.8 us (37%)
  starting transfers between devices  20.7 us (36%)
  Pallas kernels  14 us (25%)
  other arithmetic  0.93 us (2%)
    ppermute x26, waiting for transfers between devices, shift(): lax.ppermute(x, 'aux', [(i, self.other(i, offset)) for i in range(self.z...  20.8 us
    ppermute x26, starting transfers between devices, shift(): lax.ppermute(x, 'aux', [(i, self.other(i, offset)) for i in range(self.z...  20.7 us
    pallas_call x1, Pallas kernels, exchange(): pl.pallas_call(functools.partial(exchange_kernel, grid, per_owner), out_s...  8.79 us
    pallas_call x1, Pallas kernels, prepare(): pl.pallas_call(prepare_kernel, out_shape=pltpu.VMEM((n_tiles, aux_dev * b...  5.2 us
  transfers between devices with their start and end apart: 26, of which 13 were waited for; matrix products, arithmetic and copies ran while one was open for 0% of the time, Pallas kernels for 9%

profile of v3, /device:TPU:0, one launch (start us, length us, event | category | flops | bytes accessed | tf_op | source)
XLA Modules:
  0.0 56.6 jit_solution(5834869629945313463)
XLA Ops:
  0.0 0.0 copy-start
  0.0 0.0 copy-start.4
  0.0 0.0 copy-start.3
  0.0 0.0 copy-start.2
  0.0 3.1 %collective-permute-start.1 = (f32[256,128]{1,0:T(8,128)}, f32[256,128]{1,0:T(8,128)S(1)}, u32[]{:S(2)}, u32[]{:S(2)}) collective-permute-start(f32[256,128]{1,0:T(8,128)} %refs_0_.1), channel_id=1, source_target_pairs={{0,4},{1,5},{2,6},{3,7},{4,0},{5,1},{6,2},{7,3},{8,12},{9,13},{10,... | collective-permute-start | bytes 393224 | tf_op jit(solution)/shard_map/ppermute | solution.py:78
  3.1 2.5 %collective-permute-start = (f32[256,128]{1,0:T(8,128)}, f32[256,128]{1,0:T(8,128)S(1)}, u32[]{:S(2)}, u32[]{:S(2)}) collective-permute-start(f32[256,128]{1,0:T(8,128)} %refs_0_.1), channel_id=1, source_target_pairs={{0,12},{1,13},{2,14},{3,15},{4,8},{5,9},{6,10},{7,11},{8,4},{9,5},... | collective-permute-start | bytes 393224 | tf_op jit(solution)/shard_map/ppermute | solution.py:78
  5.6 1.5 %collective-permute-start.2 = (f32[256,128]{1,0:T(8,128)}, f32[256,128]{1,0:T(8,128)S(1)}, u32[]{:S(2)}, u32[]{:S(2)}) collective-permute-start(f32[256,128]{1,0:T(8,128)} %refs_0_.1), channel_id=1, source_target_pairs={{0,2},{1,3},{2,0},{3,1},{4,6},{5,7},{6,4},{7,5},{8,10},{9,11},{10,... | collective-permute-start | bytes 393224 | tf_op jit(solution)/shard_map/ppermute | solution.py:78
  7.1 0.0 collective-permute-start.7
  7.1 5.2 %prepare.1.split_ref = bf16[32,512,256]{2,1,0:T(8,128)(2,1)S(1)} custom-call(f32[32,4,128,128]{3,2,1,0:T(8,128)} %tiles_ref.1), custom_call_target="tpu_custom_call" | custom-call | flops 12582912 | bytes 16777216 | tf_op jit(solution)/shard_map/prepare/pallas_call | solution.py:47
  12.3 0.0 collective-permute-done.1.refs_2_
  12.3 0.0 collective-permute-done.refs_6_
  12.3 0.7 %collective-permute-start.4 = (f32[256,128]{1,0:T(8,128)S(1)}, f32[256,128]{1,0:T(8,128)S(1)}, u32[]{:S(2)}, u32[]{:S(2)}) collective-permute-start(f32[256,128]{1,0:T(8,128)S(1)} %collective-permute-done.refs_6_), channel_id=1, source_target_pairs={{0,4},{1,5},{2,6},{3,7},{4,0},{5,1},{6,2},{7,3},{8,12},{9,13},{10,... | collective-permute-start | bytes 393224 | tf_op jit(solution)/shard_map/ppermute | solution.py:78
  13.1 0.0 collective-permute-done.2.refs_1_
  13.1 0.2 collective-permute-start.8
  13.3 0.3 collective-permute-start.9
  13.6 1.0 %collective-permute-start.3 = (f32[256,128]{1,0:T(8,128)S(1)}, f32[256,128]{1,0:T(8,128)S(1)}, u32[]{:S(2)}, u32[]{:S(2)}) collective-permute-start(f32[256,128]{1,0:T(8,128)S(1)} %collective-permute-done.1.refs_2_), channel_id=1, source_target_pairs={{0,2},{1,3},{2,0},{3,1},{4,6},{5,7},{6,4},{7,5},{8,10},{9,11},{10,... | collective-permute-start | bytes 393224 | tf_op jit(solution)/shard_map/ppermute | solution.py:78
  14.6 0.0 collective-permute-done.7.refs_8_
  14.6 1.1 %collective-permute-start.6 = (f32[256,128]{1,0:T(8,128)S(1)}, f32[256,128]{1,0:T(8,128)S(1)}, u32[]{:S(2)}, u32[]{:S(2)}) collective-permute-start(f32[256,128]{1,0:T(8,128)S(1)} %collective-permute-done.refs_6_), channel_id=1, source_target_pairs={{0,2},{1,3},{2,0},{3,1},{4,6},{5,7},{6,4},{7,5},{8,10},{9,11},{10,... | collective-permute-start | bytes 393224 | tf_op jit(solution)/shard_map/ppermute | solution.py:78
  15.6 2.7 %collective-permute-done.4.refs_4_ = f32[256,128]{1,0:T(8,128)S(1)} collective-permute-done((f32[256,128]{1,0:T(8,128)S(1)}, f32[256,128]{1,0:T(8,128)S(1)}, u32[]{:S(2)}, u32[]{:S(2)}) %collective-permute-start.4) | collective-permute-done | bytes 131104 | tf_op jit(solution)/shard_map/ppermute | solution.py:78
  18.3 0.5 collective-permute-start.5
  18.8 0.0 collective-permute-done.8.refs_9_
  18.8 0.0 collective-permute-start.13
  18.8 0.0 collective-permute-done.9.refs_10_
  18.8 0.5 collective-permute-start.11
  19.3 0.6 %collective-permute-done.3.refs_3_ = f32[256,128]{1,0:T(8,128)S(1)} collective-permute-done((f32[256,128]{1,0:T(8,128)S(1)}, f32[256,128]{1,0:T(8,128)S(1)}, u32[]{:S(2)}, u32[]{:S(2)}) %collective-permute-start.3) | collective-permute-done | bytes 131104 | tf_op jit(solution)/shard_map/ppermute | solution.py:78
  19.9 0.0 collective-permute-start.10
  19.9 2.8 %collective-permute-done.6.refs_7_ = f32[256,128]{1,0:T(8,128)S(1)} collective-permute-done((f32[256,128]{1,0:T(8,128)S(1)}, f32[256,128]{1,0:T(8,128)S(1)}, u32[]{:S(2)}, u32[]{:S(2)}) %collective-permute-start.6) | collective-permute-done | bytes 131104 | tf_op jit(solution)/shard_map/ppermute | solution.py:78
  22.7 0.0 collective-permute-start.14
  22.7 2.1 %collective-permute-done.5.refs_5_ = f32[256,128]{1,0:T(8,128)S(1)} collective-permute-done((f32[256,128]{1,0:T(8,128)S(1)}, f32[256,128]{1,0:T(8,128)S(1)}, u32[]{:S(2)}, u32[]{:S(2)}) %collective-permute-start.5) | collective-permute-done | bytes 131104 | tf_op jit(solution)/shard_map/ppermute | solution.py:78
  24.9 0.0 collective-permute-start.12
  24.9 0.0 collective-permute-done.13.refs_14_
  24.9 0.0 collective-permute-done.10.refs_11_
  24.9 0.0 collective-permute-done.14.refs_15_
  24.9 0.0 collective-permute-done.11.refs_12_
  24.9 1.3 %collective-permute-done.12.refs_13_ = f32[256,128]{1,0:T(8,128)S(1)} collective-permute-done((f32[256,128]{1,0:T(8,128)S(1)}, f32[256,128]{1,0:T(8,128)S(1)}, u32[]{:S(2)}, u32[]{:S(2)}) %collective-permute-start.12) | collective-permute-done | bytes 131104 | tf_op jit(solution)/shard_map/ppermute | solution.py:78
  26.2 0.0 copy-done
  26.2 0.0 copy-done.4
  26.2 0.0 copy-done.3
  26.2 0.0 copy-done.2
  26.2 0.0 copy-done.1
  26.2 8.8 %exchange.1 = (f32[2,256,128]{2,1,0:T(8,128)S(1)}, f32[2,256,128]{2,1,0:T(8,128)S(1)}, f32[2,256,128]{2,1,0:T(8,128)S(1)}, f32[2,256,128]{2,1,0:T(8,128)S(1)}, f...) custom-call(s32[32]{0:T(128)S(1)} %bitcast.31, ...), custom_call_target="tpu_custom_call" | custom-call | tf_op jit(solution)/shard_map/exchange/pallas_call | solution.py:186
  35.0 0.2 collective-permute-start.16
  35.2 0.4 collective-permute-start.20
  35.6 0.1 collective-permute-start.15
  35.8 0.4 collective-permute-start.23
  36.1 0.5 collective-permute-done.16
  36.7 0.8 %collective-permute-start.17 = (f32[256,128]{1,0:T(8,128)S(1)}, f32[256,128]{1,0:T(8,128)S(1)}, u32[]{:S(2)}, u32[]{:S(2)}) collective-permute-start(f32[256,128]{1,0:T(8,128)S(1)} %slice_bitcast_fusion.4), channel_id=1, source_target_pairs={{0,2},{1,3},{2,0},{3,1},{4,6},{5,7},{6,4},{7,5},{8,10},{9,11},{10,... | collective-permute-start | bytes 393224 | tf_op jit(solution)/shard_map/ppermute | solution.py:78
  37.5 0.0 collective-permute-done.20
  37.6 1.3 %collective-permute-start.21 = (f32[256,128]{1,0:T(8,128)S(1)}, f32[256,128]{1,0:T(8,128)S(1)}, u32[]{:S(2)}, u32[]{:S(2)}) collective-permute-start(f32[256,128]{1,0:T(8,128)S(1)} %slice_bitcast_fusion.2), channel_id=1, source_target_pairs={{0,2},{1,3},{2,0},{3,1},{4,6},{5,7},{6,4},{7,5},{8,10},{9,11},{10,... | collective-permute-start | bytes 393224 | tf_op jit(solution)/shard_map/ppermute | solution.py:78
  38.9 0.0 collective-permute-done.23
  39.0 0.8 %collective-permute-start.24 = (f32[256,128]{1,0:T(8,128)S(1)}, f32[256,128]{1,0:T(8,128)S(1)}, u32[]{:S(2)}, u32[]{:S(2)}) collective-permute-start(f32[256,128]{1,0:T(8,128)S(1)} %slice_bitcast_fusion), channel_id=1, source_target_pairs={{0,2},{1,3},{2,0},{3,1},{4,6},{5,7},{6,4},{7,5},{8,10},{9,11},{10,... | collective-permute-start | bytes 393224 | tf_op jit(solution)/shard_map/ppermute | solution.py:78
  39.8 0.0 collective-permute-done.15
  39.8 3.3 %collective-permute-done.17 = f32[256,128]{1,0:T(8,128)S(1)} collective-permute-done((f32[256,128]{1,0:T(8,128)S(1)}, f32[256,128]{1,0:T(8,128)S(1)}, u32[]{:S(2)}, u32[]{:S(2)}) %collective-permute-start.17) | collective-permute-done | bytes 131104 | tf_op jit(solution)/shard_map/ppermute | solution.py:78
  43.1 1.3 %collective-permute-start.18 = (f32[256,128]{1,0:T(8,128)S(1)}, f32[256,128]{1,0:T(8,128)S(1)}, u32[]{:S(2)}, u32[]{:S(2)}) collective-permute-start(f32[256,128]{1,0:T(8,128)S(1)} %fusion.2), channel_id=1, source_target_pairs={{0,8},{1,9},{2,10},{3,11},{4,12},{5,13},{6,14},{7,15},{8,0},{9,1},... | collective-permute-start | bytes 393224 | tf_op jit(solution)/shard_map/ppermute | solution.py:78
  44.4 1.5 %collective-permute-done.21 = f32[256,128]{1,0:T(8,128)S(1)} collective-permute-done((f32[256,128]{1,0:T(8,128)S(1)}, f32[256,128]{1,0:T(8,128)S(1)}, u32[]{:S(2)}, u32[]{:S(2)}) %collective-permute-start.21) | collective-permute-done | bytes 131104 | tf_op jit(solution)/shard_map/ppermute | solution.py:78
  45.9 1.4 %collective-permute-start.22 = (f32[256,128]{1,0:T(8,128)S(1)}, f32[256,128]{1,0:T(8,128)S(1)}, u32[]{:S(2)}, u32[]{:S(2)}) collective-permute-start(f32[256,128]{1,0:T(8,128)S(1)} %fusion.1), channel_id=1, source_target_pairs={{0,4},{1,5},{2,6},{3,7},{4,0},{5,1},{6,2},{7,3},{8,12},{9,13},{10,... | collective-permute-start | bytes 393224 | tf_op jit(solution)/shard_map/ppermute | solution.py:78
  47.3 0.6 %collective-permute-done.24 = f32[256,128]{1,0:T(8,128)S(1)} collective-permute-done((f32[256,128]{1,0:T(8,128)S(1)}, f32[256,128]{1,0:T(8,128)S(1)}, u32[]{:S(2)}, u32[]{:S(2)}) %collective-permute-start.24) | collective-permute-done | bytes 131104 | tf_op jit(solution)/shard_map/ppermute | solution.py:78
  47.9 1.9 %collective-permute-start.25 = (f32[256,128]{1,0:T(8,128)S(1)}, f32[256,128]{1,0:T(8,128)S(1)}, u32[]{:S(2)}, u32[]{:S(2)}) collective-permute-start(f32[256,128]{1,0:T(8,128)S(1)} %fusion), channel_id=1, source_target_pairs={{0,12},{1,13},{2,14},{3,15},{4,8},{5,9},{6,10},{7,11},{8,4},{9,5},... | collective-permute-start | bytes 393224 | tf_op jit(solution)/shard_map/ppermute | solution.py:78
  49.8 1.1 %collective-permute-done.18 = f32[256,128]{1,0:T(8,128)S(1)} collective-permute-done((f32[256,128]{1,0:T(8,128)S(1)}, f32[256,128]{1,0:T(8,128)S(1)}, u32[]{:S(2)}, u32[]{:S(2)}) %collective-permute-start.18) | collective-permute-done | bytes 131104 | tf_op jit(solution)/shard_map/ppermute | solution.py:78
  50.9 0.6 %collective-permute-start.19 = (f32[256,128]{1,0:T(8,128)S(1)}, f32[256,128]{1,0:T(8,128)S(1)}, u32[]{:S(2)}, u32[]{:S(2)}) collective-permute-start(f32[256,128]{1,0:T(8,128)S(1)} %slice_bitcast_fusion.6), channel_id=1, source_target_pairs={{0,2},{1,3},{2,0},{3,1},{4,6},{5,7},{6,4},{7,5},{8,10},{9,11},{10,... | collective-permute-start | bytes 393224 | tf_op jit(solution)/shard_map/ppermute | solution.py:78
  51.5 0.4 collective-permute-done.22
  51.9 3.0 %collective-permute-done.25 = f32[256,128]{1,0:T(8,128)S(1)} collective-permute-done((f32[256,128]{1,0:T(8,128)S(1)}, f32[256,128]{1,0:T(8,128)S(1)}, u32[]{:S(2)}, u32[]{:S(2)}) %collective-permute-start.25) | collective-permute-done | bytes 131104 | tf_op jit(solution)/shard_map/ppermute | solution.py:78
  54.9 1.0 %collective-permute-done.19 = f32[256,128]{1,0:T(8,128)S(1)} collective-permute-done((f32[256,128]{1,0:T(8,128)S(1)}, f32[256,128]{1,0:T(8,128)S(1)}, u32[]{:S(2)}, u32[]{:S(2)}) %collective-permute-start.19) | collective-permute-done | bytes 131104 | tf_op jit(solution)/shard_map/ppermute | solution.py:78
  55.9 0.7 %fusion.6 = f32[256,128]{1,0:T(8,128)} fusion(f32[256,128]{1,0:T(8,128)S(1)} %collective-permute-done.25, f32[256,128]{1,0:T(8,128)S(1)} %collective-permute-done.22, f32[256,128]{1,0:T(8,128)S(1)} %collective-permute-done.18, f32[256,128]{1,0:T(8,128)S(1)} %collective-permute-done.19, f32[2,256,128]{2,1,0:T(8,128)S(1)} %add.33), kind=kLoop, calls=%fused_computation.14 | loop fusion | flops 131072 | bytes 786432 | tf_op jit(solution)/shard_map/add | solution.py:102
  (12 shorter events, 0.3 us)
Async XLA Ops:
  0.0 26.2 %copy-start = (f32[256,128]{1,0:T(8,128)S(1)}, f32[256,128]{1,0:T(8,128)}, u32[]{:S(2)}) copy-start(f32[256,128]{1,0:T(8,128)} %refs_0_.1) | copy-start | bytes 393220
  0.0 26.2 %copy-start.4 = (s32[32]{0:T(128)S(1)}, s32[32]{0:T(128)}, u32[]{:S(2)}) copy-start(s32[32]{0:T(128)} %order_ref.1) | copy-start | bytes 388
  0.0 26.2 %copy-start.3 = (s32[32]{0:T(128)S(1)}, s32[32]{0:T(128)}, u32[]{:S(2)}) copy-start(s32[32]{0:T(128)} %cols_ref.1) | copy-start | bytes 388
  0.0 26.2 %copy-start.2 = (s32[32]{0:T(128)S(1)}, s32[32]{0:T(128)}, u32[]{:S(2)}) copy-start(s32[32]{0:T(128)} %sub_ref.1) | copy-start | bytes 388
  0.0 26.2 %copy-start.1 = (s32[32,1]{0,1:T(1,128)S(1)}, s32[32,1]{0,1:T(1,128)}, u32[]{:S(2)}) copy-start(s32[32,1]{0,1:T(1,128)} %param.7) | copy-start | bytes 388
  0.0 12.3 %collective-permute-start.1 = (f32[256,128]{1,0:T(8,128)}, f32[256,128]{1,0:T(8,128)S(1)}, u32[]{:S(2)}, u32[]{:S(2)}) collective-permute-start(f32[256,128]{1,0:T(8,128)} %refs_0_.1), channel_id=1, source_target_pairs={{0,4},{1,5},{2,6},{3,7},{4,0},{5,1},{6,2},{7,3},{8,12},{9,13},{10,... | collective-permute-start | bytes 393224 | tf_op jit(solution)/shard_map/ppermute | solution.py:78
  3.1 9.2 %collective-permute-start = (f32[256,128]{1,0:T(8,128)}, f32[256,128]{1,0:T(8,128)S(1)}, u32[]{:S(2)}, u32[]{:S(2)}) collective-permute-start(f32[256,128]{1,0:T(8,128)} %refs_0_.1), channel_id=1, source_target_pairs={{0,12},{1,13},{2,14},{3,15},{4,8},{5,9},{6,10},{7,11},{8,4},{9,5},... | collective-permute-start | bytes 393224 | tf_op jit(solution)/shard_map/ppermute | solution.py:78
  5.6 7.5 %collective-permute-start.2 = (f32[256,128]{1,0:T(8,128)}, f32[256,128]{1,0:T(8,128)S(1)}, u32[]{:S(2)}, u32[]{:S(2)}) collective-permute-start(f32[256,128]{1,0:T(8,128)} %refs_0_.1), channel_id=1, source_target_pairs={{0,2},{1,3},{2,0},{3,1},{4,6},{5,7},{6,4},{7,5},{8,10},{9,11},{10,... | collective-permute-start | bytes 393224 | tf_op jit(solution)/shard_map/ppermute | solution.py:78
  7.1 7.5 %collective-permute-start.7 = (f32[256,128]{1,0:T(8,128)}, f32[256,128]{1,0:T(8,128)S(1)}, u32[]{:S(2)}, u32[]{:S(2)}) collective-permute-start(f32[256,128]{1,0:T(8,128)} %refs_0_.1), channel_id=1, source_target_pairs={{0,1},{1,0},{2,3},{3,2},{4,5},{5,4},{6,7},{7,6},{8,9},{9,8},{10,11... | collective-permute-start | bytes 393224 | tf_op jit(solution)/shard_map/ppermute | solution.py:78
  12.3 6.0 %collective-permute-start.4 = (f32[256,128]{1,0:T(8,128)S(1)}, f32[256,128]{1,0:T(8,128)S(1)}, u32[]{:S(2)}, u32[]{:S(2)}) collective-permute-start(f32[256,128]{1,0:T(8,128)S(1)} %collective-permute-done.refs_6_), channel_id=1, source_target_pairs={{0,4},{1,5},{2,6},{3,7},{4,0},{5,1},{6,2},{7,3},{8,12},{9,13},{10,... | collective-permute-start | bytes 393224 | tf_op jit(solution)/shard_map/ppermute | solution.py:78
  13.1 5.7 %collective-permute-start.8 = (f32[256,128]{1,0:T(8,128)S(1)}, f32[256,128]{1,0:T(8,128)S(1)}, u32[]{:S(2)}, u32[]{:S(2)}) collective-permute-start(f32[256,128]{1,0:T(8,128)S(1)} %collective-permute-done.2.refs_1_), channel_id=1, source_target_pairs={{0,1},{1,0},{2,3},{3,2},{4,5},{5,4},{6,7},{7,6},{8,9},{9,8},{10,11... | collective-permute-start | bytes 393224 | tf_op jit(solution)/shard_map/ppermute | solution.py:78
  13.3 5.5 %collective-permute-start.9 = (f32[256,128]{1,0:T(8,128)S(1)}, f32[256,128]{1,0:T(8,128)S(1)}, u32[]{:S(2)}, u32[]{:S(2)}) collective-permute-start(f32[256,128]{1,0:T(8,128)S(1)} %collective-permute-done.1.refs_2_), channel_id=1, source_target_pairs={{0,1},{1,0},{2,3},{3,2},{4,5},{5,4},{6,7},{7,6},{8,9},{9,8},{10,11... | collective-permute-start | bytes 393224 | tf_op jit(solution)/shard_map/ppermute | solution.py:78
  13.6 6.3 %collective-permute-start.3 = (f32[256,128]{1,0:T(8,128)S(1)}, f32[256,128]{1,0:T(8,128)S(1)}, u32[]{:S(2)}, u32[]{:S(2)}) collective-permute-start(f32[256,128]{1,0:T(8,128)S(1)} %collective-permute-done.1.refs_2_), channel_id=1, source_target_pairs={{0,2},{1,3},{2,0},{3,1},{4,6},{5,7},{6,4},{7,5},{8,10},{9,11},{10,... | collective-permute-start | bytes 393224 | tf_op jit(solution)/shard_map/ppermute | solution.py:78
  14.6 8.2 %collective-permute-start.6 = (f32[256,128]{1,0:T(8,128)S(1)}, f32[256,128]{1,0:T(8,128)S(1)}, u32[]{:S(2)}, u32[]{:S(2)}) collective-permute-start(f32[256,128]{1,0:T(8,128)S(1)} %collective-permute-done.refs_6_), channel_id=1, source_target_pairs={{0,2},{1,3},{2,0},{3,1},{4,6},{5,7},{6,4},{7,5},{8,10},{9,11},{10,... | collective-permute-start | bytes 393224 | tf_op jit(solution)/shard_map/ppermute | solution.py:78
  18.3 6.5 %collective-permute-start.5 = (f32[256,128]{1,0:T(8,128)S(1)}, f32[256,128]{1,0:T(8,128)S(1)}, u32[]{:S(2)}, u32[]{:S(2)}) collective-permute-start(f32[256,128]{1,0:T(8,128)S(1)} %collective-permute-done.4.refs_4_), channel_id=1, source_target_pairs={{0,2},{1,3},{2,0},{3,1},{4,6},{5,7},{6,4},{7,5},{8,10},{9,11},{10,... | collective-permute-start | bytes 393224 | tf_op jit(solution)/shard_map/ppermute | solution.py:78
  18.8 6.0 %collective-permute-start.13 = (f32[256,128]{1,0:T(8,128)S(1)}, f32[256,128]{1,0:T(8,128)S(1)}, u32[]{:S(2)}, u32[]{:S(2)}) collective-permute-start(f32[256,128]{1,0:T(8,128)S(1)} %collective-permute-done.refs_6_), channel_id=1, source_target_pairs={{0,1},{1,0},{2,3},{3,2},{4,5},{5,4},{6,7},{7,6},{8,9},{9,8},{10,11... | collective-permute-start | bytes 393224 | tf_op jit(solution)/shard_map/ppermute | solution.py:78
  18.8 6.0 %collective-permute-start.11 = (f32[256,128]{1,0:T(8,128)S(1)}, f32[256,128]{1,0:T(8,128)S(1)}, u32[]{:S(2)}, u32[]{:S(2)}) collective-permute-start(f32[256,128]{1,0:T(8,128)S(1)} %collective-permute-done.4.refs_4_), channel_id=1, source_target_pairs={{0,1},{1,0},{2,3},{3,2},{4,5},{5,4},{6,7},{7,6},{8,9},{9,8},{10,11... | collective-permute-start | bytes 393224 | tf_op jit(solution)/shard_map/ppermute | solution.py:78
  19.9 4.9 %collective-permute-start.10 = (f32[256,128]{1,0:T(8,128)S(1)}, f32[256,128]{1,0:T(8,128)S(1)}, u32[]{:S(2)}, u32[]{:S(2)}) collective-permute-start(f32[256,128]{1,0:T(8,128)S(1)} %collective-permute-done.3.refs_3_), channel_id=1, source_target_pairs={{0,1},{1,0},{2,3},{3,2},{4,5},{5,4},{6,7},{7,6},{8,9},{9,8},{10,11... | collective-permute-start | bytes 393224 | tf_op jit(solution)/shard_map/ppermute | solution.py:78
  22.7 2.1 %collective-permute-start.14 = (f32[256,128]{1,0:T(8,128)S(1)}, f32[256,128]{1,0:T(8,128)S(1)}, u32[]{:S(2)}, u32[]{:S(2)}) collective-permute-start(f32[256,128]{1,0:T(8,128)S(1)} %collective-permute-done.6.refs_7_), channel_id=1, source_target_pairs={{0,1},{1,0},{2,3},{3,2},{4,5},{5,4},{6,7},{7,6},{8,9},{9,8},{10,11... | collective-permute-start | bytes 393224 | tf_op jit(solution)/shard_map/ppermute | solution.py:78
  24.9 1.3 %collective-permute-start.12 = (f32[256,128]{1,0:T(8,128)S(1)}, f32[256,128]{1,0:T(8,128)S(1)}, u32[]{:S(2)}, u32[]{:S(2)}) collective-permute-start(f32[256,128]{1,0:T(8,128)S(1)} %collective-permute-done.5.refs_5_), channel_id=1, source_target_pairs={{0,1},{1,0},{2,3},{3,2},{4,5},{5,4},{6,7},{7,6},{8,9},{9,8},{10,11... | collective-permute-start | bytes 393224 | tf_op jit(solution)/shard_map/ppermute | solution.py:78
  35.0 1.6 %collective-permute-start.16 = (f32[2,256,128]{2,1,0:T(8,128)S(1)}, f32[2,256,128]{2,1,0:T(8,128)S(1)}, u32[]{:S(2)}, u32[]{:S(2)}) collective-permute-start(f32[2,256,128]{2,1,0:T(8,128)S(1)} %get-tuple-element.24), channel_id=1, source_target_pairs={{0,1},{1,0},{2,3},{3,2},{4,5},{5,4},{6,7},{7,6},{8,9},{9,8},{10,11... | collective-permute-start | bytes 786440 | tf_op jit(solution)/shard_map/ppermute | solution.py:78
  35.2 2.3 %collective-permute-start.20 = (f32[2,256,128]{2,1,0:T(8,128)S(1)}, f32[2,256,128]{2,1,0:T(8,128)S(1)}, u32[]{:S(2)}, u32[]{:S(2)}) collective-permute-start(f32[2,256,128]{2,1,0:T(8,128)S(1)} %get-tuple-element.28), channel_id=1, source_target_pairs={{0,1},{1,0},{2,3},{3,2},{4,5},{5,4},{6,7},{7,6},{8,9},{9,8},{10,11... | collective-permute-start | bytes 786440 | tf_op jit(solution)/shard_map/ppermute | solution.py:78
  35.6 4.2 %collective-permute-start.15 = (f32[2,256,128]{2,1,0:T(8,128)S(1)}, f32[2,256,128]{2,1,0:T(8,128)S(1)}, u32[]{:S(2)}, u32[]{:S(2)}) collective-permute-start(f32[2,256,128]{2,1,0:T(8,128)S(1)} %get-tuple-element.22), channel_id=1, source_target_pairs={{0,1},{1,0},{2,3},{3,2},{4,5},{5,4},{6,7},{7,6},{8,9},{9,8},{10,11... | collective-permute-start | bytes 786440 | tf_op jit(solution)/shard_map/ppermute | solution.py:78
  35.8 3.2 %collective-permute-start.23 = (f32[2,256,128]{2,1,0:T(8,128)S(1)}, f32[2,256,128]{2,1,0:T(8,128)S(1)}, u32[]{:S(2)}, u32[]{:S(2)}) collective-permute-start(f32[2,256,128]{2,1,0:T(8,128)S(1)} %get-tuple-element.30), channel_id=1, source_target_pairs={{0,1},{1,0},{2,3},{3,2},{4,5},{5,4},{6,7},{7,6},{8,9},{9,8},{10,11... | collective-permute-start | bytes 786440 | tf_op jit(solution)/shard_map/ppermute | solution.py:78
  36.7 6.4 %collective-permute-start.17 = (f32[256,128]{1,0:T(8,128)S(1)}, f32[256,128]{1,0:T(8,128)S(1)}, u32[]{:S(2)}, u32[]{:S(2)}) collective-permute-start(f32[256,128]{1,0:T(8,128)S(1)} %slice_bitcast_fusion.4), channel_id=1, source_target_pairs={{0,2},{1,3},{2,0},{3,1},{4,6},{5,7},{6,4},{7,5},{8,10},{9,11},{10,... | collective-permute-start | bytes 393224 | tf_op jit(solution)/shard_map/ppermute | solution.py:78
  37.6 8.3 %collective-permute-start.21 = (f32[256,128]{1,0:T(8,128)S(1)}, f32[256,128]{1,0:T(8,128)S(1)}, u32[]{:S(2)}, u32[]{:S(2)}) collective-permute-start(f32[256,128]{1,0:T(8,128)S(1)} %slice_bitcast_fusion.2), channel_id=1, source_target_pairs={{0,2},{1,3},{2,0},{3,1},{4,6},{5,7},{6,4},{7,5},{8,10},{9,11},{10,... | collective-permute-start | bytes 393224 | tf_op jit(solution)/shard_map/ppermute | solution.py:78
  39.0 9.0 %collective-permute-start.24 = (f32[256,128]{1,0:T(8,128)S(1)}, f32[256,128]{1,0:T(8,128)S(1)}, u32[]{:S(2)}, u32[]{:S(2)}) collective-permute-start(f32[256,128]{1,0:T(8,128)S(1)} %slice_bitcast_fusion), channel_id=1, source_target_pairs={{0,2},{1,3},{2,0},{3,1},{4,6},{5,7},{6,4},{7,5},{8,10},{9,11},{10,... | collective-permute-start | bytes 393224 | tf_op jit(solution)/shard_map/ppermute | solution.py:78
  43.1 7.8 %collective-permute-start.18 = (f32[256,128]{1,0:T(8,128)S(1)}, f32[256,128]{1,0:T(8,128)S(1)}, u32[]{:S(2)}, u32[]{:S(2)}) collective-permute-start(f32[256,128]{1,0:T(8,128)S(1)} %fusion.2), channel_id=1, source_target_pairs={{0,8},{1,9},{2,10},{3,11},{4,12},{5,13},{6,14},{7,15},{8,0},{9,1},... | collective-permute-start | bytes 393224 | tf_op jit(solution)/shard_map/ppermute | solution.py:78
  45.9 6.0 %collective-permute-start.22 = (f32[256,128]{1,0:T(8,128)S(1)}, f32[256,128]{1,0:T(8,128)S(1)}, u32[]{:S(2)}, u32[]{:S(2)}) collective-permute-start(f32[256,128]{1,0:T(8,128)S(1)} %fusion.1), channel_id=1, source_target_pairs={{0,4},{1,5},{2,6},{3,7},{4,0},{5,1},{6,2},{7,3},{8,12},{9,13},{10,... | collective-permute-start | bytes 393224 | tf_op jit(solution)/shard_map/ppermute | solution.py:78
  47.9 7.0 %collective-permute-start.25 = (f32[256,128]{1,0:T(8,128)S(1)}, f32[256,128]{1,0:T(8,128)S(1)}, u32[]{:S(2)}, u32[]{:S(2)}) collective-permute-start(f32[256,128]{1,0:T(8,128)S(1)} %fusion), channel_id=1, source_target_pairs={{0,12},{1,13},{2,14},{3,15},{4,8},{5,9},{6,10},{7,11},{8,4},{9,5},... | collective-permute-start | bytes 393224 | tf_op jit(solution)/shard_map/ppermute | solution.py:78
  50.9 5.0 %collective-permute-start.19 = (f32[256,128]{1,0:T(8,128)S(1)}, f32[256,128]{1,0:T(8,128)S(1)}, u32[]{:S(2)}, u32[]{:S(2)}) collective-permute-start(f32[256,128]{1,0:T(8,128)S(1)} %slice_bitcast_fusion.6), channel_id=1, source_target_pairs={{0,2},{1,3},{2,0},{3,1},{4,6},{5,7},{6,4},{7,5},{8,10},{9,11},{10,... | collective-permute-start | bytes 393224 | tf_op jit(solution)/shard_map/ppermute | solution.py:78

commit v4 on v3

--- a/solution.py
+++ b/solution.py
@@ -9,7 +9,6 @@
 
 F32, BF16 = jnp.float32, jnp.bfloat16
 MIB = 1 << 20
-HALF_UNROLL, FIT, OUT = 16, 16, 16
 
 
 def halves(x):
@@ -84,22 +83,28 @@
     held[1, 0, 0] = grid.shift(x, (1, 0, 0))
     held[0, 1, 0] = grid.shift(x, (0, 1, 0))
     held[3, 0, 0], (beside, held[1, 0, 0]) = tie(held[3, 0, 0], beside, held[1, 0, 0])
+    held[3, 1, 0] = grid.shift(held[3, 0, 0], (0, 1, 0))
     held[2, 0, 0] = grid.shift(held[3, 0, 0], (1, 0, 0))
-    for k in (3, 1, 2):
-        held[k, 1, 0] = grid.shift(held[k, 0, 0], (0, 1, 0))
+    held[3, 1, 0], (held[1, 0, 0],) = tie(held[3, 1, 0], held[1, 0, 0])
+    held[2, 1, 0] = grid.shift(held[3, 1, 0], (1, 0, 0))
+    held[1, 1, 0] = grid.shift(held[1, 0, 0], (0, 1, 0))
     for k, j, _ in list(held):
         held[k, j, 1] = grid.shift(held[k, j, 0], (0, 0, 1))
     return [held[o] for o in grid.offsets], beside
 
 
 def scatter_sums(grid, parts):
-    crossed = {k: grid.shift(parts[1][k], (0, 0, 1)) for k in (2, 1, 3, 0)}
-    pairs = {k: parts[0][k] + crossed[k] for k in (2, 1, 3, 0)}
-    total = {k: pairs[k][0] + grid.shift(pairs[k][1], (0, 1, 0)) for k in (2, 1, 3)}
-    got = {k: grid.shift(total[k], (k, 0, 0)) for k in (2, 1, 3)}
-    last, (got[2],) = tie(pairs[0][1], got[2])
-    out = pairs[0][0] + grid.shift(last, (0, 1, 0))
-    return out + got[2] + got[1] + got[3]
+    crossed = {k: grid.shift(parts[1][k], (0, 0, 1)) for k in (2, 3, 1, 0)}
+    pairs = {k: parts[0][k] + crossed[k] for k in (2, 3, 1, 0)}
+    far_away = grid.shift(pairs[2][1], (1, 0, 0))
+    far_here, (far_away,) = tie(pairs[2][0], far_away)
+    far_here = grid.shift(far_here, (1, 0, 0))
+    near = pairs[1][0] + grid.shift(pairs[1][1], (0, 1, 0))
+    mirror = grid.shift(pairs[3][1] + far_away, (0, 1, 0))
+    own, (mirror,) = tie(pairs[0][1], mirror)
+    mirror = pairs[3][0] + far_here + mirror
+    own = pairs[0][0] + grid.shift(own, (0, 1, 0))
+    return own + grid.shift(near, (1, 0, 0)) + grid.shift(mirror, (3, 0, 0))
 
 
 def exchange_kernel(grid, per_owner, owner_ref, sub_ref, cols_ref, order_ref, split_ref, *refs):
@@ -129,22 +134,17 @@
             wide[t, :, p * pair + block : (p + 1) * pair] = lo[p * block : (p + 1) * block]
         return 0
 
-    lax.fori_loop(0, n_tiles, half_step, 0, unroll=HALF_UNROLL)
-    fitted[...] = jnp.zeros_like(fitted)
-
-    def fit_step(step, _):
-        left, right = [], []
-        for i in range(FIT):
-            t = step * FIT + i
-            c_hi, c_lo = halves(coeff[order_ref[position(t)]].T)
-            left.append(jnp.concatenate([jnp.concatenate([c_hi, c_hi], axis=1), jnp.concatenate([c_lo, c_lo], axis=1)], axis=0))
-            w = wide[t]
-            right.append(jnp.concatenate([w[:, p * pair : p * pair + block] for p in range(aux_dev)], axis=1))
-            right.append(jnp.concatenate([w[:, p * pair + block : (p + 1) * pair] for p in range(aux_dev)], axis=1))
-        fitted[...] += dot(jnp.concatenate(left, axis=1), jnp.concatenate(right, axis=0))
-        return 0
-
-    lax.fori_loop(0, n_tiles // FIT, fit_step, 0)
+    lax.fori_loop(0, n_tiles, half_step, 0, unroll=True)
+    left, right_hi, right_lo = [], [], []
+    for t in range(n_tiles):
+        c_hi, c_lo = halves(coeff[order_ref[position(t)]].T)
+        left.append(jnp.concatenate([c_hi, c_lo], axis=0))
+        w = wide[t]
+        right_hi.append(jnp.concatenate([w[:, p * pair : p * pair + block] for p in range(aux_dev)], axis=1))
+        right_lo.append(jnp.concatenate([w[:, p * pair + block : (p + 1) * pair] for p in range(aux_dev)], axis=1))
+    left = jnp.concatenate(left, axis=1)
+    fitted[...] = dot(left, jnp.concatenate(right_hi, axis=0))
+    fitted[:block, :] += dot(left[:block], jnp.concatenate(right_lo, axis=0))
     for p in range(aux_dev):
         at = pl.ds(p * block, block)
         f_hi, f_lo = halves((fitted[:block, at] + fitted[block:, at]).T)
@@ -153,14 +153,10 @@
         weights[p * pair + block : (p + 1) * pair, :] = both
     summed[...] = jnp.zeros_like(summed)
 
-    def out_step(step, _):
-        both = dot(wide[pl.ds(step * OUT, OUT)].reshape(OUT * block, -1), weights[...])
-        value = both[:, :block] + both[:, block:]
-        for i in range(OUT):
-            summed[position(step * OUT + i)] += value[i * block : (i + 1) * block]
-        return 0
-
-    lax.fori_loop(0, n_tiles // OUT, out_step, 0)
+    both = dot(wide[...].reshape(n_tiles * block, -1), weights[...])
+    value = both[:, :block] + both[:, block:]
+    for t in range(n_tiles):
+        summed[position(t)] += value[t * block : (t + 1) * block]
     if grid:
         for c in range(grid.core):
             for k in range(grid.z):

time: 56.8 us -> 54.1 us (0.952)
  Pallas kernels: 14 us -> 12.6 us
  starting transfers between devices: 20.7 us -> 19.9 us
    pallas_call x1, Pallas kernels: 8.79 us -> 7.42 us  [exchange(): pl.pallas_call(functools.partial(exchange_kernel, grid, per_owner), out_s...]
    ppermute x26, starting transfers between devices: 20.7 us -> 19.9 us  [shift(): lax.ppermute(x, 'aux', [(i, self.other(i, offset)) for i in range(self.z...]
  transfers between devices with their start and end apart: 26 -> 26, of which waited for: 13 -> 12; matrix products, arithmetic and copies ran while one was open for 0% -> 0% of each run, Pallas kernels for 9% -> 10%
where the time goes in v4:
time: 54.1 us; the launch traced here: 53.9 us
  waiting for transfers between devices  20.3 us (38%)
  starting transfers between devices  19.9 us (37%)
  Pallas kernels  12.6 us (23%)
  other arithmetic  0.91 us (2%)
    ppermute x26, waiting for transfers between devices, shift(): lax.ppermute(x, 'aux', [(i, self.other(i, offset)) for i in range(self.z...  20.3 us
    ppermute x26, starting transfers between devices, shift(): lax.ppermute(x, 'aux', [(i, self.other(i, offset)) for i in range(self.z...  19.9 us
    pallas_call x1, Pallas kernels, exchange(): pl.pallas_call(functools.partial(exchange_kernel, grid, per_owner), out_s...  7.42 us
    pallas_call x1, Pallas kernels, prepare(): pl.pallas_call(prepare_kernel, out_shape=pltpu.VMEM((n_tiles, aux_dev * b...  5.2 us
  transfers between devices with their start and end apart: 26, of which 12 were waited for; matrix products, arithmetic and copies ran while one was open for 0% of the time, Pallas kernels for 10%

profile of v4, /device:TPU:0, one launch (start us, length us, event | category | flops | bytes accessed | tf_op | source)
XLA Modules:
  0.0 53.9 jit_solution(9741050891927694727)
XLA Ops:
  0.0 0.0 copy-start
  0.0 0.0 copy-start.4
  0.0 0.0 copy-start.3
  0.0 0.0 copy-start.2
  0.0 3.1 %collective-permute-start.1 = (f32[256,128]{1,0:T(8,128)}, f32[256,128]{1,0:T(8,128)S(1)}, u32[]{:S(2)}, u32[]{:S(2)}) collective-permute-start(f32[256,128]{1,0:T(8,128)} %refs_0_.1), channel_id=1, source_target_pairs={{0,4},{1,5},{2,6},{3,7},{4,0},{5,1},{6,2},{7,3},{8,12},{9,13},{10,... | collective-permute-start | bytes 393224 | tf_op jit(solution)/shard_map/ppermute | solution.py:77
  3.1 2.5 %collective-permute-start = (f32[256,128]{1,0:T(8,128)}, f32[256,128]{1,0:T(8,128)S(1)}, u32[]{:S(2)}, u32[]{:S(2)}) collective-permute-start(f32[256,128]{1,0:T(8,128)} %refs_0_.1), channel_id=1, source_target_pairs={{0,12},{1,13},{2,14},{3,15},{4,8},{5,9},{6,10},{7,11},{8,4},{9,5},... | collective-permute-start | bytes 393224 | tf_op jit(solution)/shard_map/ppermute | solution.py:77
  5.6 1.5 %collective-permute-start.2 = (f32[256,128]{1,0:T(8,128)}, f32[256,128]{1,0:T(8,128)S(1)}, u32[]{:S(2)}, u32[]{:S(2)}) collective-permute-start(f32[256,128]{1,0:T(8,128)} %refs_0_.1), channel_id=1, source_target_pairs={{0,2},{1,3},{2,0},{3,1},{4,6},{5,7},{6,4},{7,5},{8,10},{9,11},{10,... | collective-permute-start | bytes 393224 | tf_op jit(solution)/shard_map/ppermute | solution.py:77
  7.1 5.2 %prepare.1.split_ref = bf16[32,512,256]{2,1,0:T(8,128)(2,1)S(1)} custom-call(f32[32,4,128,128]{3,2,1,0:T(8,128)} %tiles_ref.1), custom_call_target="tpu_custom_call" | custom-call | flops 12582912 | bytes 16777216 | tf_op jit(solution)/shard_map/prepare/pallas_call | solution.py:46
  12.3 0.0 collective-permute-done.1.refs_2_
  12.3 0.0 collective-permute-done.refs_6_
  12.3 1.1 %collective-permute-start.3 = (f32[256,128]{1,0:T(8,128)S(1)}, f32[256,128]{1,0:T(8,128)S(1)}, u32[]{:S(2)}, u32[]{:S(2)}) collective-permute-start(f32[256,128]{1,0:T(8,128)S(1)} %collective-permute-done.refs_6_), channel_id=1, source_target_pairs={{0,2},{1,3},{2,0},{3,1},{4,6},{5,7},{6,4},{7,5},{8,10},{9,11},{10,... | collective-permute-start | bytes 393224 | tf_op jit(solution)/shard_map/ppermute | solution.py:77
  13.5 0.0 copy-done
  13.5 0.0 collective-permute-start.7
  13.5 0.5 collective-permute-start.13
  14.0 0.6 %collective-permute-start.5 = (f32[256,128]{1,0:T(8,128)S(1)}, f32[256,128]{1,0:T(8,128)S(1)}, u32[]{:S(2)}, u32[]{:S(2)}) collective-permute-start(f32[256,128]{1,0:T(8,128)S(1)} %collective-permute-done.refs_6_), channel_id=1, source_target_pairs={{0,4},{1,5},{2,6},{3,7},{4,0},{5,1},{6,2},{7,3},{8,12},{9,13},{10,... | collective-permute-start | bytes 393224 | tf_op jit(solution)/shard_map/ppermute | solution.py:77
  14.6 0.0 collective-permute-done.2.refs_1_
  14.6 0.0 collective-permute-start.8
  14.6 2.8 %collective-permute-done.3.refs_7_ = f32[256,128]{1,0:T(8,128)S(1)} collective-permute-done((f32[256,128]{1,0:T(8,128)S(1)}, f32[256,128]{1,0:T(8,128)S(1)}, u32[]{:S(2)}, u32[]{:S(2)}) %collective-permute-start.3) | collective-permute-done | bytes 131104 | tf_op jit(solution)/shard_map/ppermute | solution.py:77
  17.4 1.0 %collective-permute-start.4 = (f32[256,128]{1,0:T(8,128)S(1)}, f32[256,128]{1,0:T(8,128)S(1)}, u32[]{:S(2)}, u32[]{:S(2)}) collective-permute-start(f32[256,128]{1,0:T(8,128)S(1)} %collective-permute-done.1.refs_2_), channel_id=1, source_target_pairs={{0,2},{1,3},{2,0},{3,1},{4,6},{5,7},{6,4},{7,5},{8,10},{9,11},{10,... | collective-permute-start | bytes 393224 | tf_op jit(solution)/shard_map/ppermute | solution.py:77
  18.4 0.0 collective-permute-done.7.refs_8_
  18.4 0.6 %collective-permute-start.6 = (f32[256,128]{1,0:T(8,128)S(1)}, f32[256,128]{1,0:T(8,128)S(1)}, u32[]{:S(2)}, u32[]{:S(2)}) collective-permute-start(f32[256,128]{1,0:T(8,128)S(1)} %collective-permute-done.3.refs_7_), channel_id=1, source_target_pairs={{0,4},{1,5},{2,6},{3,7},{4,0},{5,1},{6,2},{7,3},{8,12},{9,13},{10,... | collective-permute-start | bytes 393224 | tf_op jit(solution)/shard_map/ppermute | solution.py:77
  19.0 0.0 collective-permute-done.8.refs_9_
  19.0 0.0 collective-permute-start.9
  19.0 0.0 collective-permute-done.13.refs_14_
  19.0 0.5 collective-permute-start.14
  19.5 0.7 %collective-permute-done.5.refs_4_ = f32[256,128]{1,0:T(8,128)S(1)} collective-permute-done((f32[256,128]{1,0:T(8,128)S(1)}, f32[256,128]{1,0:T(8,128)S(1)}, u32[]{:S(2)}, u32[]{:S(2)}) %collective-permute-start.5) | collective-permute-done | bytes 131104 | tf_op jit(solution)/shard_map/ppermute | solution.py:77
  20.3 0.0 collective-permute-start.11
  20.3 2.1 %collective-permute-done.4.refs_3_ = f32[256,128]{1,0:T(8,128)S(1)} collective-permute-done((f32[256,128]{1,0:T(8,128)S(1)}, f32[256,128]{1,0:T(8,128)S(1)}, u32[]{:S(2)}, u32[]{:S(2)}) %collective-permute-start.4) | collective-permute-done | bytes 131104 | tf_op jit(solution)/shard_map/ppermute | solution.py:77
  22.3 0.0 collective-permute-start.10
  22.3 1.0 %collective-permute-done.6.refs_5_ = f32[256,128]{1,0:T(8,128)S(1)} collective-permute-done((f32[256,128]{1,0:T(8,128)S(1)}, f32[256,128]{1,0:T(8,128)S(1)}, u32[]{:S(2)}, u32[]{:S(2)}) %collective-permute-start.6) | collective-permute-done | bytes 131104 | tf_op jit(solution)/shard_map/ppermute | solution.py:77
  23.4 0.0 collective-permute-start.12
  23.4 0.0 collective-permute-done.11.refs_12_
  23.4 0.0 collective-permute-done.9.refs_10_
  23.4 0.0 collective-permute-done.14.refs_15_
  23.4 0.3 collective-permute-done.10.refs_11_
  23.7 1.0 %collective-permute-done.12.refs_13_ = f32[256,128]{1,0:T(8,128)S(1)} collective-permute-done((f32[256,128]{1,0:T(8,128)S(1)}, f32[256,128]{1,0:T(8,128)S(1)}, u32[]{:S(2)}, u32[]{:S(2)}) %collective-permute-start.12) | collective-permute-done | bytes 131104 | tf_op jit(solution)/shard_map/ppermute | solution.py:77
  24.7 0.0 copy-done.4
  24.7 0.0 copy-done.3
  24.7 0.0 copy-done.2
  24.8 0.0 copy-done.1
  24.8 7.4 %exchange.1 = (f32[2,256,128]{2,1,0:T(8,128)S(1)}, f32[2,256,128]{2,1,0:T(8,128)S(1)}, f32[2,256,128]{2,1,0:T(8,128)S(1)}, f32[2,256,128]{2,1,0:T(8,128)S(1)}, f...) custom-call(s32[32]{0:T(128)S(1)} %bitcast.31, ...), custom_call_target="tpu_custom_call" | custom-call | tf_op jit(solution)/shard_map/exchange/pallas_call | solution.py:182
  32.2 0.2 collective-permute-start.17
  32.4 0.4 collective-permute-start.21
  32.8 0.1 collective-permute-start.15
  32.9 0.4 collective-permute-start.16
  33.3 0.5 collective-permute-done.17
  33.9 0.7 %collective-permute-start.18 = (f32[256,128]{1,0:T(8,128)S(1)}, f32[256,128]{1,0:T(8,128)S(1)}, u32[]{:S(2)}, u32[]{:S(2)}) collective-permute-start(f32[256,128]{1,0:T(8,128)S(1)} %get-tuple-element.39), channel_id=1, source_target_pairs={{0,4},{1,5},{2,6},{3,7},{4,0},{5,1},{6,2},{7,3},{8,12},{9,13},{10,... | collective-permute-start | bytes 393224 | tf_op jit(solution)/shard_map/ppermute | solution.py:77
  34.5 0.0 collective-permute-done.21
  34.6 1.1 %collective-permute-start.22 = (f32[256,128]{1,0:T(8,128)S(1)}, f32[256,128]{1,0:T(8,128)S(1)}, u32[]{:S(2)}, u32[]{:S(2)}) collective-permute-start(f32[256,128]{1,0:T(8,128)S(1)} %slice_bitcast_fusion.1), channel_id=1, source_target_pairs={{0,2},{1,3},{2,0},{3,1},{4,6},{5,7},{6,4},{7,5},{8,10},{9,11},{10,... | collective-permute-start | bytes 393224 | tf_op jit(solution)/shard_map/ppermute | solution.py:77
  35.7 0.0 collective-permute-done.15
  35.8 0.0 collective-permute-done.16
  35.8 3.6 %collective-permute-done.18 = f32[256,128]{1,0:T(8,128)S(1)} collective-permute-done((f32[256,128]{1,0:T(8,128)S(1)}, f32[256,128]{1,0:T(8,128)S(1)}, u32[]{:S(2)}, u32[]{:S(2)}) %collective-permute-start.18) | collective-permute-done | bytes 131104 | tf_op jit(solution)/shard_map/ppermute | solution.py:77
  39.5 1.1 %collective-permute-start.19 = (f32[256,128]{1,0:T(8,128)S(1)}, f32[256,128]{1,0:T(8,128)S(1)}, u32[]{:S(2)}, u32[]{:S(2)}) collective-permute-start(f32[256,128]{1,0:T(8,128)S(1)} %fusion.3), channel_id=1, source_target_pairs={{0,2},{1,3},{2,0},{3,1},{4,6},{5,7},{6,4},{7,5},{8,10},{9,11},{10,... | collective-permute-start | bytes 393224 | tf_op jit(solution)/shard_map/ppermute | solution.py:77
  40.5 0.7 %collective-permute-start.24 = (f32[256,128]{1,0:T(8,128)S(1)}, f32[256,128]{1,0:T(8,128)S(1)}, u32[]{:S(2)}, u32[]{:S(2)}) collective-permute-start(f32[256,128]{1,0:T(8,128)S(1)} %get-tuple-element.37), channel_id=1, source_target_pairs={{0,4},{1,5},{2,6},{3,7},{4,0},{5,1},{6,2},{7,3},{8,12},{9,13},{10,... | collective-permute-start | bytes 393224 | tf_op jit(solution)/shard_map/ppermute | solution.py:77
  41.2 0.0 collective-permute-done.22
  41.2 1.4 %collective-permute-start.23 = (f32[256,128]{1,0:T(8,128)S(1)}, f32[256,128]{1,0:T(8,128)S(1)}, u32[]{:S(2)}, u32[]{:S(2)}) collective-permute-start(f32[256,128]{1,0:T(8,128)S(1)} %fusion.2), channel_id=1, source_target_pairs={{0,4},{1,5},{2,6},{3,7},{4,0},{5,1},{6,2},{7,3},{8,12},{9,13},{10,... | collective-permute-start | bytes 393224 | tf_op jit(solution)/shard_map/ppermute | solution.py:77
  42.6 1.9 %collective-permute-done.19 = f32[256,128]{1,0:T(8,128)S(1)} collective-permute-done((f32[256,128]{1,0:T(8,128)S(1)}, f32[256,128]{1,0:T(8,128)S(1)}, u32[]{:S(2)}, u32[]{:S(2)}) %collective-permute-start.19) | collective-permute-done | bytes 131104 | tf_op jit(solution)/shard_map/ppermute | solution.py:77
  44.5 1.0 %collective-permute-start.20 = (f32[256,128]{1,0:T(8,128)S(1)}, f32[256,128]{1,0:T(8,128)S(1)}, u32[]{:S(2)}, u32[]{:S(2)}) collective-permute-start(f32[256,128]{1,0:T(8,128)S(1)} %slice_bitcast_fusion.6), channel_id=1, source_target_pairs={{0,2},{1,3},{2,0},{3,1},{4,6},{5,7},{6,4},{7,5},{8,10},{9,11},{10,... | collective-permute-start | bytes 393224 | tf_op jit(solution)/shard_map/ppermute | solution.py:77
  45.5 0.9 %collective-permute-done.24 = f32[256,128]{1,0:T(8,128)S(1)} collective-permute-done((f32[256,128]{1,0:T(8,128)S(1)}, f32[256,128]{1,0:T(8,128)S(1)}, u32[]{:S(2)}, u32[]{:S(2)}) %collective-permute-start.24) | collective-permute-done | bytes 131104 | tf_op jit(solution)/shard_map/ppermute | solution.py:77
  46.4 1.4 %collective-permute-start.25 = (f32[256,128]{1,0:T(8,128)S(1)}, f32[256,128]{1,0:T(8,128)S(1)}, u32[]{:S(2)}, u32[]{:S(2)}) collective-permute-start(f32[256,128]{1,0:T(8,128)S(1)} %fusion.1), channel_id=1, source_target_pairs={{0,12},{1,13},{2,14},{3,15},{4,8},{5,9},{6,10},{7,11},{8,4},{9,5},... | collective-permute-start | bytes 393224 | tf_op jit(solution)/shard_map/ppermute | solution.py:77
  47.8 0.0 collective-permute-done.23
  47.8 1.7 %collective-permute-done.20 = f32[256,128]{1,0:T(8,128)S(1)} collective-permute-done((f32[256,128]{1,0:T(8,128)S(1)}, f32[256,128]{1,0:T(8,128)S(1)}, u32[]{:S(2)}, u32[]{:S(2)}) %collective-permute-start.20) | collective-permute-done | bytes 131104 | tf_op jit(solution)/shard_map/ppermute | solution.py:77
  49.5 3.7 %collective-permute-done.25 = f32[256,128]{1,0:T(8,128)S(1)} collective-permute-done((f32[256,128]{1,0:T(8,128)S(1)}, f32[256,128]{1,0:T(8,128)S(1)}, u32[]{:S(2)}, u32[]{:S(2)}) %collective-permute-start.25) | collective-permute-done | bytes 131104 | tf_op jit(solution)/shard_map/ppermute | solution.py:77
  53.2 0.7 %fusion.6 = f32[256,128]{1,0:T(8,128)} fusion(f32[256,128]{1,0:T(8,128)S(1)} %collective-permute-done.25, f32[256,128]{1,0:T(8,128)S(1)} %collective-permute-done.23, f32[256,128]{1,0:T(8,128)S(1)} %collective-permute-done.20, f32[2,256,128]{2,1,0:T(8,128)S(1)} %add.33), kind=kLoop, calls=%fused_computation.14 | loop fusion | flops 98304 | bytes 655360 | tf_op jit(solution)/shard_map/add | solution.py:107
  (11 shorter events, 0.3 us)
Async XLA Ops:
  0.0 13.5 %copy-start = (f32[256,128]{1,0:T(8,128)S(1)}, f32[256,128]{1,0:T(8,128)}, u32[]{:S(2)}) copy-start(f32[256,128]{1,0:T(8,128)} %refs_0_.1) | copy-start | bytes 393220
  0.0 24.7 %copy-start.4 = (s32[32]{0:T(128)S(1)}, s32[32]{0:T(128)}, u32[]{:S(2)}) copy-start(s32[32]{0:T(128)} %order_ref.1) | copy-start | bytes 388
  0.0 24.7 %copy-start.3 = (s32[32]{0:T(128)S(1)}, s32[32]{0:T(128)}, u32[]{:S(2)}) copy-start(s32[32]{0:T(128)} %cols_ref.1) | copy-start | bytes 388
  0.0 24.7 %copy-start.2 = (s32[32]{0:T(128)S(1)}, s32[32]{0:T(128)}, u32[]{:S(2)}) copy-start(s32[32]{0:T(128)} %sub_ref.1) | copy-start | bytes 388
  0.0 24.7 %copy-start.1 = (s32[32,1]{0,1:T(1,128)S(1)}, s32[32,1]{0,1:T(1,128)}, u32[]{:S(2)}) copy-start(s32[32,1]{0,1:T(1,128)} %param.7) | copy-start | bytes 388
  0.0 12.3 %collective-permute-start.1 = (f32[256,128]{1,0:T(8,128)}, f32[256,128]{1,0:T(8,128)S(1)}, u32[]{:S(2)}, u32[]{:S(2)}) collective-permute-start(f32[256,128]{1,0:T(8,128)} %refs_0_.1), channel_id=1, source_target_pairs={{0,4},{1,5},{2,6},{3,7},{4,0},{5,1},{6,2},{7,3},{8,12},{9,13},{10,... | collective-permute-start | bytes 393224 | tf_op jit(solution)/shard_map/ppermute | solution.py:77
  3.1 9.2 %collective-permute-start = (f32[256,128]{1,0:T(8,128)}, f32[256,128]{1,0:T(8,128)S(1)}, u32[]{:S(2)}, u32[]{:S(2)}) collective-permute-start(f32[256,128]{1,0:T(8,128)} %refs_0_.1), channel_id=1, source_target_pairs={{0,12},{1,13},{2,14},{3,15},{4,8},{5,9},{6,10},{7,11},{8,4},{9,5},... | collective-permute-start | bytes 393224 | tf_op jit(solution)/shard_map/ppermute | solution.py:77
  5.6 9.0 %collective-permute-start.2 = (f32[256,128]{1,0:T(8,128)}, f32[256,128]{1,0:T(8,128)S(1)}, u32[]{:S(2)}, u32[]{:S(2)}) collective-permute-start(f32[256,128]{1,0:T(8,128)} %refs_0_.1), channel_id=1, source_target_pairs={{0,2},{1,3},{2,0},{3,1},{4,6},{5,7},{6,4},{7,5},{8,10},{9,11},{10,... | collective-permute-start | bytes 393224 | tf_op jit(solution)/shard_map/ppermute | solution.py:77
  12.3 5.0 %collective-permute-start.3 = (f32[256,128]{1,0:T(8,128)S(1)}, f32[256,128]{1,0:T(8,128)S(1)}, u32[]{:S(2)}, u32[]{:S(2)}) collective-permute-start(f32[256,128]{1,0:T(8,128)S(1)} %collective-permute-done.refs_6_), channel_id=1, source_target_pairs={{0,2},{1,3},{2,0},{3,1},{4,6},{5,7},{6,4},{7,5},{8,10},{9,11},{10,... | collective-permute-start | bytes 393224 | tf_op jit(solution)/shard_map/ppermute | solution.py:77
  13.5 5.0 %collective-permute-start.7 = (f32[256,128]{1,0:T(8,128)S(1)}, f32[256,128]{1,0:T(8,128)S(1)}, u32[]{:S(2)}, u32[]{:S(2)}) collective-permute-start(f32[256,128]{1,0:T(8,128)S(1)} %copy-done), channel_id=1, source_target_pairs={{0,1},{1,0},{2,3},{3,2},{4,5},{5,4},{6,7},{7,6},{8,9},{9,8},{10,11... | collective-permute-start | bytes 393224 | tf_op jit(solution)/shard_map/ppermute | solution.py:77
  13.5 5.6 %collective-permute-start.13 = (f32[256,128]{1,0:T(8,128)S(1)}, f32[256,128]{1,0:T(8,128)S(1)}, u32[]{:S(2)}, u32[]{:S(2)}) collective-permute-start(f32[256,128]{1,0:T(8,128)S(1)} %collective-permute-done.refs_6_), channel_id=1, source_target_pairs={{0,1},{1,0},{2,3},{3,2},{4,5},{5,4},{6,7},{7,6},{8,9},{9,8},{10,11... | collective-permute-start | bytes 393224 | tf_op jit(solution)/shard_map/ppermute | solution.py:77
  14.0 6.3 %collective-permute-start.5 = (f32[256,128]{1,0:T(8,128)S(1)}, f32[256,128]{1,0:T(8,128)S(1)}, u32[]{:S(2)}, u32[]{:S(2)}) collective-permute-start(f32[256,128]{1,0:T(8,128)S(1)} %collective-permute-done.refs_6_), channel_id=1, source_target_pairs={{0,4},{1,5},{2,6},{3,7},{4,0},{5,1},{6,2},{7,3},{8,12},{9,13},{10,... | collective-permute-start | bytes 393224 | tf_op jit(solution)/shard_map/ppermute | solution.py:77
  14.6 4.5 %collective-permute-start.8 = (f32[256,128]{1,0:T(8,128)S(1)}, f32[256,128]{1,0:T(8,128)S(1)}, u32[]{:S(2)}, u32[]{:S(2)}) collective-permute-start(f32[256,128]{1,0:T(8,128)S(1)} %collective-permute-done.2.refs_1_), channel_id=1, source_target_pairs={{0,1},{1,0},{2,3},{3,2},{4,5},{5,4},{6,7},{7,6},{8,9},{9,8},{10,11... | collective-permute-start | bytes 393224 | tf_op jit(solution)/shard_map/ppermute | solution.py:77
  17.4 5.0 %collective-permute-start.4 = (f32[256,128]{1,0:T(8,128)S(1)}, f32[256,128]{1,0:T(8,128)S(1)}, u32[]{:S(2)}, u32[]{:S(2)}) collective-permute-start(f32[256,128]{1,0:T(8,128)S(1)} %collective-permute-done.1.refs_2_), channel_id=1, source_target_pairs={{0,2},{1,3},{2,0},{3,1},{4,6},{5,7},{6,4},{7,5},{8,10},{9,11},{10,... | collective-permute-start | bytes 393224 | tf_op jit(solution)/shard_map/ppermute | solution.py:77
  18.4 5.0 %collective-permute-start.6 = (f32[256,128]{1,0:T(8,128)S(1)}, f32[256,128]{1,0:T(8,128)S(1)}, u32[]{:S(2)}, u32[]{:S(2)}) collective-permute-start(f32[256,128]{1,0:T(8,128)S(1)} %collective-permute-done.3.refs_7_), channel_id=1, source_target_pairs={{0,4},{1,5},{2,6},{3,7},{4,0},{5,1},{6,2},{7,3},{8,12},{9,13},{10,... | collective-permute-start | bytes 393224 | tf_op jit(solution)/shard_map/ppermute | solution.py:77
  19.0 4.4 %collective-permute-start.9 = (f32[256,128]{1,0:T(8,128)S(1)}, f32[256,128]{1,0:T(8,128)S(1)}, u32[]{:S(2)}, u32[]{:S(2)}) collective-permute-start(f32[256,128]{1,0:T(8,128)S(1)} %collective-permute-done.1.refs_2_), channel_id=1, source_target_pairs={{0,1},{1,0},{2,3},{3,2},{4,5},{5,4},{6,7},{7,6},{8,9},{9,8},{10,11... | collective-permute-start | bytes 393224 | tf_op jit(solution)/shard_map/ppermute | solution.py:77
  19.0 4.4 %collective-permute-start.14 = (f32[256,128]{1,0:T(8,128)S(1)}, f32[256,128]{1,0:T(8,128)S(1)}, u32[]{:S(2)}, u32[]{:S(2)}) collective-permute-start(f32[256,128]{1,0:T(8,128)S(1)} %collective-permute-done.3.refs_7_), channel_id=1, source_target_pairs={{0,1},{1,0},{2,3},{3,2},{4,5},{5,4},{6,7},{7,6},{8,9},{9,8},{10,11... | collective-permute-start | bytes 393224 | tf_op jit(solution)/shard_map/ppermute | solution.py:77
  20.3 3.1 %collective-permute-start.11 = (f32[256,128]{1,0:T(8,128)S(1)}, f32[256,128]{1,0:T(8,128)S(1)}, u32[]{:S(2)}, u32[]{:S(2)}) collective-permute-start(f32[256,128]{1,0:T(8,128)S(1)} %collective-permute-done.5.refs_4_), channel_id=1, source_target_pairs={{0,1},{1,0},{2,3},{3,2},{4,5},{5,4},{6,7},{7,6},{8,9},{9,8},{10,11... | collective-permute-start | bytes 393224 | tf_op jit(solution)/shard_map/ppermute | solution.py:77
  22.3 1.3 %collective-permute-start.10 = (f32[256,128]{1,0:T(8,128)S(1)}, f32[256,128]{1,0:T(8,128)S(1)}, u32[]{:S(2)}, u32[]{:S(2)}) collective-permute-start(f32[256,128]{1,0:T(8,128)S(1)} %collective-permute-done.4.refs_3_), channel_id=1, source_target_pairs={{0,1},{1,0},{2,3},{3,2},{4,5},{5,4},{6,7},{7,6},{8,9},{9,8},{10,11... | collective-permute-start | bytes 393224 | tf_op jit(solution)/shard_map/ppermute | solution.py:77
  23.4 1.3 %collective-permute-start.12 = (f32[256,128]{1,0:T(8,128)S(1)}, f32[256,128]{1,0:T(8,128)S(1)}, u32[]{:S(2)}, u32[]{:S(2)}) collective-permute-start(f32[256,128]{1,0:T(8,128)S(1)} %collective-permute-done.6.refs_5_), channel_id=1, source_target_pairs={{0,1},{1,0},{2,3},{3,2},{4,5},{5,4},{6,7},{7,6},{8,9},{9,8},{10,11... | collective-permute-start | bytes 393224 | tf_op jit(solution)/shard_map/ppermute | solution.py:77
  32.2 1.6 %collective-permute-start.17 = (f32[2,256,128]{2,1,0:T(8,128)S(1)}, f32[2,256,128]{2,1,0:T(8,128)S(1)}, u32[]{:S(2)}, u32[]{:S(2)}) collective-permute-start(f32[2,256,128]{2,1,0:T(8,128)S(1)} %get-tuple-element.32), channel_id=1, source_target_pairs={{0,1},{1,0},{2,3},{3,2},{4,5},{5,4},{6,7},{7,6},{8,9},{9,8},{10,11... | collective-permute-start | bytes 786440 | tf_op jit(solution)/shard_map/ppermute | solution.py:77
  32.4 2.1 %collective-permute-start.21 = (f32[2,256,128]{2,1,0:T(8,128)S(1)}, f32[2,256,128]{2,1,0:T(8,128)S(1)}, u32[]{:S(2)}, u32[]{:S(2)}) collective-permute-start(f32[2,256,128]{2,1,0:T(8,128)S(1)} %get-tuple-element.36), channel_id=1, source_target_pairs={{0,1},{1,0},{2,3},{3,2},{4,5},{5,4},{6,7},{7,6},{8,9},{9,8},{10,11... | collective-permute-start | bytes 786440 | tf_op jit(solution)/shard_map/ppermute | solution.py:77
  32.8 3.0 %collective-permute-start.15 = (f32[2,256,128]{2,1,0:T(8,128)S(1)}, f32[2,256,128]{2,1,0:T(8,128)S(1)}, u32[]{:S(2)}, u32[]{:S(2)}) collective-permute-start(f32[2,256,128]{2,1,0:T(8,128)S(1)} %get-tuple-element.28), channel_id=1, source_target_pairs={{0,1},{1,0},{2,3},{3,2},{4,5},{5,4},{6,7},{7,6},{8,9},{9,8},{10,11... | collective-permute-start | bytes 786440 | tf_op jit(solution)/shard_map/ppermute | solution.py:77
  32.9 2.9 %collective-permute-start.16 = (f32[2,256,128]{2,1,0:T(8,128)S(1)}, f32[2,256,128]{2,1,0:T(8,128)S(1)}, u32[]{:S(2)}, u32[]{:S(2)}) collective-permute-start(f32[2,256,128]{2,1,0:T(8,128)S(1)} %get-tuple-element.30), channel_id=1, source_target_pairs={{0,1},{1,0},{2,3},{3,2},{4,5},{5,4},{6,7},{7,6},{8,9},{9,8},{10,11... | collective-permute-start | bytes 786440 | tf_op jit(solution)/shard_map/ppermute | solution.py:77
  33.9 5.6 %collective-permute-start.18 = (f32[256,128]{1,0:T(8,128)S(1)}, f32[256,128]{1,0:T(8,128)S(1)}, u32[]{:S(2)}, u32[]{:S(2)}) collective-permute-start(f32[256,128]{1,0:T(8,128)S(1)} %get-tuple-element.39), channel_id=1, source_target_pairs={{0,4},{1,5},{2,6},{3,7},{4,0},{5,1},{6,2},{7,3},{8,12},{9,13},{10,... | collective-permute-start | bytes 393224 | tf_op jit(solution)/shard_map/ppermute | solution.py:77
  34.6 6.6 %collective-permute-start.22 = (f32[256,128]{1,0:T(8,128)S(1)}, f32[256,128]{1,0:T(8,128)S(1)}, u32[]{:S(2)}, u32[]{:S(2)}) collective-permute-start(f32[256,128]{1,0:T(8,128)S(1)} %slice_bitcast_fusion.1), channel_id=1, source_target_pairs={{0,2},{1,3},{2,0},{3,1},{4,6},{5,7},{6,4},{7,5},{8,10},{9,11},{10,... | collective-permute-start | bytes 393224 | tf_op jit(solution)/shard_map/ppermute | solution.py:77
  39.5 5.0 %collective-permute-start.19 = (f32[256,128]{1,0:T(8,128)S(1)}, f32[256,128]{1,0:T(8,128)S(1)}, u32[]{:S(2)}, u32[]{:S(2)}) collective-permute-start(f32[256,128]{1,0:T(8,128)S(1)} %fusion.3), channel_id=1, source_target_pairs={{0,2},{1,3},{2,0},{3,1},{4,6},{5,7},{6,4},{7,5},{8,10},{9,11},{10,... | collective-permute-start | bytes 393224 | tf_op jit(solution)/shard_map/ppermute | solution.py:77
  40.5 5.8 %collective-permute-start.24 = (f32[256,128]{1,0:T(8,128)S(1)}, f32[256,128]{1,0:T(8,128)S(1)}, u32[]{:S(2)}, u32[]{:S(2)}) collective-permute-start(f32[256,128]{1,0:T(8,128)S(1)} %get-tuple-element.37), channel_id=1, source_target_pairs={{0,4},{1,5},{2,6},{3,7},{4,0},{5,1},{6,2},{7,3},{8,12},{9,13},{10,... | collective-permute-start | bytes 393224 | tf_op jit(solution)/shard_map/ppermute | solution.py:77
  41.2 6.6 %collective-permute-start.23 = (f32[256,128]{1,0:T(8,128)S(1)}, f32[256,128]{1,0:T(8,128)S(1)}, u32[]{:S(2)}, u32[]{:S(2)}) collective-permute-start(f32[256,128]{1,0:T(8,128)S(1)} %fusion.2), channel_id=1, source_target_pairs={{0,4},{1,5},{2,6},{3,7},{4,0},{5,1},{6,2},{7,3},{8,12},{9,13},{10,... | collective-permute-start | bytes 393224 | tf_op jit(solution)/shard_map/ppermute | solution.py:77
  44.5 5.0 %collective-permute-start.20 = (f32[256,128]{1,0:T(8,128)S(1)}, f32[256,128]{1,0:T(8,128)S(1)}, u32[]{:S(2)}, u32[]{:S(2)}) collective-permute-start(f32[256,128]{1,0:T(8,128)S(1)} %slice_bitcast_fusion.6), channel_id=1, source_target_pairs={{0,2},{1,3},{2,0},{3,1},{4,6},{5,7},{6,4},{7,5},{8,10},{9,11},{10,... | collective-permute-start | bytes 393224 | tf_op jit(solution)/shard_map/ppermute | solution.py:77
  46.4 6.8 %collective-permute-start.25 = (f32[256,128]{1,0:T(8,128)S(1)}, f32[256,128]{1,0:T(8,128)S(1)}, u32[]{:S(2)}, u32[]{:S(2)}) collective-permute-start(f32[256,128]{1,0:T(8,128)S(1)} %fusion.1), channel_id=1, source_target_pairs={{0,12},{1,13},{2,14},{3,15},{4,8},{5,9},{6,10},{7,11},{8,4},{9,5},... | collective-permute-start | bytes 393224 | tf_op jit(solution)/shard_map/ppermute | solution.py:77

commit v5 on v4

--- a/solution.py
+++ b/solution.py
@@ -78,19 +78,21 @@
 
 
 def gather_shards(grid, x, beside):
-    held = {(0, 0, 0): x}
-    held[3, 0, 0] = grid.shift(x, (3, 0, 0))
-    held[1, 0, 0] = grid.shift(x, (1, 0, 0))
-    held[0, 1, 0] = grid.shift(x, (0, 1, 0))
-    held[3, 0, 0], (beside, held[1, 0, 0]) = tie(held[3, 0, 0], beside, held[1, 0, 0])
-    held[3, 1, 0] = grid.shift(held[3, 0, 0], (0, 1, 0))
-    held[2, 0, 0] = grid.shift(held[3, 0, 0], (1, 0, 0))
-    held[3, 1, 0], (held[1, 0, 0],) = tie(held[3, 1, 0], held[1, 0, 0])
-    held[2, 1, 0] = grid.shift(held[3, 1, 0], (1, 0, 0))
-    held[1, 1, 0] = grid.shift(held[1, 0, 0], (0, 1, 0))
-    for k, j, _ in list(held):
-        held[k, j, 1] = grid.shift(held[k, j, 0], (0, 0, 1))
-    return [held[o] for o in grid.offsets], beside
+    held = {(0, 0): x}
+    held[3, 0] = grid.shift(x, (3, 0, 0))
+    held[1, 0] = grid.shift(x, (1, 0, 0))
+    held[0, 1] = grid.shift(x, (0, 1, 0))
+    held[3, 0], (beside, held[1, 0], held[0, 1]) = tie(held[3, 0], beside, held[1, 0], held[0, 1])
+
+    held[3, 1] = grid.shift(held[3, 0], (0, 1, 0))
+    both = grid.shift(jnp.concatenate([held[3, 0], held[0, 1]], axis=0), (1, 0, 0))
+    held[2, 1] = grid.shift(held[3, 1], (1, 0, 0))
+    groups = {(o,): a for o, a in held.items()}
+    groups[(2, 0), (1, 1)] = both
+
+    packs = [[o + (0,) for o in key] for key in groups] + [[o + (1,) for o in key] for key in groups]
+    arrays = list(groups.values())
+    return packs, arrays + [grid.shift(a, (0, 0, 1)) for a in arrays], beside
 
 
 def scatter_sums(grid, parts):
@@ -107,17 +109,18 @@
     return own + grid.shift(near, (1, 0, 0)) + grid.shift(mirror, (3, 0, 0))
 
 
-def exchange_kernel(grid, per_owner, owner_ref, sub_ref, cols_ref, order_ref, split_ref, *refs):
+def exchange_kernel(grid, per_owner, packs, owner_ref, sub_ref, cols_ref, order_ref, split_ref, *refs):
     n_tiles, rows, pair = split_ref.shape
     block = pair // 2
     aux_dev = rows // block
-    n_shards = len(grid.offsets) if grid else 1
-    shards, refs = refs[:n_shards], refs[n_shards:]
+    shards, refs = refs[: len(packs)], refs[len(packs) :]
     *outs, coeff, wide, fitted, weights, summed = refs
     me = lax.axis_index("aux")
     if grid:
-        for ref, offset in zip(shards, grid.offsets):
-            coeff[pl.ds(grid.other(me, offset) * per_owner, per_owner)] = ref[...].reshape(per_owner, block, -1)
+        for ref, offsets in zip(shards, packs):
+            for i, offset in enumerate(offsets):
+                shard = ref[i * per_owner * block : (i + 1) * per_owner * block]
+                coeff[pl.ds(grid.other(me, offset) * per_owner, per_owner)] = shard.reshape(per_owner, block, -1)
     else:
         coeff[...] = shards[0][...].reshape(coeff.shape)
 
@@ -167,7 +170,7 @@
         outs[0][...] = summed[...].reshape(outs[0].shape)
 
 
-def exchange(grid, tile_owner, tile_sub, tile_cols, row_order, split, shards):
+def exchange(grid, tile_owner, tile_sub, tile_cols, row_order, split, packs, shards):
     n_tiles, rows, pair = split.shape
     block, width = pair // 2, shards[0].shape[1]
     aux_dev = rows // block
@@ -180,7 +183,7 @@
     else:
         out_shape = [jax.ShapeDtypeStruct((n_blocks * block, width), F32)]
     return pl.pallas_call(
-        functools.partial(exchange_kernel, grid, per_owner),
+        functools.partial(exchange_kernel, grid, per_owner, packs),
         out_shape=out_shape,
         in_specs=[smem] * 4 + [vmem] * (1 + len(shards)),
         out_specs=[vmem] * len(out_shape),
@@ -201,11 +204,11 @@
     grid = Grid(n_aux) if n_aux == 16 else None
     split = prepare(tiles)
     if grid:
-        shards, split = gather_shards(grid, orbitals, split)
-    else:
-        shards = [lax.all_gather(orbitals, "aux", axis=0, tiled=True)]
+        packs, shards, split = gather_shards(grid, orbitals, split)
+    else:
+        packs, shards = [()], [lax.all_gather(orbitals, "aux", axis=0, tiled=True)]
     split = pltpu.with_memory_space_constraint(split, pltpu.VMEM)
-    outs = exchange(grid, tile_owner, tile_sub, tile_cols, row_order, split, shards)
+    outs = exchange(grid, tile_owner, tile_sub, tile_cols, row_order, split, packs, shards)
     if not grid:
         return lax.psum_scatter(outs[0], "aux", scatter_dimension=0, tiled=True)
     return scatter_sums(grid, [outs[: grid.z], outs[grid.z :]])

time: 54.1 us -> 54.2 us (level)
    ppermute x26 -> x24, starting transfers between devices: 19.9 us -> 20.2 us  [shift(): lax.ppermute(x, 'aux', [(i, self.other(i, offset)) for i in range(self.z...]
    ppermute x26 -> x24, waiting for transfers between devices: 20.3 us -> 20.1 us  [shift(): lax.ppermute(x, 'aux', [(i, self.other(i, offset)) for i in range(self.z...]
  transfers between devices with their start and end apart: 26 -> 24, of which waited for: 12 -> 11; matrix products, arithmetic and copies ran while one was open for 0% -> 0% of each run, Pallas kernels for 10% -> 10%
where the time goes in v5:
time: 54.2 us; the launch traced here: 54 us
  starting transfers between devices  20.2 us (37%)
  waiting for transfers between devices  20.1 us (37%)
  Pallas kernels  12.6 us (23%)
  other arithmetic  0.9 us (2%)
    ppermute x24, starting transfers between devices, shift(): lax.ppermute(x, 'aux', [(i, self.other(i, offset)) for i in range(self.z...  20.2 us
    ppermute x24, waiting for transfers between devices, shift(): lax.ppermute(x, 'aux', [(i, self.other(i, offset)) for i in range(self.z...  20.1 us
    pallas_call x1, Pallas kernels, exchange(): pl.pallas_call(functools.partial(exchange_kernel, grid, per_owner, packs)...  7.42 us
    pallas_call x1, Pallas kernels, prepare(): pl.pallas_call(prepare_kernel, out_shape=pltpu.VMEM((n_tiles, aux_dev * b...  5.2 us
  transfers between devices with their start and end apart: 24, of which 11 were waited for; matrix products, arithmetic and copies ran while one was open for 0% of the time, Pallas kernels for 10%

profile of v5, /device:TPU:0, one launch (start us, length us, event | category | flops | bytes accessed | tf_op | source)
XLA Modules:
  0.0 54.0 jit_solution(6022386404060498148)
XLA Ops:
  0.0 0.0 copy-start
  0.0 0.0 copy-start.4
  0.0 0.0 copy-start.3
  0.0 0.0 copy-start.2
  0.0 0.0 copy-start.1
  0.0 3.0 %collective-permute-start.2 = (f32[256,128]{1,0:T(8,128)}, f32[256,128]{1,0:T(8,128)S(1)}, u32[]{:S(2)}, u32[]{:S(2)}) collective-permute-start(f32[256,128]{1,0:T(8,128)} %refs_0_.1), channel_id=1, source_target_pairs={{0,2},{1,3},{2,0},{3,1},{4,6},{5,7},{6,4},{7,5},{8,10},{9,11},{10,... | collective-permute-start | bytes 393224 | tf_op jit(solution)/shard_map/ppermute | solution.py:77
  3.1 1.6 %collective-permute-start.1 = (f32[256,128]{1,0:T(8,128)}, f32[256,128]{1,0:T(8,128)S(1)}, u32[]{:S(2)}, u32[]{:S(2)}) collective-permute-start(f32[256,128]{1,0:T(8,128)} %refs_0_.1), channel_id=1, source_target_pairs={{0,4},{1,5},{2,6},{3,7},{4,0},{5,1},{6,2},{7,3},{8,12},{9,13},{10,... | collective-permute-start | bytes 393224 | tf_op jit(solution)/shard_map/ppermute | solution.py:77
  4.6 2.5 %collective-permute-start = (f32[256,128]{1,0:T(8,128)}, f32[256,128]{1,0:T(8,128)S(1)}, u32[]{:S(2)}, u32[]{:S(2)}) collective-permute-start(f32[256,128]{1,0:T(8,128)} %refs_0_.1), channel_id=1, source_target_pairs={{0,12},{1,13},{2,14},{3,15},{4,8},{5,9},{6,10},{7,11},{8,4},{9,5},... | collective-permute-start | bytes 393224 | tf_op jit(solution)/shard_map/ppermute | solution.py:77
  7.1 5.2 %prepare.1.split_ref = bf16[32,512,256]{2,1,0:T(8,128)(2,1)S(1)} custom-call(f32[32,4,128,128]{3,2,1,0:T(8,128)} %tiles_ref.1), custom_call_target="tpu_custom_call" | custom-call | flops 12582912 | bytes 16777216 | tf_op jit(solution)/shard_map/prepare/pallas_call | solution.py:46
  12.3 0.0 collective-permute-done.2.refs_3_
  12.3 0.0 collective-permute-done.1.refs_2_
  12.3 0.8 %collective-permute-done.refs_1_ = f32[256,128]{1,0:T(8,128)S(1)} collective-permute-done((f32[256,128]{1,0:T(8,128)}, f32[256,128]{1,0:T(8,128)S(1)}, u32[]{:S(2)}, u32[]{:S(2)}) %collective-permute-start) | collective-permute-done | bytes 131104 | tf_op jit(solution)/shard_map/ppermute | solution.py:77
  13.1 0.7 %collective-permute-start.5 = (f32[512,128]{1,0:T(8,128)S(1)}, f32[512,128]{1,0:T(8,128)S(1)}, u32[]{:S(2)}, u32[]{:S(2)}) collective-permute-start(f32[512,128]{1,0:T(8,128)S(1)} %pad_maximum_fusion), channel_id=1, source_target_pairs={{0,4},{1,5},{2,6},{3,7},{4,0},{5,1},{6,2},{7,3},{8,12},{9,13},{10,... | collective-permute-start | bytes 786440 | tf_op jit(solution)/shard_map/ppermute | solution.py:77
  13.9 0.5 collective-permute-start.3
  14.4 0.0 copy-done
  14.4 0.0 collective-permute-start.6
  14.4 0.5 collective-permute-start.8
  14.9 3.9 %collective-permute-done.3.refs_4_ = f32[256,128]{1,0:T(8,128)S(1)} collective-permute-done((f32[256,128]{1,0:T(8,128)S(1)}, f32[256,128]{1,0:T(8,128)S(1)}, u32[]{:S(2)}, u32[]{:S(2)}) %collective-permute-start.3) | collective-permute-done | bytes 131104 | tf_op jit(solution)/shard_map/ppermute | solution.py:77
  18.8 1.4 %collective-permute-start.4 = (f32[256,128]{1,0:T(8,128)S(1)}, f32[256,128]{1,0:T(8,128)S(1)}, u32[]{:S(2)}, u32[]{:S(2)}) collective-permute-start(f32[256,128]{1,0:T(8,128)S(1)} %collective-permute-done.3.refs_4_), channel_id=1, source_target_pairs={{0,4},{1,5},{2,6},{3,7},{4,0},{5,1},{6,2},{7,3},{8,12},{9,13},{10,... | collective-permute-start | bytes 393224 | tf_op jit(solution)/shard_map/ppermute | solution.py:77
  20.2 0.9 %collective-permute-done.5.refs_6_ = f32[512,128]{1,0:T(8,128)S(1)} collective-permute-done((f32[512,128]{1,0:T(8,128)S(1)}, f32[512,128]{1,0:T(8,128)S(1)}, u32[]{:S(2)}, u32[]{:S(2)}) %collective-permute-start.5) | collective-permute-done | bytes 262176 | tf_op jit(solution)/shard_map/ppermute | solution.py:77
  21.1 0.0 collective-permute-start.12
  21.1 0.5 collective-permute-start.9
  21.6 0.0 collective-permute-done.6.refs_7_
  21.6 0.0 collective-permute-start.7
  21.6 0.0 collective-permute-done.8.refs_9_
  21.6 0.5 collective-permute-start.10
  22.1 1.7 %collective-permute-done.4.refs_5_ = f32[256,128]{1,0:T(8,128)S(1)} collective-permute-done((f32[256,128]{1,0:T(8,128)S(1)}, f32[256,128]{1,0:T(8,128)S(1)}, u32[]{:S(2)}, u32[]{:S(2)}) %collective-permute-start.4) | collective-permute-done | bytes 131104 | tf_op jit(solution)/shard_map/ppermute | solution.py:77
  23.8 0.0 collective-permute-start.11
  23.8 0.0 collective-permute-done.9.refs_10_
  23.8 0.0 collective-permute-done.7.refs_8_
  23.8 0.0 collective-permute-done.10.refs_11_
  23.8 1.3 %collective-permute-done.11.refs_12_ = f32[256,128]{1,0:T(8,128)S(1)} collective-permute-done((f32[256,128]{1,0:T(8,128)S(1)}, f32[256,128]{1,0:T(8,128)S(1)}, u32[]{:S(2)}, u32[]{:S(2)}) %collective-permute-start.11) | collective-permute-done | bytes 131104 | tf_op jit(solution)/shard_map/ppermute | solution.py:77
  25.2 0.0 collective-permute-done.12.refs_13_
  25.2 0.0 copy-done.4
  25.2 0.0 copy-done.3
  25.2 0.0 copy-done.2
  25.2 0.0 copy-done.1
  25.2 7.4 %exchange.1 = (f32[2,256,128]{2,1,0:T(8,128)S(1)}, f32[2,256,128]{2,1,0:T(8,128)S(1)}, f32[2,256,128]{2,1,0:T(8,128)S(1)}, f32[2,256,128]{2,1,0:T(8,128)S(1)}, f...) custom-call(s32[32]{0:T(128)S(1)} %bitcast.31, ...), custom_call_target="tpu_custom_call" | custom-call | tf_op jit(solution)/shard_map/exchange/pallas_call | solution.py:185
  32.6 0.2 collective-permute-start.15
  32.8 0.4 collective-permute-start.19
  33.2 0.1 collective-permute-start.13
  33.3 0.4 collective-permute-start.14
  33.7 0.5 collective-permute-done.15
  34.3 1.4 %collective-permute-start.16 = (f32[256,128]{1,0:T(8,128)S(1)}, f32[256,128]{1,0:T(8,128)S(1)}, u32[]{:S(2)}, u32[]{:S(2)}) collective-permute-start(f32[256,128]{1,0:T(8,128)S(1)} %get-tuple-element.37), channel_id=1, source_target_pairs={{0,4},{1,5},{2,6},{3,7},{4,0},{5,1},{6,2},{7,3},{8,12},{9,13},{10,... | collective-permute-start | bytes 393224 | tf_op jit(solution)/shard_map/ppermute | solution.py:77
  35.7 0.0 collective-permute-done.19
  35.8 0.6 %collective-permute-start.20 = (f32[256,128]{1,0:T(8,128)S(1)}, f32[256,128]{1,0:T(8,128)S(1)}, u32[]{:S(2)}, u32[]{:S(2)}) collective-permute-start(f32[256,128]{1,0:T(8,128)S(1)} %slice_bitcast_fusion.1), channel_id=1, source_target_pairs={{0,2},{1,3},{2,0},{3,1},{4,6},{5,7},{6,4},{7,5},{8,10},{9,11},{10,... | collective-permute-start | bytes 393224 | tf_op jit(solution)/shard_map/ppermute | solution.py:77
  36.3 0.0 collective-permute-done.13
  36.4 0.0 collective-permute-done.14
  36.4 3.4 %collective-permute-done.16 = f32[256,128]{1,0:T(8,128)S(1)} collective-permute-done((f32[256,128]{1,0:T(8,128)S(1)}, f32[256,128]{1,0:T(8,128)S(1)}, u32[]{:S(2)}, u32[]{:S(2)}) %collective-permute-start.16) | collective-permute-done | bytes 131104 | tf_op jit(solution)/shard_map/ppermute | solution.py:77
  39.9 0.6 %collective-permute-start.17 = (f32[256,128]{1,0:T(8,128)S(1)}, f32[256,128]{1,0:T(8,128)S(1)}, u32[]{:S(2)}, u32[]{:S(2)}) collective-permute-start(f32[256,128]{1,0:T(8,128)S(1)} %fusion.3), channel_id=1, source_target_pairs={{0,2},{1,3},{2,0},{3,1},{4,6},{5,7},{6,4},{7,5},{8,10},{9,11},{10,... | collective-permute-start | bytes 393224 | tf_op jit(solution)/shard_map/ppermute | solution.py:77
  40.5 1.4 %collective-permute-start.22 = (f32[256,128]{1,0:T(8,128)S(1)}, f32[256,128]{1,0:T(8,128)S(1)}, u32[]{:S(2)}, u32[]{:S(2)}) collective-permute-start(f32[256,128]{1,0:T(8,128)S(1)} %get-tuple-element.35), channel_id=1, source_target_pairs={{0,4},{1,5},{2,6},{3,7},{4,0},{5,1},{6,2},{7,3},{8,12},{9,13},{10,... | collective-permute-start | bytes 393224 | tf_op jit(solution)/shard_map/ppermute | solution.py:77
  41.8 0.0 collective-permute-done.20
  41.9 0.7 %collective-permute-start.21 = (f32[256,128]{1,0:T(8,128)S(1)}, f32[256,128]{1,0:T(8,128)S(1)}, u32[]{:S(2)}, u32[]{:S(2)}) collective-permute-start(f32[256,128]{1,0:T(8,128)S(1)} %fusion.2), channel_id=1, source_target_pairs={{0,4},{1,5},{2,6},{3,7},{4,0},{5,1},{6,2},{7,3},{8,12},{9,13},{10,... | collective-permute-start | bytes 393224 | tf_op jit(solution)/shard_map/ppermute | solution.py:77
  42.6 2.3 %collective-permute-done.17 = f32[256,128]{1,0:T(8,128)S(1)} collective-permute-done((f32[256,128]{1,0:T(8,128)S(1)}, f32[256,128]{1,0:T(8,128)S(1)}, u32[]{:S(2)}, u32[]{:S(2)}) %collective-permute-start.17) | collective-permute-done | bytes 131104 | tf_op jit(solution)/shard_map/ppermute | solution.py:77
  44.9 0.5 collective-permute-start.18
  45.4 0.9 %collective-permute-done.22 = f32[256,128]{1,0:T(8,128)S(1)} collective-permute-done((f32[256,128]{1,0:T(8,128)S(1)}, f32[256,128]{1,0:T(8,128)S(1)}, u32[]{:S(2)}, u32[]{:S(2)}) %collective-permute-start.22) | collective-permute-done | bytes 131104 | tf_op jit(solution)/shard_map/ppermute | solution.py:77
  46.3 2.7 %collective-permute-start.23 = (f32[256,128]{1,0:T(8,128)S(1)}, f32[256,128]{1,0:T(8,128)S(1)}, u32[]{:S(2)}, u32[]{:S(2)}) collective-permute-start(f32[256,128]{1,0:T(8,128)S(1)} %fusion.1), channel_id=1, source_target_pairs={{0,12},{1,13},{2,14},{3,15},{4,8},{5,9},{6,10},{7,11},{8,4},{9,5},... | collective-permute-start | bytes 393224 | tf_op jit(solution)/shard_map/ppermute | solution.py:77
  49.0 0.0 collective-permute-done.21
  49.0 0.9 %collective-permute-done.18 = f32[256,128]{1,0:T(8,128)S(1)} collective-permute-done((f32[256,128]{1,0:T(8,128)S(1)}, f32[256,128]{1,0:T(8,128)S(1)}, u32[]{:S(2)}, u32[]{:S(2)}) %collective-permute-start.18) | collective-permute-done | bytes 131104 | tf_op jit(solution)/shard_map/ppermute | solution.py:77
  49.9 3.4 %collective-permute-done.23 = f32[256,128]{1,0:T(8,128)S(1)} collective-permute-done((f32[256,128]{1,0:T(8,128)S(1)}, f32[256,128]{1,0:T(8,128)S(1)}, u32[]{:S(2)}, u32[]{:S(2)}) %collective-permute-start.23) | collective-permute-done | bytes 131104 | tf_op jit(solution)/shard_map/ppermute | solution.py:77
  53.3 0.7 %fusion.6 = f32[256,128]{1,0:T(8,128)} fusion(f32[256,128]{1,0:T(8,128)S(1)} %collective-permute-done.23, f32[256,128]{1,0:T(8,128)S(1)} %collective-permute-done.21, f32[256,128]{1,0:T(8,128)S(1)} %collective-permute-done.18, f32[2,256,128]{2,1,0:T(8,128)S(1)} %add.33), kind=kLoop, calls=%fused_computation.15 | loop fusion | flops 98304 | bytes 655360 | tf_op jit(solution)/shard_map/add | solution.py:109
  (11 shorter events, 0.2 us)
Async XLA Ops:
  0.0 14.4 %copy-start = (f32[256,128]{1,0:T(8,128)S(1)}, f32[256,128]{1,0:T(8,128)}, u32[]{:S(2)}) copy-start(f32[256,128]{1,0:T(8,128)} %refs_0_.1) | copy-start | bytes 393220
  0.0 25.2 %copy-start.4 = (s32[32]{0:T(128)S(1)}, s32[32]{0:T(128)}, u32[]{:S(2)}) copy-start(s32[32]{0:T(128)} %order_ref.1) | copy-start | bytes 388
  0.0 25.2 %copy-start.3 = (s32[32]{0:T(128)S(1)}, s32[32]{0:T(128)}, u32[]{:S(2)}) copy-start(s32[32]{0:T(128)} %cols_ref.1) | copy-start | bytes 388
  0.0 25.2 %copy-start.2 = (s32[32]{0:T(128)S(1)}, s32[32]{0:T(128)}, u32[]{:S(2)}) copy-start(s32[32]{0:T(128)} %sub_ref.1) | copy-start | bytes 388
  0.0 25.2 %copy-start.1 = (s32[32,1]{0,1:T(1,128)S(1)}, s32[32,1]{0,1:T(1,128)}, u32[]{:S(2)}) copy-start(s32[32,1]{0,1:T(1,128)} %param.7) | copy-start | bytes 388
  0.0 12.3 %collective-permute-start.2 = (f32[256,128]{1,0:T(8,128)}, f32[256,128]{1,0:T(8,128)S(1)}, u32[]{:S(2)}, u32[]{:S(2)}) collective-permute-start(f32[256,128]{1,0:T(8,128)} %refs_0_.1), channel_id=1, source_target_pairs={{0,2},{1,3},{2,0},{3,1},{4,6},{5,7},{6,4},{7,5},{8,10},{9,11},{10,... | collective-permute-start | bytes 393224 | tf_op jit(solution)/shard_map/ppermute | solution.py:77
  3.1 9.3 %collective-permute-start.1 = (f32[256,128]{1,0:T(8,128)}, f32[256,128]{1,0:T(8,128)S(1)}, u32[]{:S(2)}, u32[]{:S(2)}) collective-permute-start(f32[256,128]{1,0:T(8,128)} %refs_0_.1), channel_id=1, source_target_pairs={{0,4},{1,5},{2,6},{3,7},{4,0},{5,1},{6,2},{7,3},{8,12},{9,13},{10,... | collective-permute-start | bytes 393224 | tf_op jit(solution)/shard_map/ppermute | solution.py:77
  4.6 8.5 %collective-permute-start = (f32[256,128]{1,0:T(8,128)}, f32[256,128]{1,0:T(8,128)S(1)}, u32[]{:S(2)}, u32[]{:S(2)}) collective-permute-start(f32[256,128]{1,0:T(8,128)} %refs_0_.1), channel_id=1, source_target_pairs={{0,12},{1,13},{2,14},{3,15},{4,8},{5,9},{6,10},{7,11},{8,4},{9,5},... | collective-permute-start | bytes 393224 | tf_op jit(solution)/shard_map/ppermute | solution.py:77
  13.1 8.0 %collective-permute-start.5 = (f32[512,128]{1,0:T(8,128)S(1)}, f32[512,128]{1,0:T(8,128)S(1)}, u32[]{:S(2)}, u32[]{:S(2)}) collective-permute-start(f32[512,128]{1,0:T(8,128)S(1)} %pad_maximum_fusion), channel_id=1, source_target_pairs={{0,4},{1,5},{2,6},{3,7},{4,0},{5,1},{6,2},{7,3},{8,12},{9,13},{10,... | collective-permute-start | bytes 786440 | tf_op jit(solution)/shard_map/ppermute | solution.py:77
  13.9 5.0 %collective-permute-start.3 = (f32[256,128]{1,0:T(8,128)S(1)}, f32[256,128]{1,0:T(8,128)S(1)}, u32[]{:S(2)}, u32[]{:S(2)}) collective-permute-start(f32[256,128]{1,0:T(8,128)S(1)} %collective-permute-done.refs_1_), channel_id=1, source_target_pairs={{0,2},{1,3},{2,0},{3,1},{4,6},{5,7},{6,4},{7,5},{8,10},{9,11},{10,... | collective-permute-start | bytes 393224 | tf_op jit(solution)/shard_map/ppermute | solution.py:77
  14.4 7.2 %collective-permute-start.6 = (f32[256,128]{1,0:T(8,128)S(1)}, f32[256,128]{1,0:T(8,128)S(1)}, u32[]{:S(2)}, u32[]{:S(2)}) collective-permute-start(f32[256,128]{1,0:T(8,128)S(1)} %copy-done), channel_id=1, source_target_pairs={{0,1},{1,0},{2,3},{3,2},{4,5},{5,4},{6,7},{7,6},{8,9},{9,8},{10,11... | collective-permute-start | bytes 393224 | tf_op jit(solution)/shard_map/ppermute | solution.py:77
  14.4 7.3 %collective-permute-start.8 = (f32[256,128]{1,0:T(8,128)S(1)}, f32[256,128]{1,0:T(8,128)S(1)}, u32[]{:S(2)}, u32[]{:S(2)}) collective-permute-start(f32[256,128]{1,0:T(8,128)S(1)} %collective-permute-done.1.refs_2_), channel_id=1, source_target_pairs={{0,1},{1,0},{2,3},{3,2},{4,5},{5,4},{6,7},{7,6},{8,9},{9,8},{10,11... | collective-permute-start | bytes 393224 | tf_op jit(solution)/shard_map/ppermute | solution.py:77
  18.8 5.0 %collective-permute-start.4 = (f32[256,128]{1,0:T(8,128)S(1)}, f32[256,128]{1,0:T(8,128)S(1)}, u32[]{:S(2)}, u32[]{:S(2)}) collective-permute-start(f32[256,128]{1,0:T(8,128)S(1)} %collective-permute-done.3.refs_4_), channel_id=1, source_target_pairs={{0,4},{1,5},{2,6},{3,7},{4,0},{5,1},{6,2},{7,3},{8,12},{9,13},{10,... | collective-permute-start | bytes 393224 | tf_op jit(solution)/shard_map/ppermute | solution.py:77
  21.1 4.0 %collective-permute-start.12 = (f32[512,128]{1,0:T(8,128)S(1)}, f32[512,128]{1,0:T(8,128)S(1)}, u32[]{:S(2)}, u32[]{:S(2)}) collective-permute-start(f32[512,128]{1,0:T(8,128)S(1)} %collective-permute-done.5.refs_6_), channel_id=1, source_target_pairs={{0,1},{1,0},{2,3},{3,2},{4,5},{5,4},{6,7},{7,6},{8,9},{9,8},{10,11... | collective-permute-start | bytes 786440 | tf_op jit(solution)/shard_map/ppermute | solution.py:77
  21.1 2.7 %collective-permute-start.9 = (f32[256,128]{1,0:T(8,128)S(1)}, f32[256,128]{1,0:T(8,128)S(1)}, u32[]{:S(2)}, u32[]{:S(2)}) collective-permute-start(f32[256,128]{1,0:T(8,128)S(1)} %collective-permute-done.2.refs_3_), channel_id=1, source_target_pairs={{0,1},{1,0},{2,3},{3,2},{4,5},{5,4},{6,7},{7,6},{8,9},{9,8},{10,11... | collective-permute-start | bytes 393224 | tf_op jit(solution)/shard_map/ppermute | solution.py:77
  21.6 2.2 %collective-permute-start.7 = (f32[256,128]{1,0:T(8,128)S(1)}, f32[256,128]{1,0:T(8,128)S(1)}, u32[]{:S(2)}, u32[]{:S(2)}) collective-permute-start(f32[256,128]{1,0:T(8,128)S(1)} %collective-permute-done.refs_1_), channel_id=1, source_target_pairs={{0,1},{1,0},{2,3},{3,2},{4,5},{5,4},{6,7},{7,6},{8,9},{9,8},{10,11... | collective-permute-start | bytes 393224 | tf_op jit(solution)/shard_map/ppermute | solution.py:77
  21.6 2.2 %collective-permute-start.10 = (f32[256,128]{1,0:T(8,128)S(1)}, f32[256,128]{1,0:T(8,128)S(1)}, u32[]{:S(2)}, u32[]{:S(2)}) collective-permute-start(f32[256,128]{1,0:T(8,128)S(1)} %collective-permute-done.3.refs_4_), channel_id=1, source_target_pairs={{0,1},{1,0},{2,3},{3,2},{4,5},{5,4},{6,7},{7,6},{8,9},{9,8},{10,11... | collective-permute-start | bytes 393224 | tf_op jit(solution)/shard_map/ppermute | solution.py:77
  23.8 1.3 %collective-permute-start.11 = (f32[256,128]{1,0:T(8,128)S(1)}, f32[256,128]{1,0:T(8,128)S(1)}, u32[]{:S(2)}, u32[]{:S(2)}) collective-permute-start(f32[256,128]{1,0:T(8,128)S(1)} %collective-permute-done.4.refs_5_), channel_id=1, source_target_pairs={{0,1},{1,0},{2,3},{3,2},{4,5},{5,4},{6,7},{7,6},{8,9},{9,8},{10,11... | collective-permute-start | bytes 393224 | tf_op jit(solution)/shard_map/ppermute | solution.py:77
  32.6 1.6 %collective-permute-start.15 = (f32[2,256,128]{2,1,0:T(8,128)S(1)}, f32[2,256,128]{2,1,0:T(8,128)S(1)}, u32[]{:S(2)}, u32[]{:S(2)}) collective-permute-start(f32[2,256,128]{2,1,0:T(8,128)S(1)} %get-tuple-element.30), channel_id=1, source_target_pairs={{0,1},{1,0},{2,3},{3,2},{4,5},{5,4},{6,7},{7,6},{8,9},{9,8},{10,11... | collective-permute-start | bytes 786440 | tf_op jit(solution)/shard_map/ppermute | solution.py:77
  32.8 2.9 %collective-permute-start.19 = (f32[2,256,128]{2,1,0:T(8,128)S(1)}, f32[2,256,128]{2,1,0:T(8,128)S(1)}, u32[]{:S(2)}, u32[]{:S(2)}) collective-permute-start(f32[2,256,128]{2,1,0:T(8,128)S(1)} %get-tuple-element.34), channel_id=1, source_target_pairs={{0,1},{1,0},{2,3},{3,2},{4,5},{5,4},{6,7},{7,6},{8,9},{9,8},{10,11... | collective-permute-start | bytes 786440 | tf_op jit(solution)/shard_map/ppermute | solution.py:77
  33.2 3.2 %collective-permute-start.13 = (f32[2,256,128]{2,1,0:T(8,128)S(1)}, f32[2,256,128]{2,1,0:T(8,128)S(1)}, u32[]{:S(2)}, u32[]{:S(2)}) collective-permute-start(f32[2,256,128]{2,1,0:T(8,128)S(1)} %get-tuple-element.26), channel_id=1, source_target_pairs={{0,1},{1,0},{2,3},{3,2},{4,5},{5,4},{6,7},{7,6},{8,9},{9,8},{10,11... | collective-permute-start | bytes 786440 | tf_op jit(solution)/shard_map/ppermute | solution.py:77
  33.3 3.1 %collective-permute-start.14 = (f32[2,256,128]{2,1,0:T(8,128)S(1)}, f32[2,256,128]{2,1,0:T(8,128)S(1)}, u32[]{:S(2)}, u32[]{:S(2)}) collective-permute-start(f32[2,256,128]{2,1,0:T(8,128)S(1)} %get-tuple-element.28), channel_id=1, source_target_pairs={{0,1},{1,0},{2,3},{3,2},{4,5},{5,4},{6,7},{7,6},{8,9},{9,8},{10,11... | collective-permute-start | bytes 786440 | tf_op jit(solution)/shard_map/ppermute | solution.py:77
  34.3 5.6 %collective-permute-start.16 = (f32[256,128]{1,0:T(8,128)S(1)}, f32[256,128]{1,0:T(8,128)S(1)}, u32[]{:S(2)}, u32[]{:S(2)}) collective-permute-start(f32[256,128]{1,0:T(8,128)S(1)} %get-tuple-element.37), channel_id=1, source_target_pairs={{0,4},{1,5},{2,6},{3,7},{4,0},{5,1},{6,2},{7,3},{8,12},{9,13},{10,... | collective-permute-start | bytes 393224 | tf_op jit(solution)/shard_map/ppermute | solution.py:77
  35.8 6.1 %collective-permute-start.20 = (f32[256,128]{1,0:T(8,128)S(1)}, f32[256,128]{1,0:T(8,128)S(1)}, u32[]{:S(2)}, u32[]{:S(2)}) collective-permute-start(f32[256,128]{1,0:T(8,128)S(1)} %slice_bitcast_fusion.1), channel_id=1, source_target_pairs={{0,2},{1,3},{2,0},{3,1},{4,6},{5,7},{6,4},{7,5},{8,10},{9,11},{10,... | collective-permute-start | bytes 393224 | tf_op jit(solution)/shard_map/ppermute | solution.py:77
  39.9 5.0 %collective-permute-start.17 = (f32[256,128]{1,0:T(8,128)S(1)}, f32[256,128]{1,0:T(8,128)S(1)}, u32[]{:S(2)}, u32[]{:S(2)}) collective-permute-start(f32[256,128]{1,0:T(8,128)S(1)} %fusion.3), channel_id=1, source_target_pairs={{0,2},{1,3},{2,0},{3,1},{4,6},{5,7},{6,4},{7,5},{8,10},{9,11},{10,... | collective-permute-start | bytes 393224 | tf_op jit(solution)/shard_map/ppermute | solution.py:77
  40.5 5.8 %collective-permute-start.22 = (f32[256,128]{1,0:T(8,128)S(1)}, f32[256,128]{1,0:T(8,128)S(1)}, u32[]{:S(2)}, u32[]{:S(2)}) collective-permute-start(f32[256,128]{1,0:T(8,128)S(1)} %get-tuple-element.35), channel_id=1, source_target_pairs={{0,4},{1,5},{2,6},{3,7},{4,0},{5,1},{6,2},{7,3},{8,12},{9,13},{10,... | collective-permute-start | bytes 393224 | tf_op jit(solution)/shard_map/ppermute | solution.py:77
  41.9 7.1 %collective-permute-start.21 = (f32[256,128]{1,0:T(8,128)S(1)}, f32[256,128]{1,0:T(8,128)S(1)}, u32[]{:S(2)}, u32[]{:S(2)}) collective-permute-start(f32[256,128]{1,0:T(8,128)S(1)} %fusion.2), channel_id=1, source_target_pairs={{0,4},{1,5},{2,6},{3,7},{4,0},{5,1},{6,2},{7,3},{8,12},{9,13},{10,... | collective-permute-start | bytes 393224 | tf_op jit(solution)/shard_map/ppermute | solution.py:77
  44.9 5.0 %collective-permute-start.18 = (f32[256,128]{1,0:T(8,128)S(1)}, f32[256,128]{1,0:T(8,128)S(1)}, u32[]{:S(2)}, u32[]{:S(2)}) collective-permute-start(f32[256,128]{1,0:T(8,128)S(1)} %slice_bitcast_fusion.6), channel_id=1, source_target_pairs={{0,2},{1,3},{2,0},{3,1},{4,6},{5,7},{6,4},{7,5},{8,10},{9,11},{10,... | collective-permute-start | bytes 393224 | tf_op jit(solution)/shard_map/ppermute | solution.py:77
  46.3 6.9 %collective-permute-start.23 = (f32[256,128]{1,0:T(8,128)S(1)}, f32[256,128]{1,0:T(8,128)S(1)}, u32[]{:S(2)}, u32[]{:S(2)}) collective-permute-start(f32[256,128]{1,0:T(8,128)S(1)} %fusion.1), channel_id=1, source_target_pairs={{0,12},{1,13},{2,14},{3,15},{4,8},{5,9},{6,10},{7,11},{8,4},{9,5},... | collective-permute-start | bytes 393224 | tf_op jit(solution)/shard_map/ppermute | solution.py:77

commit v6 on v5

--- a/solution.py
+++ b/solution.py
@@ -99,14 +99,14 @@
     crossed = {k: grid.shift(parts[1][k], (0, 0, 1)) for k in (2, 3, 1, 0)}
     pairs = {k: parts[0][k] + crossed[k] for k in (2, 3, 1, 0)}
     far_away = grid.shift(pairs[2][1], (1, 0, 0))
-    far_here, (far_away,) = tie(pairs[2][0], far_away)
-    far_here = grid.shift(far_here, (1, 0, 0))
     near = pairs[1][0] + grid.shift(pairs[1][1], (0, 1, 0))
     mirror = grid.shift(pairs[3][1] + far_away, (0, 1, 0))
+    both = grid.shift(jnp.concatenate([pairs[2][0], near], axis=0), (1, 0, 0))
+    far_here, near = both[: near.shape[0]], both[near.shape[0] :]
     own, (mirror,) = tie(pairs[0][1], mirror)
     mirror = pairs[3][0] + far_here + mirror
     own = pairs[0][0] + grid.shift(own, (0, 1, 0))
-    return own + grid.shift(near, (1, 0, 0)) + grid.shift(mirror, (3, 0, 0))
+    return own + near + grid.shift(mirror, (3, 0, 0))
 
 
 def exchange_kernel(grid, per_owner, packs, owner_ref, sub_ref, cols_ref, order_ref, split_ref, *refs):

time: 54.2 us -> 55.4 us (1.022)
  waiting for transfers between devices: 20.1 us -> 21.9 us
  starting transfers between devices: 20.2 us -> 19.5 us
    ppermute x24 -> x23, waiting for transfers between devices: 20.1 us -> 21.9 us  [shift(): lax.ppermute(x, 'aux', [(i, self.other(i, offset)) for i in range(self.z...]
    ppermute x24 -> x23, starting transfers between devices: 20.2 us -> 19.5 us  [shift(): lax.ppermute(x, 'aux', [(i, self.other(i, offset)) for i in range(self.z...]
  transfers between devices with their start and end apart: 24 -> 23, of which waited for: 11 -> 11; matrix products, arithmetic and copies ran while one was open for 0% -> 0% of each run, Pallas kernels for 10% -> 9%
where the time goes in v6:
time: 55.4 us; the launch traced here: 55.2 us
  waiting for transfers between devices  21.9 us (40%)
  starting transfers between devices  19.5 us (35%)
  Pallas kernels  12.6 us (23%)
  other arithmetic  0.93 us (2%)
    ppermute x23, waiting for transfers between devices, shift(): lax.ppermute(x, 'aux', [(i, self.other(i, offset)) for i in range(self.z...  21.9 us
    ppermute x23, starting transfers between devices, shift(): lax.ppermute(x, 'aux', [(i, self.other(i, offset)) for i in range(self.z...  19.5 us
    pallas_call x1, Pallas kernels, exchange(): pl.pallas_call(functools.partial(exchange_kernel, grid, per_owner, packs)...  7.42 us
    pallas_call x1, Pallas kernels, prepare(): pl.pallas_call(prepare_kernel, out_shape=pltpu.VMEM((n_tiles, aux_dev * b...  5.2 us
  transfers between devices with their start and end apart: 23, of which 11 were waited for; matrix products, arithmetic and copies ran while one was open for 0% of the time, Pallas kernels for 9%

profile of v6, /device:TPU:0, one launch (start us, length us, event | category | flops | bytes accessed | tf_op | source)
XLA Modules:
  0.0 55.2 jit_solution(1308240823374719926)
XLA Ops:
  0.0 0.0 copy-start
  0.0 0.0 copy-start.4
  0.0 0.0 copy-start.3
  0.0 0.0 copy-start.2
  0.0 0.0 copy-start.1
  0.0 3.0 %collective-permute-start.2 = (f32[256,128]{1,0:T(8,128)}, f32[256,128]{1,0:T(8,128)S(1)}, u32[]{:S(2)}, u32[]{:S(2)}) collective-permute-start(f32[256,128]{1,0:T(8,128)} %refs_0_.1), channel_id=1, source_target_pairs={{0,2},{1,3},{2,0},{3,1},{4,6},{5,7},{6,4},{7,5},{8,10},{9,11},{10,... | collective-permute-start | bytes 393224 | tf_op jit(solution)/shard_map/ppermute | solution.py:77
  3.1 1.6 %collective-permute-start.1 = (f32[256,128]{1,0:T(8,128)}, f32[256,128]{1,0:T(8,128)S(1)}, u32[]{:S(2)}, u32[]{:S(2)}) collective-permute-start(f32[256,128]{1,0:T(8,128)} %refs_0_.1), channel_id=1, source_target_pairs={{0,4},{1,5},{2,6},{3,7},{4,0},{5,1},{6,2},{7,3},{8,12},{9,13},{10,... | collective-permute-start | bytes 393224 | tf_op jit(solution)/shard_map/ppermute | solution.py:77
  4.6 2.5 %collective-permute-start = (f32[256,128]{1,0:T(8,128)}, f32[256,128]{1,0:T(8,128)S(1)}, u32[]{:S(2)}, u32[]{:S(2)}) collective-permute-start(f32[256,128]{1,0:T(8,128)} %refs_0_.1), channel_id=1, source_target_pairs={{0,12},{1,13},{2,14},{3,15},{4,8},{5,9},{6,10},{7,11},{8,4},{9,5},... | collective-permute-start | bytes 393224 | tf_op jit(solution)/shard_map/ppermute | solution.py:77
  7.1 5.2 %prepare.1.split_ref = bf16[32,512,256]{2,1,0:T(8,128)(2,1)S(1)} custom-call(f32[32,4,128,128]{3,2,1,0:T(8,128)} %tiles_ref.1), custom_call_target="tpu_custom_call" | custom-call | flops 12582912 | bytes 16777216 | tf_op jit(solution)/shard_map/prepare/pallas_call | solution.py:46
  12.3 0.0 collective-permute-done.2.refs_3_
  12.3 0.0 collective-permute-done.1.refs_2_
  12.3 0.8 %collective-permute-done.refs_1_ = f32[256,128]{1,0:T(8,128)S(1)} collective-permute-done((f32[256,128]{1,0:T(8,128)}, f32[256,128]{1,0:T(8,128)S(1)}, u32[]{:S(2)}, u32[]{:S(2)}) %collective-permute-start) | collective-permute-done | bytes 131104 | tf_op jit(solution)/shard_map/ppermute | solution.py:77
  13.1 0.7 %collective-permute-start.5 = (f32[512,128]{1,0:T(8,128)S(1)}, f32[512,128]{1,0:T(8,128)S(1)}, u32[]{:S(2)}, u32[]{:S(2)}) collective-permute-start(f32[512,128]{1,0:T(8,128)S(1)} %pad_maximum_fusion), channel_id=1, source_target_pairs={{0,4},{1,5},{2,6},{3,7},{4,0},{5,1},{6,2},{7,3},{8,12},{9,13},{10,... | collective-permute-start | bytes 786440 | tf_op jit(solution)/shard_map/ppermute | solution.py:77
  13.9 0.5 collective-permute-start.3
  14.4 0.0 copy-done
  14.4 0.0 collective-permute-start.6
  14.4 0.5 collective-permute-start.8
  14.9 3.9 %collective-permute-done.3.refs_4_ = f32[256,128]{1,0:T(8,128)S(1)} collective-permute-done((f32[256,128]{1,0:T(8,128)S(1)}, f32[256,128]{1,0:T(8,128)S(1)}, u32[]{:S(2)}, u32[]{:S(2)}) %collective-permute-start.3) | collective-permute-done | bytes 131104 | tf_op jit(solution)/shard_map/ppermute | solution.py:77
  18.8 1.4 %collective-permute-start.4 = (f32[256,128]{1,0:T(8,128)S(1)}, f32[256,128]{1,0:T(8,128)S(1)}, u32[]{:S(2)}, u32[]{:S(2)}) collective-permute-start(f32[256,128]{1,0:T(8,128)S(1)} %collective-permute-done.3.refs_4_), channel_id=1, source_target_pairs={{0,4},{1,5},{2,6},{3,7},{4,0},{5,1},{6,2},{7,3},{8,12},{9,13},{10,... | collective-permute-start | bytes 393224 | tf_op jit(solution)/shard_map/ppermute | solution.py:77
  20.2 0.9 %collective-permute-done.5.refs_6_ = f32[512,128]{1,0:T(8,128)S(1)} collective-permute-done((f32[512,128]{1,0:T(8,128)S(1)}, f32[512,128]{1,0:T(8,128)S(1)}, u32[]{:S(2)}, u32[]{:S(2)}) %collective-permute-start.5) | collective-permute-done | bytes 262176 | tf_op jit(solution)/shard_map/ppermute | solution.py:77
  21.1 0.0 collective-permute-start.12
  21.1 0.5 collective-permute-start.9
  21.6 0.0 collective-permute-done.6.refs_7_
  21.6 0.0 collective-permute-start.7
  21.6 0.0 collective-permute-done.8.refs_9_
  21.6 0.5 collective-permute-start.10
  22.1 1.7 %collective-permute-done.4.refs_5_ = f32[256,128]{1,0:T(8,128)S(1)} collective-permute-done((f32[256,128]{1,0:T(8,128)S(1)}, f32[256,128]{1,0:T(8,128)S(1)}, u32[]{:S(2)}, u32[]{:S(2)}) %collective-permute-start.4) | collective-permute-done | bytes 131104 | tf_op jit(solution)/shard_map/ppermute | solution.py:77
  23.8 0.0 collective-permute-start.11
  23.8 0.0 collective-permute-done.9.refs_10_
  23.8 0.0 collective-permute-done.7.refs_8_
  23.8 0.0 collective-permute-done.10.refs_11_
  23.8 1.3 %collective-permute-done.11.refs_12_ = f32[256,128]{1,0:T(8,128)S(1)} collective-permute-done((f32[256,128]{1,0:T(8,128)S(1)}, f32[256,128]{1,0:T(8,128)S(1)}, u32[]{:S(2)}, u32[]{:S(2)}) %collective-permute-start.11) | collective-permute-done | bytes 131104 | tf_op jit(solution)/shard_map/ppermute | solution.py:77
  25.2 0.0 collective-permute-done.12.refs_13_
  25.2 0.0 copy-done.4
  25.2 0.0 copy-done.3
  25.2 0.0 copy-done.2
  25.2 0.0 copy-done.1
  25.2 7.4 %exchange.1 = (f32[2,256,128]{2,1,0:T(8,128)S(1)}, f32[2,256,128]{2,1,0:T(8,128)S(1)}, f32[2,256,128]{2,1,0:T(8,128)S(1)}, f32[2,256,128]{2,1,0:T(8,128)S(1)}, f...) custom-call(s32[32]{0:T(128)S(1)} %bitcast.27, ...), custom_call_target="tpu_custom_call" | custom-call | tf_op jit(solution)/shard_map/exchange/pallas_call | solution.py:185
  32.6 0.2 collective-permute-start.19
  32.8 0.4 collective-permute-start.15
  33.2 0.1 collective-permute-start.13
  33.3 0.4 collective-permute-start.14
  33.7 0.5 collective-permute-done.19
  34.3 0.6 %collective-permute-start.20 = (f32[256,128]{1,0:T(8,128)S(1)}, f32[256,128]{1,0:T(8,128)S(1)}, u32[]{:S(2)}, u32[]{:S(2)}) collective-permute-start(f32[256,128]{1,0:T(8,128)S(1)} %slice_bitcast_fusion.1), channel_id=1, source_target_pairs={{0,2},{1,3},{2,0},{3,1},{4,6},{5,7},{6,4},{7,5},{8,10},{9,11},{10,... | collective-permute-start | bytes 393224 | tf_op jit(solution)/shard_map/ppermute | solution.py:77
  34.8 0.0 collective-permute-done.15
  34.9 1.4 %collective-permute-start.16 = (f32[256,128]{1,0:T(8,128)S(1)}, f32[256,128]{1,0:T(8,128)S(1)}, u32[]{:S(2)}, u32[]{:S(2)}) collective-permute-start(f32[256,128]{1,0:T(8,128)S(1)} %get-tuple-element.34), channel_id=1, source_target_pairs={{0,4},{1,5},{2,6},{3,7},{4,0},{5,1},{6,2},{7,3},{8,12},{9,13},{10,... | collective-permute-start | bytes 393224 | tf_op jit(solution)/shard_map/ppermute | solution.py:77
  36.3 0.0 collective-permute-done.13
  36.4 0.0 collective-permute-done.14
  36.4 3.4 %collective-permute-done.20 = f32[256,128]{1,0:T(8,128)S(1)} collective-permute-done((f32[256,128]{1,0:T(8,128)S(1)}, f32[256,128]{1,0:T(8,128)S(1)}, u32[]{:S(2)}, u32[]{:S(2)}) %collective-permute-start.20) | collective-permute-done | bytes 131104 | tf_op jit(solution)/shard_map/ppermute | solution.py:77
  39.9 1.4 %collective-permute-start.21 = (f32[512,128]{1,0:T(8,128)S(1)}, f32[512,128]{1,0:T(8,128)S(1)}, u32[]{:S(2)}, u32[]{:S(2)}) collective-permute-start(f32[512,128]{1,0:T(8,128)S(1)} %pad_maximum_fusion.1), channel_id=1, source_target_pairs={{0,4},{1,5},{2,6},{3,7},{4,0},{5,1},{6,2},{7,3},{8,12},{9,13},{10,... | collective-permute-start | bytes 786440 | tf_op jit(solution)/shard_map/ppermute | solution.py:77
  41.4 0.0 collective-permute-done.16
  41.4 0.6 %collective-permute-start.17 = (f32[256,128]{1,0:T(8,128)S(1)}, f32[256,128]{1,0:T(8,128)S(1)}, u32[]{:S(2)}, u32[]{:S(2)}) collective-permute-start(f32[256,128]{1,0:T(8,128)S(1)} %fusion.3), channel_id=1, source_target_pairs={{0,2},{1,3},{2,0},{3,1},{4,6},{5,7},{6,4},{7,5},{8,10},{9,11},{10,... | collective-permute-start | bytes 393224 | tf_op jit(solution)/shard_map/ppermute | solution.py:77
  42.0 4.5 %collective-permute-done.17 = f32[256,128]{1,0:T(8,128)S(1)} collective-permute-done((f32[256,128]{1,0:T(8,128)S(1)}, f32[256,128]{1,0:T(8,128)S(1)}, u32[]{:S(2)}, u32[]{:S(2)}) %collective-permute-start.17) | collective-permute-done | bytes 131104 | tf_op jit(solution)/shard_map/ppermute | solution.py:77
  46.4 0.5 collective-permute-start.18
  46.9 0.6 %collective-permute-done.21 = f32[512,128]{1,0:T(8,128)S(1)} collective-permute-done((f32[512,128]{1,0:T(8,128)S(1)}, f32[512,128]{1,0:T(8,128)S(1)}, u32[]{:S(2)}, u32[]{:S(2)}) %collective-permute-start.21) | collective-permute-done | bytes 262176 | tf_op jit(solution)/shard_map/ppermute | solution.py:77
  47.5 2.7 %collective-permute-start.22 = (f32[256,128]{1,0:T(8,128)S(1)}, f32[256,128]{1,0:T(8,128)S(1)}, u32[]{:S(2)}, u32[]{:S(2)}) collective-permute-start(f32[256,128]{1,0:T(8,128)S(1)} %fusion), channel_id=1, source_target_pairs={{0,12},{1,13},{2,14},{3,15},{4,8},{5,9},{6,10},{7,11},{8,4},{9,5},... | collective-permute-start | bytes 393224 | tf_op jit(solution)/shard_map/ppermute | solution.py:77
  50.2 1.2 %collective-permute-done.18 = f32[256,128]{1,0:T(8,128)S(1)} collective-permute-done((f32[256,128]{1,0:T(8,128)S(1)}, f32[256,128]{1,0:T(8,128)S(1)}, u32[]{:S(2)}, u32[]{:S(2)}) %collective-permute-start.18) | collective-permute-done | bytes 131104 | tf_op jit(solution)/shard_map/ppermute | solution.py:77
  51.4 3.1 %collective-permute-done.22 = f32[256,128]{1,0:T(8,128)S(1)} collective-permute-done((f32[256,128]{1,0:T(8,128)S(1)}, f32[256,128]{1,0:T(8,128)S(1)}, u32[]{:S(2)}, u32[]{:S(2)}) %collective-permute-start.22) | collective-permute-done | bytes 131104 | tf_op jit(solution)/shard_map/ppermute | solution.py:77
  54.5 0.7 %fusion.1 = f32[256,128]{1,0:T(8,128)} fusion(f32[256,128]{1,0:T(8,128)S(1)} %collective-permute-done.22, f32[512,128]{1,0:T(8,128)S(1)} %collective-permute-done.21, f32[256,128]{1,0:T(8,128)S(1)} %collective-permute-done.18, f32[2,256,128]{2,1,0:T(8,128)S(1)} %add.33), kind=kLoop, calls=%fused_computation.6 | loop fusion | flops 98304 | bytes 655360 | tf_op jit(solution)/shard_map/add | solution.py:109
  (12 shorter events, 0.3 us)
Async XLA Ops:
  0.0 14.4 %copy-start = (f32[256,128]{1,0:T(8,128)S(1)}, f32[256,128]{1,0:T(8,128)}, u32[]{:S(2)}) copy-start(f32[256,128]{1,0:T(8,128)} %refs_0_.1) | copy-start | bytes 393220
  0.0 25.2 %copy-start.4 = (s32[32]{0:T(128)S(1)}, s32[32]{0:T(128)}, u32[]{:S(2)}) copy-start(s32[32]{0:T(128)} %order_ref.1) | copy-start | bytes 388
  0.0 25.2 %copy-start.3 = (s32[32]{0:T(128)S(1)}, s32[32]{0:T(128)}, u32[]{:S(2)}) copy-start(s32[32]{0:T(128)} %cols_ref.1) | copy-start | bytes 388
  0.0 25.2 %copy-start.2 = (s32[32]{0:T(128)S(1)}, s32[32]{0:T(128)}, u32[]{:S(2)}) copy-start(s32[32]{0:T(128)} %sub_ref.1) | copy-start | bytes 388
  0.0 25.2 %copy-start.1 = (s32[32,1]{0,1:T(1,128)S(1)}, s32[32,1]{0,1:T(1,128)}, u32[]{:S(2)}) copy-start(s32[32,1]{0,1:T(1,128)} %param.7) | copy-start | bytes 388
  0.0 12.3 %collective-permute-start.2 = (f32[256,128]{1,0:T(8,128)}, f32[256,128]{1,0:T(8,128)S(1)}, u32[]{:S(2)}, u32[]{:S(2)}) collective-permute-start(f32[256,128]{1,0:T(8,128)} %refs_0_.1), channel_id=1, source_target_pairs={{0,2},{1,3},{2,0},{3,1},{4,6},{5,7},{6,4},{7,5},{8,10},{9,11},{10,... | collective-permute-start | bytes 393224 | tf_op jit(solution)/shard_map/ppermute | solution.py:77
  3.1 9.3 %collective-permute-start.1 = (f32[256,128]{1,0:T(8,128)}, f32[256,128]{1,0:T(8,128)S(1)}, u32[]{:S(2)}, u32[]{:S(2)}) collective-permute-start(f32[256,128]{1,0:T(8,128)} %refs_0_.1), channel_id=1, source_target_pairs={{0,4},{1,5},{2,6},{3,7},{4,0},{5,1},{6,2},{7,3},{8,12},{9,13},{10,... | collective-permute-start | bytes 393224 | tf_op jit(solution)/shard_map/ppermute | solution.py:77
  4.6 8.5 %collective-permute-start = (f32[256,128]{1,0:T(8,128)}, f32[256,128]{1,0:T(8,128)S(1)}, u32[]{:S(2)}, u32[]{:S(2)}) collective-permute-start(f32[256,128]{1,0:T(8,128)} %refs_0_.1), channel_id=1, source_target_pairs={{0,12},{1,13},{2,14},{3,15},{4,8},{5,9},{6,10},{7,11},{8,4},{9,5},... | collective-permute-start | bytes 393224 | tf_op jit(solution)/shard_map/ppermute | solution.py:77
  13.1 8.0 %collective-permute-start.5 = (f32[512,128]{1,0:T(8,128)S(1)}, f32[512,128]{1,0:T(8,128)S(1)}, u32[]{:S(2)}, u32[]{:S(2)}) collective-permute-start(f32[512,128]{1,0:T(8,128)S(1)} %pad_maximum_fusion), channel_id=1, source_target_pairs={{0,4},{1,5},{2,6},{3,7},{4,0},{5,1},{6,2},{7,3},{8,12},{9,13},{10,... | collective-permute-start | bytes 786440 | tf_op jit(solution)/shard_map/ppermute | solution.py:77
  13.9 5.0 %collective-permute-start.3 = (f32[256,128]{1,0:T(8,128)S(1)}, f32[256,128]{1,0:T(8,128)S(1)}, u32[]{:S(2)}, u32[]{:S(2)}) collective-permute-start(f32[256,128]{1,0:T(8,128)S(1)} %collective-permute-done.refs_1_), channel_id=1, source_target_pairs={{0,2},{1,3},{2,0},{3,1},{4,6},{5,7},{6,4},{7,5},{8,10},{9,11},{10,... | collective-permute-start | bytes 393224 | tf_op jit(solution)/shard_map/ppermute | solution.py:77
  14.4 7.2 %collective-permute-start.6 = (f32[256,128]{1,0:T(8,128)S(1)}, f32[256,128]{1,0:T(8,128)S(1)}, u32[]{:S(2)}, u32[]{:S(2)}) collective-permute-start(f32[256,128]{1,0:T(8,128)S(1)} %copy-done), channel_id=1, source_target_pairs={{0,1},{1,0},{2,3},{3,2},{4,5},{5,4},{6,7},{7,6},{8,9},{9,8},{10,11... | collective-permute-start | bytes 393224 | tf_op jit(solution)/shard_map/ppermute | solution.py:77
  14.4 7.3 %collective-permute-start.8 = (f32[256,128]{1,0:T(8,128)S(1)}, f32[256,128]{1,0:T(8,128)S(1)}, u32[]{:S(2)}, u32[]{:S(2)}) collective-permute-start(f32[256,128]{1,0:T(8,128)S(1)} %collective-permute-done.1.refs_2_), channel_id=1, source_target_pairs={{0,1},{1,0},{2,3},{3,2},{4,5},{5,4},{6,7},{7,6},{8,9},{9,8},{10,11... | collective-permute-start | bytes 393224 | tf_op jit(solution)/shard_map/ppermute | solution.py:77
  18.8 5.0 %collective-permute-start.4 = (f32[256,128]{1,0:T(8,128)S(1)}, f32[256,128]{1,0:T(8,128)S(1)}, u32[]{:S(2)}, u32[]{:S(2)}) collective-permute-start(f32[256,128]{1,0:T(8,128)S(1)} %collective-permute-done.3.refs_4_), channel_id=1, source_target_pairs={{0,4},{1,5},{2,6},{3,7},{4,0},{5,1},{6,2},{7,3},{8,12},{9,13},{10,... | collective-permute-start | bytes 393224 | tf_op jit(solution)/shard_map/ppermute | solution.py:77
  21.1 4.0 %collective-permute-start.12 = (f32[512,128]{1,0:T(8,128)S(1)}, f32[512,128]{1,0:T(8,128)S(1)}, u32[]{:S(2)}, u32[]{:S(2)}) collective-permute-start(f32[512,128]{1,0:T(8,128)S(1)} %collective-permute-done.5.refs_6_), channel_id=1, source_target_pairs={{0,1},{1,0},{2,3},{3,2},{4,5},{5,4},{6,7},{7,6},{8,9},{9,8},{10,11... | collective-permute-start | bytes 786440 | tf_op jit(solution)/shard_map/ppermute | solution.py:77
  21.1 2.7 %collective-permute-start.9 = (f32[256,128]{1,0:T(8,128)S(1)}, f32[256,128]{1,0:T(8,128)S(1)}, u32[]{:S(2)}, u32[]{:S(2)}) collective-permute-start(f32[256,128]{1,0:T(8,128)S(1)} %collective-permute-done.2.refs_3_), channel_id=1, source_target_pairs={{0,1},{1,0},{2,3},{3,2},{4,5},{5,4},{6,7},{7,6},{8,9},{9,8},{10,11... | collective-permute-start | bytes 393224 | tf_op jit(solution)/shard_map/ppermute | solution.py:77
  21.6 2.2 %collective-permute-start.7 = (f32[256,128]{1,0:T(8,128)S(1)}, f32[256,128]{1,0:T(8,128)S(1)}, u32[]{:S(2)}, u32[]{:S(2)}) collective-permute-start(f32[256,128]{1,0:T(8,128)S(1)} %collective-permute-done.refs_1_), channel_id=1, source_target_pairs={{0,1},{1,0},{2,3},{3,2},{4,5},{5,4},{6,7},{7,6},{8,9},{9,8},{10,11... | collective-permute-start | bytes 393224 | tf_op jit(solution)/shard_map/ppermute | solution.py:77
  21.6 2.2 %collective-permute-start.10 = (f32[256,128]{1,0:T(8,128)S(1)}, f32[256,128]{1,0:T(8,128)S(1)}, u32[]{:S(2)}, u32[]{:S(2)}) collective-permute-start(f32[256,128]{1,0:T(8,128)S(1)} %collective-permute-done.3.refs_4_), channel_id=1, source_target_pairs={{0,1},{1,0},{2,3},{3,2},{4,5},{5,4},{6,7},{7,6},{8,9},{9,8},{10,11... | collective-permute-start | bytes 393224 | tf_op jit(solution)/shard_map/ppermute | solution.py:77
  23.8 1.3 %collective-permute-start.11 = (f32[256,128]{1,0:T(8,128)S(1)}, f32[256,128]{1,0:T(8,128)S(1)}, u32[]{:S(2)}, u32[]{:S(2)}) collective-permute-start(f32[256,128]{1,0:T(8,128)S(1)} %collective-permute-done.4.refs_5_), channel_id=1, source_target_pairs={{0,1},{1,0},{2,3},{3,2},{4,5},{5,4},{6,7},{7,6},{8,9},{9,8},{10,11... | collective-permute-start | bytes 393224 | tf_op jit(solution)/shard_map/ppermute | solution.py:77
  32.6 1.6 %collective-permute-start.19 = (f32[2,256,128]{2,1,0:T(8,128)S(1)}, f32[2,256,128]{2,1,0:T(8,128)S(1)}, u32[]{:S(2)}, u32[]{:S(2)}) collective-permute-start(f32[2,256,128]{2,1,0:T(8,128)S(1)} %get-tuple-element.31), channel_id=1, source_target_pairs={{0,1},{1,0},{2,3},{3,2},{4,5},{5,4},{6,7},{7,6},{8,9},{9,8},{10,11... | collective-permute-start | bytes 786440 | tf_op jit(solution)/shard_map/ppermute | solution.py:77
  32.8 2.0 %collective-permute-start.15 = (f32[2,256,128]{2,1,0:T(8,128)S(1)}, f32[2,256,128]{2,1,0:T(8,128)S(1)}, u32[]{:S(2)}, u32[]{:S(2)}) collective-permute-start(f32[2,256,128]{2,1,0:T(8,128)S(1)} %get-tuple-element.28), channel_id=1, source_target_pairs={{0,1},{1,0},{2,3},{3,2},{4,5},{5,4},{6,7},{7,6},{8,9},{9,8},{10,11... | collective-permute-start | bytes 786440 | tf_op jit(solution)/shard_map/ppermute | solution.py:77
  33.2 3.2 %collective-permute-start.13 = (f32[2,256,128]{2,1,0:T(8,128)S(1)}, f32[2,256,128]{2,1,0:T(8,128)S(1)}, u32[]{:S(2)}, u32[]{:S(2)}) collective-permute-start(f32[2,256,128]{2,1,0:T(8,128)S(1)} %get-tuple-element.24), channel_id=1, source_target_pairs={{0,1},{1,0},{2,3},{3,2},{4,5},{5,4},{6,7},{7,6},{8,9},{9,8},{10,11... | collective-permute-start | bytes 786440 | tf_op jit(solution)/shard_map/ppermute | solution.py:77
  33.3 3.1 %collective-permute-start.14 = (f32[2,256,128]{2,1,0:T(8,128)S(1)}, f32[2,256,128]{2,1,0:T(8,128)S(1)}, u32[]{:S(2)}, u32[]{:S(2)}) collective-permute-start(f32[2,256,128]{2,1,0:T(8,128)S(1)} %get-tuple-element.26), channel_id=1, source_target_pairs={{0,1},{1,0},{2,3},{3,2},{4,5},{5,4},{6,7},{7,6},{8,9},{9,8},{10,11... | collective-permute-start | bytes 786440 | tf_op jit(solution)/shard_map/ppermute | solution.py:77
  34.3 5.6 %collective-permute-start.20 = (f32[256,128]{1,0:T(8,128)S(1)}, f32[256,128]{1,0:T(8,128)S(1)}, u32[]{:S(2)}, u32[]{:S(2)}) collective-permute-start(f32[256,128]{1,0:T(8,128)S(1)} %slice_bitcast_fusion.1), channel_id=1, source_target_pairs={{0,2},{1,3},{2,0},{3,1},{4,6},{5,7},{6,4},{7,5},{8,10},{9,11},{10,... | collective-permute-start | bytes 393224 | tf_op jit(solution)/shard_map/ppermute | solution.py:77
  34.9 6.5 %collective-permute-start.16 = (f32[256,128]{1,0:T(8,128)S(1)}, f32[256,128]{1,0:T(8,128)S(1)}, u32[]{:S(2)}, u32[]{:S(2)}) collective-permute-start(f32[256,128]{1,0:T(8,128)S(1)} %get-tuple-element.34), channel_id=1, source_target_pairs={{0,4},{1,5},{2,6},{3,7},{4,0},{5,1},{6,2},{7,3},{8,12},{9,13},{10,... | collective-permute-start | bytes 393224 | tf_op jit(solution)/shard_map/ppermute | solution.py:77
  39.9 7.6 %collective-permute-start.21 = (f32[512,128]{1,0:T(8,128)S(1)}, f32[512,128]{1,0:T(8,128)S(1)}, u32[]{:S(2)}, u32[]{:S(2)}) collective-permute-start(f32[512,128]{1,0:T(8,128)S(1)} %pad_maximum_fusion.1), channel_id=1, source_target_pairs={{0,4},{1,5},{2,6},{3,7},{4,0},{5,1},{6,2},{7,3},{8,12},{9,13},{10,... | collective-permute-start | bytes 786440 | tf_op jit(solution)/shard_map/ppermute | solution.py:77
  41.4 5.0 %collective-permute-start.17 = (f32[256,128]{1,0:T(8,128)S(1)}, f32[256,128]{1,0:T(8,128)S(1)}, u32[]{:S(2)}, u32[]{:S(2)}) collective-permute-start(f32[256,128]{1,0:T(8,128)S(1)} %fusion.3), channel_id=1, source_target_pairs={{0,2},{1,3},{2,0},{3,1},{4,6},{5,7},{6,4},{7,5},{8,10},{9,11},{10,... | collective-permute-start | bytes 393224 | tf_op jit(solution)/shard_map/ppermute | solution.py:77
  46.4 5.0 %collective-permute-start.18 = (f32[256,128]{1,0:T(8,128)S(1)}, f32[256,128]{1,0:T(8,128)S(1)}, u32[]{:S(2)}, u32[]{:S(2)}) collective-permute-start(f32[256,128]{1,0:T(8,128)S(1)} %slice_bitcast_fusion.6), channel_id=1, source_target_pairs={{0,2},{1,3},{2,0},{3,1},{4,6},{5,7},{6,4},{7,5},{8,10},{9,11},{10,... | collective-permute-start | bytes 393224 | tf_op jit(solution)/shard_map/ppermute | solution.py:77
  47.5 6.9 %collective-permute-start.22 = (f32[256,128]{1,0:T(8,128)S(1)}, f32[256,128]{1,0:T(8,128)S(1)}, u32[]{:S(2)}, u32[]{:S(2)}) collective-permute-start(f32[256,128]{1,0:T(8,128)S(1)} %fusion), channel_id=1, source_target_pairs={{0,12},{1,13},{2,14},{3,15},{4,8},{5,9},{6,10},{7,11},{8,4},{9,5},... | collective-permute-start | bytes 393224 | tf_op jit(solution)/shard_map/ppermute | solution.py:77
